TPU v7x, 32 devices: a whole 2x2x4 slice. The times are simulated.
32 devices in a mesh: img: 8 (over z, y), strip: 4 (over x, core).
Axes of the slice: x: 2, y: 2, z: 4, core: 2. Of those that a mesh axis runs over, the one named last changes fastest.
Arguments:
- tokens: bfloat16 [32, 256, 2048], P('img', 'strip'), may hold values from -6 to 6
- cotangent: bfloat16 [32, 256, 2048], P('img', 'strip'), may hold values from -6 to 6
- bin_ids: int32 [32], replicated, may hold values from 0 to 1023
- level_table: float32 [1024, 2048], P(('img', 'strip')), may hold values from -6 to 6
- table_moment: float32 [1024, 2048], P(('img', 'strip')), may hold values from -2048 to 2048
- matrices: float32 [2048, 18, 2048], P(('img', 'strip')), may hold values from -2 to 2
- matrix_moment: float32 [2048, 18, 2048], P(('img', 'strip')), may hold values from -16384 to 16384
- modulation_bias: float32 [6, 2048], P(None, ('img', 'strip')), may hold values from -1 to 1
- bias_moment: float32 [6, 2048], P(None, ('img', 'strip')), may hold values from -32768 to 32768
Outputs:
- block_out: bfloat16 [32, 256, 2048], P('img', 'strip')
- input_grad: bfloat16 [32, 256, 2048], P('img', 'strip')
- table_grad: float32 [1024, 2048], P(('img', 'strip'))
- table_momentum: float32 [1024, 2048], P(('img', 'strip'))
- table_new: float32 [1024, 2048], P(('img', 'strip'))
- matrix_momentum: float32 [2048, 18, 2048], P(('img', 'strip'))
- matrix_new: float32 [2048, 18, 2048], P(('img', 'strip'))
- bias_momentum: float32 [6, 2048], P(None, ('img', 'strip'))
- bias_new: float32 [6, 2048], P(None, ('img', 'strip'))
All inputs are finite; a program needn't handle non-finite values.
Results may differ from a plain program's by a relative error of at most 0.017.
The roundings to bfloat16 on the way count: a program that leaves them out, or rounds other values in their place, can miss the bound.
Values may be sent and summed in bfloat16 or wider, within the bound.
No kernel may reach another device: no remote copies, remote signals or barrier semaphores. Data moves between devices by JAX's collectives and lax.ppermute only.
A program may use at most 832 MiB of HBM per device.

v0:
```python
import math

import jax
import jax.numpy as jnp
from jax import lax
from jax.sharding import PartitionSpec as P

D = 2048
HEADS = 16
HD = 128
FF = 8192
NS_STEPS = 2


highest = lax.Precision.HIGHEST
norm_eps = 1e-06
coef_one = 3.4445
coef_two = -4.775
coef_three = 2.0315
matrix_decay = 0.95
vector_decay = 0.9
matrix_rate = 0.5
bias_rate = 0.003
table_rate = 0.02


def normalize(values):
    center = values - jnp.mean(values, axis=-1, keepdims=True)
    inverse = lax.rsqrt(jnp.mean(center * center, axis=-1, keepdims=True) + norm_eps)
    return (center * inverse, inverse)


def norm_back(grad_hat, normed, inverse):
    mean_grad = jnp.mean(grad_hat, axis=-1, keepdims=True)
    mean_cross = jnp.mean(grad_hat * normed, axis=-1, keepdims=True)
    return inverse * (grad_hat - mean_grad - normed * mean_cross)


def gelu_slope(values):
    cumulative = 0.5 * (1.0 + lax.erf(values * 0.7071067811865476))
    density = jnp.exp(-0.5 * values * values) * 0.3989422804014327
    return cumulative + values * density


def silu_slope(values):
    logistic = jax.nn.sigmoid(values)
    return logistic * (1.0 + values * (1.0 - logistic))


def mlp_piece(second_in, pieces):
    up_piece, down_piece = pieces
    preact = jnp.einsum("ntk,rbk->ntbr", second_in, up_piece, preferred_element_type=jnp.float32)
    hidden = jax.nn.gelu(preact, approximate=False).astype(jnp.bfloat16)
    output = jnp.einsum("ntbr,rbk->ntk", hidden, down_piece, preferred_element_type=jnp.float32)
    return (output, hidden)


def on_device(
    tokens,
    cotangent,
    bin_ids,
    level_table,
    table_moment,
    matrices,
    matrix_moment,
    modulation_bias,
    bias_moment,
):
    strip_count = lax.axis_size("strip")
    image_groups = lax.axis_size("img")
    position = lax.axis_index("img") * strip_count + lax.axis_index("strip")
    blocks = FF // D
    start_down = 4 + blocks
    start_ada = 4 + 2 * blocks
    whole_images, upstream = (
        lax.all_to_all(tokens, "strip", split_axis=0, concat_axis=1, tiled=True),
        lax.all_to_all(cotangent, "strip", split_axis=0, concat_axis=1, tiled=True),
    )
    images, length, model_width = whole_images.shape
    shard_rows = matrices.shape[0]
    table_rows = level_table.shape[0]
    row_ids = position * table_rows + jnp.arange(table_rows, dtype=jnp.int32)
    selector = (bin_ids[:, None] == row_ids[None, :]).astype(jnp.float32)
    condition = lax.psum(jnp.dot(selector, level_table, precision=highest), ("img", "strip"))
    active = jax.nn.silu(condition).astype(jnp.bfloat16)
    ada_weight = matrices[:, start_ada:, :].astype(jnp.bfloat16)
    mod_columns = (
        jnp.einsum("nk,ruk->nur", active, ada_weight, preferred_element_type=jnp.float32)
        + modulation_bias[None]
    )
    modulation = lax.all_to_all(
        mod_columns, ("img", "strip"), split_axis=0, concat_axis=2, tiled=True
    )
    shift_one = modulation[:, 0][:, None, :]
    scale_one = modulation[:, 1][:, None, :]
    gate_one = modulation[:, 2][:, None, :]
    shift_two = modulation[:, 3][:, None, :]
    scale_two = modulation[:, 4][:, None, :]
    gate_two = modulation[:, 5][:, None, :]
    inputs = whole_images.astype(jnp.float32)
    normed_one, inverse_one = normalize(inputs)
    first_in = (normed_one * (1.0 + scale_one) + shift_one).astype(jnp.bfloat16)
    attention = lax.all_gather(
        matrices[:, :4, :].astype(jnp.bfloat16), ("img", "strip"), axis=0, tiled=True
    )
    projected = jnp.einsum(
        "ntk,juk->ntuj", first_in, attention[:, :3, :], preferred_element_type=jnp.float32
    ).astype(jnp.bfloat16)
    query = projected[:, :, 0, :].reshape(images, length, HEADS, HD)
    keys_all = projected[:, :, 1, :].reshape(images, length, HEADS, HD)
    values_all = projected[:, :, 2, :].reshape(images, length, HEADS, HD)
    factor = HD ** (-0.5)
    scores = (
        jnp.einsum("nthe,nshe->nhts", query, keys_all, preferred_element_type=jnp.float32) * factor
    )
    summit = jnp.max(scores, axis=-1, keepdims=True)
    exponent = jnp.exp(scores - summit)
    totals = jnp.sum(exponent, axis=-1, keepdims=True)
    logsum = summit + jnp.log(totals)
    probs_low = (exponent / totals).astype(jnp.bfloat16)
    mixed = jnp.einsum("nhts,nshe->nthe", probs_low, values_all, preferred_element_type=jnp.float32)
    mixed = mixed.reshape(images, length, model_width).astype(jnp.bfloat16)
    branch = jnp.einsum(
        "ntj,jk->ntk", mixed, attention[:, 3, :], preferred_element_type=jnp.float32
    )
    middle = inputs + gate_one * branch
    normed_two, inverse_two = normalize(middle)
    second_in = (normed_two * (1.0 + scale_two) + shift_two).astype(jnp.bfloat16)
    up_shard = matrices[:, 4:start_down, :].astype(jnp.bfloat16)
    down_shard = matrices[:, start_down:start_ada, :].astype(jnp.bfloat16)
    folded = mlp_piece(
        second_in,
        (
            lax.all_gather(up_shard, ("img", "strip"), axis=0, tiled=True),
            lax.all_gather(down_shard, ("img", "strip"), axis=0, tiled=True),
        ),
    )
    mlp_out, hidden_all = (folded[0], folded[1])
    total = middle + gate_two * mlp_out
    grad_total = upstream.astype(jnp.float32)
    grad_mlp = (grad_total * gate_two).astype(jnp.bfloat16)
    grad_gate_two = jnp.sum(grad_total * mlp_out, axis=1)
    up_piece = lax.all_gather(up_shard, ("img", "strip"), axis=0, tiled=True)
    down_piece = lax.all_gather(down_shard, ("img", "strip"), axis=0, tiled=True)
    preact = jnp.einsum("ntk,rbk->ntbr", second_in, up_piece, preferred_element_type=jnp.float32)
    grad_hidden = jnp.einsum(
        "ntk,rbk->ntbr", grad_mlp, down_piece, preferred_element_type=jnp.float32
    )
    grad_pre = (grad_hidden * gelu_slope(preact)).astype(jnp.bfloat16)
    grad_in = jnp.einsum("ntbr,rbk->ntk", grad_pre, up_piece, preferred_element_type=jnp.float32)
    attention_back = lax.all_gather(
        matrices[:, :4, :].astype(jnp.bfloat16), ("img", "strip"), axis=0, tiled=True
    )
    grad_shift_two = jnp.sum(grad_in, axis=1)
    grad_scale_two = jnp.sum(grad_in * normed_two, axis=1)
    grad_middle = grad_total + norm_back(grad_in * (1.0 + scale_two), normed_two, inverse_two)
    grad_branch = (grad_middle * gate_one).astype(jnp.bfloat16)
    grad_gate_one = jnp.sum(grad_middle * branch, axis=1)
    grad_mixed = jnp.einsum(
        "ntk,jk->ntj", grad_branch, attention_back[:, 3, :], preferred_element_type=jnp.float32
    ).astype(jnp.bfloat16)
    grad_heads = grad_mixed.reshape(images, length, HEADS, HD)
    scores_again = (
        jnp.einsum("nthe,nshe->nhts", query, keys_all, preferred_element_type=jnp.float32) * factor
    )
    probs = jnp.exp(scores_again - logsum)
    probs_again = probs.astype(jnp.bfloat16)
    grad_probs = jnp.einsum(
        "nthe,nshe->nhts", grad_heads, values_all, preferred_element_type=jnp.float32
    )
    grad_scores = (
        probs * (grad_probs - jnp.sum(probs * grad_probs, axis=-1, keepdims=True))
    ).astype(jnp.bfloat16)
    grad_query = (
        jnp.einsum("nhts,nshe->nthe", grad_scores, keys_all, preferred_element_type=jnp.float32)
        * factor
    )
    grad_keys = (
        jnp.einsum("nhts,nthe->nshe", grad_scores, query, preferred_element_type=jnp.float32)
        * factor
    )
    grad_values = jnp.einsum(
        "nhts,nthe->nshe", probs_again, grad_heads, preferred_element_type=jnp.float32
    )
    grad_project = jnp.stack([grad_query, grad_keys, grad_values], axis=2)
    grad_project = grad_project.reshape(images, length, 3, model_width).astype(jnp.bfloat16)
    grad_first = jnp.einsum(
        "ntuj,juk->ntk", grad_project, attention_back[:, :3, :], preferred_element_type=jnp.float32
    )
    grad_shift_one = jnp.sum(grad_first, axis=1)
    grad_scale_one = jnp.sum(grad_first * normed_one, axis=1)
    grad_input = grad_middle + norm_back(grad_first * (1.0 + scale_one), normed_one, inverse_one)
    grad_modulation = jnp.stack(
        [
            grad_shift_one,
            grad_scale_one,
            grad_gate_one,
            grad_shift_two,
            grad_scale_two,
            grad_gate_two,
        ],
        axis=1,
    )
    token_count = images * length
    first_rows = first_in.reshape(token_count, model_width)
    project_rows = grad_project.reshape(token_count, 3, model_width)
    mixed_rows = mixed.reshape(token_count, model_width)
    branch_rows = grad_branch.reshape(token_count, model_width)
    second_rows = second_in.reshape(token_count, model_width)
    gradpre_rows = grad_pre.reshape(token_count, blocks, model_width)
    hidden_rows = hidden_all.reshape(token_count, blocks, model_width)
    mlp_rows = grad_mlp.reshape(token_count, model_width)
    attention_part = jnp.einsum(
        "tuj,tk->juk", project_rows, first_rows, preferred_element_type=jnp.float32
    )
    output_part = jnp.einsum(
        "tj,tk->jk", mixed_rows, branch_rows, preferred_element_type=jnp.float32
    )[:, None, :]
    up_part = jnp.einsum(
        "tbr,tk->rbk", gradpre_rows, second_rows, preferred_element_type=jnp.float32
    )
    down_part = jnp.einsum("tbr,tk->rbk", hidden_rows, mlp_rows, preferred_element_type=jnp.float32)
    layer_grads = lax.psum_scatter(
        jnp.concatenate([attention_part, output_part, up_part, down_part], axis=1),
        ("img", "strip"),
        scatter_dimension=0,
        tiled=True,
    )
    grad_mod_all = lax.all_to_all(
        grad_modulation.astype(jnp.bfloat16),
        ("img", "strip"),
        split_axis=2,
        concat_axis=0,
        tiled=True,
    ).astype(grad_modulation.dtype)
    active_wide = active.astype(jnp.float32)
    ada_grad = jnp.einsum("nur,nk->ruk", grad_mod_all, active_wide, precision=highest)
    bias_grad = jnp.sum(grad_mod_all, axis=0)
    grad_active = jnp.einsum(
        "nur,ruk->nk", grad_mod_all, ada_weight.astype(jnp.float32), precision=highest
    )
    grad_condition = lax.psum(grad_active * silu_slope(condition), ("img", "strip"))
    table_grad = jnp.dot(selector.T, grad_condition, precision=highest)
    momentum = matrix_decay * matrix_moment + jnp.concatenate([layer_grads, ada_grad], axis=1)
    unit_count = momentum.shape[1]
    per_owner = -(-unit_count // image_groups)
    spare = per_owner * image_groups - unit_count
    outgoing = momentum.astype(jnp.bfloat16)
    outgoing = jnp.concatenate(
        [outgoing, jnp.zeros((shard_rows, spare, model_width), jnp.bfloat16)], axis=1
    )
    current = lax.all_to_all(outgoing, "img", split_axis=1, concat_axis=0, tiled=True)
    result = current.astype(jnp.float32)
    for iteration in range(NS_STEPS):
        gram = lax.psum(
            jnp.einsum("ruk,rul->ukl", current, current, preferred_element_type=jnp.float32).astype(
                jnp.bfloat16
            ),
            "strip",
        ).astype(jnp.float32)
        if iteration == 0:
            trace_sum = jnp.sum(jnp.diagonal(gram, axis1=1, axis2=2), axis=-1)
            scaling = 1.0 / (jnp.sqrt(trace_sum) + 1e-07)
            gram_low = (gram * scaling[:, None, None] * scaling[:, None, None]).astype(jnp.bfloat16)
            product = (
                jnp.einsum("ruk,ukl->rul", current, gram_low, preferred_element_type=jnp.float32)
                * scaling[None, :, None]
            )
            square = jnp.einsum(
                "ruk,ukl->rul",
                product.astype(jnp.bfloat16),
                gram_low,
                preferred_element_type=jnp.float32,
            )
            result = (
                (coef_one * scaling)[None, :, None] * current.astype(jnp.float32)
                + coef_two * product
                + coef_three * square
            )
        else:
            gram_low = gram.astype(jnp.bfloat16)
            product = jnp.einsum(
                "ruk,ukl->rul", current, gram_low, preferred_element_type=jnp.float32
            )
            square = jnp.einsum(
                "ruk,ukl->rul",
                product.astype(jnp.bfloat16),
                gram_low,
                preferred_element_type=jnp.float32,
            )
            result = (
                coef_one * current.astype(jnp.float32) + coef_two * product + coef_three * square
            )
        current = result.astype(jnp.bfloat16)
    returned = lax.all_to_all(
        result.astype(jnp.bfloat16), "img", split_axis=0, concat_axis=1, tiled=True
    ).astype(result.dtype)
    step_size = matrix_rate * 0.2 * math.sqrt(model_width)
    matrix_new = matrices - step_size * returned[:, :unit_count, :]
    bias_momentum = vector_decay * bias_moment + bias_grad
    bias_new = modulation_bias - bias_rate * bias_momentum
    table_momentum = vector_decay * table_moment + table_grad
    table_new = level_table - table_rate * table_momentum
    block_strips, grad_strips = (
        lax.all_to_all(
            total.astype(jnp.bfloat16), "strip", split_axis=1, concat_axis=0, tiled=True
        ),
        lax.all_to_all(
            grad_input.astype(jnp.bfloat16), "strip", split_axis=1, concat_axis=0, tiled=True
        ),
    )
    return (
        block_strips,
        grad_strips,
        table_grad,
        table_momentum,
        table_new,
        momentum,
        matrix_new,
        bias_momentum,
        bias_new,
    )


def solution(mesh):
    placed = (
        P("img", "strip", None),
        P("img", "strip", None),
        P(),
        P(("img", "strip"), None),
        P(("img", "strip"), None),
        P(("img", "strip"), None, None),
        P(("img", "strip"), None, None),
        P(None, ("img", "strip")),
        P(None, ("img", "strip")),
    )
    return jax.shard_map(
        on_device,
        mesh=mesh,
        in_specs=placed,
        out_specs=(
            P("img", "strip", None),
            P("img", "strip", None),
            P(("img", "strip"), None),
            P(("img", "strip"), None),
            P(("img", "strip"), None),
            P(("img", "strip"), None, None),
            P(("img", "strip"), None, None),
            P(None, ("img", "strip")),
            P(None, ("img", "strip")),
        ),
        check_vma=False,
    )
```

profile of v0, /device:TPU:0, one launch (start us, length us, event | category | flops | bytes accessed | tf_op | source)
XLA Modules:
  0.0 5670.8 jit_solution(14808957740199277512)
XLA Ops:
  19.5 122.2 %all-reduce.7.cloned.1.call-done = f32[32,2048]{1,0:T(8,128)} async-done(((f32[32,2048]{1,0:T(8,128)}), f32[32,2048]{1,0:T(8,128)}) %all-reduce.7.cloned.1.call-update) | async-done | bytes 262160 | tf_op jit(solution)/shard_map/psum | solution.py:84
  179.2 18.8 all-to-all-done.3
  201.0 144.0 %all-gather.4.cloned.1.call-done = bf16[2048,4,2048]{2,0,1:T(8,128)(2,1)} async-done(((bf16[64,4,2048]{2,0,1:T(8,128)(2,1)}), bf16[2048,4,2048]{2,0,1:T(8,128)(2,1)}) %all-gather.4.cloned.1.call-update) | async-done | bytes 33554448 | tf_op jit(solution)/shard_map/all_gather | solution.py:103
  377.6 163.8 %all-gather.6.cloned.1.call-done = bf16[2048,4,2048]{2,0,1:T(8,128)(2,1)} async-done(((bf16[64,4,2048]{2,0,1:T(8,128)(2,1)}), bf16[2048,4,2048]{2,0,1:T(8,128)(2,1)}) %all-gather.6.cloned.1.call-update) | async-done | bytes 33554448 | tf_op jit(solution)/shard_map/all_gather | solution.py:134
  560.1 177.5 %all-gather.8.cloned.1.call-done = bf16[2048,4,2048]{2,0,1:T(8,128)(2,1)} async-done(((bf16[64,4,2048]{2,0,1:T(8,128)(2,1)}), bf16[2048,4,2048]{2,0,1:T(8,128)(2,1)}) %all-gather.8.cloned.1.call-update) | async-done | bytes 33554448 | tf_op jit(solution)/shard_map/all_gather | solution.py:135
  737.6 19.0 fusion.14
  774.8 34.6 fusion.67
  838.4 23.6 convolution_bitcast_fusion.1
  867.2 31.4 convolution_bitcast_fusion
  898.6 20.6 convolution_bitcast_fusion.2
  919.2 131.9 %pad_maximum_fusion = f32[2048,12,2048]{0,2,1:T(8,128)} fusion(f32[2048,4,2048]{0,2,1:T(8,128)} %convolution_bitcast_fusion, f32[2048,4,2048]{0,2,1:T(8,128)} %convolution_bitcast_fusion.1, f32[2048,1,2048]{0,2,1:T(8,128)} %convolution_bitcast_fusion.3, f32[2048,3,2048]{0,2,1:T(8,128)} %convolution_bitcast_fusion.2), kind=kLoop, calls=%fused_computation.1 | loop fusion | flops 150994944 | bytes 402653184 | tf_op jit(solution)/shard_map/concatenate | solution.py:224
  1051.1 256.4 %copy.160 = f32[2048,12,2048]{2,1,0:T(8,128)} copy(f32[2048,12,2048]{0,2,1:T(8,128)} %pad_maximum_fusion) | data formatting | bytes 402653184 | tf_op jit(solution)/shard_map/concatenate | solution.py:224
  1354.8 2743.9 %reduce-scatter.5.cloned.1.call-done = f32[64,12,2048]{2,1,0:T(8,128)} async-done(((f32[2048,12,2048]{2,1,0:T(8,128)}), f32[64,12,2048]{2,1,0:T(8,128)}) %reduce-scatter.5.cloned.1.call-update) | async-done | bytes 6291472
  4117.7 145.1 %all_to_all.107 = bf16[64,24,2048]{2,0,1:T(8,128)(2,1)S(1)} all-to-all(bf16[64,24,2048]{2,0,1:T(8,128)(2,1)S(1)} %concatenate.29.clone), channel_id=1, replica_groups=mesh['img'=8,'strip'=4] {'img'}, dimensions={1} | all-to-all | bytes 12582912 | tf_op jit(solution)/shard_map/all_to_all | solution.py:252
  4283.8 423.1 %all-reduce.11.cloned.1.call-done = bf16[3,2048,2048]{2,1,0:T(8,128)(2,1)} async-done(((bf16[3,2048,2048]{2,1,0:T(8,128)(2,1)}), bf16[3,2048,2048]{2,1,0:T(8,128)(2,1)}) %all-reduce.11.cloned.1.call-update) | async-done | bytes 25165840 | tf_op jit(solution)/shard_map/psum | solution.py:255
  4706.9 38.4 copy.165
  4745.3 24.4 gather_fusion
  4769.8 21.0 fusion.31
  4790.9 29.3 fusion.5
  4820.2 19.9 convolution_convert_fusion
  4875.2 399.4 %all-reduce.13.cloned.1.call-done = bf16[3,2048,2048]{2,1,0:T(8,128)(2,1)} async-done(((bf16[3,2048,2048]{2,1,0:T(8,128)(2,1)}), bf16[3,2048,2048]{2,1,0:T(8,128)(2,1)}) %all-reduce.13.cloned.1.call-update) | async-done | bytes 25165840 | tf_op jit(solution)/shard_map/psum | solution.py:255
  5274.7 22.4 fusion.182
  5313.9 25.3 fusion.4
  5359.8 263.2 %all-reduce.9.cloned.1.call-done = f32[32,2048]{1,0:T(8,128)} async-done(((f32[32,2048]{1,0:T(8,128)}), f32[32,2048]{1,0:T(8,128)}) %all-reduce.9.cloned.1.call-update) | async-done | bytes 262160 | tf_op jit(solution)/shard_map/psum | solution.py:242
  (239 shorter events, 356.2 us)
Async XLA Ops:
  7.2 134.5 %all-reduce.7.cloned.1.call-start = ((), (), s32[]{:S(2)}) async-start(), calls=%async_computation.9 | async-start | bytes 524288 | tf_op jit(solution)/shard_map/psum | solution.py:84
  9.8 335.2 %all-gather.4.cloned.1.call-start = ((), (), s32[]{:S(2)}) async-start(), calls=%async_computation.10 | async-start | bytes 34603008 | tf_op jit(solution)/shard_map/all_gather | solution.py:103
  18.2 523.3 %all-gather.6.cloned.1.call-start = ((), (), s32[]{:S(2)}) async-start(), calls=%async_computation.11 | async-start | bytes 34603008 | tf_op jit(solution)/shard_map/all_gather | solution.py:134
  18.9 718.7 %all-gather.8.cloned.1.call-start = ((), (), s32[]{:S(2)}) async-start(), calls=%async_computation.12 | async-start | bytes 34603008 | tf_op jit(solution)/shard_map/all_gather | solution.py:135
  155.0 19.7 all-to-all-start
  160.1 198.0 %copy-start.35 = (f32[1,1,2048]{2,0,1:T(1,128)}, f32[1,1,2048]{2,0,1:T(1,128)S(1)}, u32[]{:S(2)}) copy-start(f32[1,1,2048]{2,0,1:T(1,128)S(1)} %get-tuple-element.79) | copy-start | bytes 24580
  160.1 209.0 %copy-start.38 = (f32[1,1,2048]{2,0,1:T(1,128)}, f32[1,1,2048]{2,0,1:T(1,128)S(1)}, u32[]{:S(2)}) copy-start(f32[1,1,2048]{2,0,1:T(1,128)S(1)} %get-tuple-element.80) | copy-start | bytes 24580
  174.7 194.4 %copy-start.2 = (bf16[4,64,2048]{2,1,0:T(8,128)(2,1)}, bf16[4,64,2048]{2,1,0:T(8,128)(2,1)S(1)}, u32[]{:S(2)}) copy-start(bf16[4,64,2048]{2,1,0:T(8,128)(2,1)S(1)} %all-to-all-done) | copy-start | bytes 3145732
  174.7 23.3 all-to-all-start.3
  178.2 3920.4 %reduce-scatter.5.cloned.1.call-start = ((), (), s32[]{:S(2)}) async-start(), calls=%async_computation.16 | async-start | bytes 276824064
  178.6 179.5 %copy-start.40 = (f32[256]{0:T(256)}, f32[256]{0:T(256)S(1)}, u32[]{:S(2)}) copy-start(f32[256]{0:T(256)S(1)} %div.56) | copy-start | bytes 3076
  179.2 178.9 %copy-start.43 = (f32[256]{0:T(256)}, f32[256]{0:T(256)S(1)}, u32[]{:S(2)}) copy-start(f32[256]{0:T(256)S(1)} %add_rsqrt_fusion.1) | copy-start | bytes 3076
  541.4 196.2 %copy-start.27 = (bf16[256,2048]{1,0:T(8,128)(2,1)S(1)}, bf16[256,2048]{1,0:T(8,128)(2,1)}, u32[]{:S(2)}) copy-start(bf16[256,2048]{1,0:T(8,128)(2,1)} %fusion.66) | copy-start | bytes 3145732
  1307.7 3399.2 %all-reduce.11.cloned.1.call-start = ((), (), s32[]{:S(2)}) async-start(), calls=%async_computation.14 | async-start | bytes 50331648 | tf_op jit(solution)/shard_map/psum | solution.py:255
  1350.3 2764.2 %copy-start.29 = (bf16[1,6,32,64]{3,2,1,0:T(8,128)(2,1)}, bf16[1,6,32,64]{3,2,1,0:T(8,128)(2,1)S(1)}, u32[]{:S(2)}) copy-start(bf16[1,6,32,64]{3,2,1,0:T(8,128)(2,1)S(1)} %all_to_all.89) | copy-start | bytes 73732
  4283.7 991.0 %all-reduce.13.cloned.1.call-start = ((), (), s32[]{:S(2)}) async-start(), calls=%async_computation.15 | async-start | bytes 50331648 | tf_op jit(solution)/shard_map/psum | solution.py:255
  4857.9 452.0 %all-to-all-start.2 = ((bf16[4,2,65536]{2,1,0:T(2,128)(2,1)}), bf16[4,2,65536]{2,1,0:T(2,128)(2,1)}, u32[]{:S(2)}, u32[]{:S(2)}) async-start(bf16[4,2,65536]{2,1,0:T(2,128)(2,1)} %reshape.632), calls=%async_computation.2 | async-start | bytes 2097152 | tf_op jit(solution)/shard_map/all_to_all | solution.py:305
  5309.9 40.9 all-to-all-start.4
  5350.8 272.2 %copy-start.28 = (f32[32,2048]{1,0:T(8,128)S(1)}, f32[32,2048]{1,0:T(8,128)}, u32[]{:S(2)}) copy-start(f32[32,2048]{1,0:T(8,128)} %param.12) | copy-start | bytes 786436
  5350.8 272.2 %copy-start.32 = (f32[32,2048]{1,0:T(8,128)S(1)}, f32[32,2048]{1,0:T(8,128)}, u32[]{:S(2)}) copy-start(f32[32,2048]{1,0:T(8,128)} %param.13) | copy-start | bytes 786436
  5350.8 272.2 %copy-start.53 = (s32[32]{0:T(128)S(1)}, s32[32]{0:T(128)}, u32[]{:S(2)}) copy-start(s32[32]{0:T(128)} %param.11) | copy-start | bytes 388
  5350.8 272.2 %copy-start.55 = (s32[32]{0:T(128)S(1)}, s32[32]{0:T(128)}, u32[]{:S(2)}) copy-start(s32[32]{0:T(128)} %copy-done.54) | copy-start | bytes 388
  5350.8 295.1 %all-to-all-start.7 = ((bf16[512,3,2048]{2,1,0:T(4,128)(2,1)}), bf16[512,3,2048]{2,1,0:T(4,128)(2,1)}, u32[]{:S(2)}, u32[]{:S(2)}) async-start(bf16[512,3,2048]{2,1,0:T(4,128)(2,1)} %copy.176), calls=%async_computation.7 | async-start | bytes 16777216 | tf_op jit(solution)/shard_map/all_to_all | solution.py:295
  5356.5 266.5 %all-reduce.9.cloned.1.call-start = ((), (), s32[]{:S(2)}) async-start(), calls=%async_computation.13 | async-start | bytes 524288 | tf_op jit(solution)/shard_map/psum | solution.py:242
  (47 other events, 927.5 us)
Sparse Core Ops, SparseCore 0:
  14.1 127.5 all-reduce.6
  145.2 199.7 all-gather.3
  348.5 192.8 all-gather.5
  544.8 192.7 all-gather.7
  1307.8 2790.8 reduce-scatter.4
  4283.8 423.0 all-reduce.10
  4840.3 434.3 all-reduce.12
  5363.4 259.5 all-reduce.8
where the time goes:
time: 5680 us; the launch traced here: 5670 us
  waiting for transfers between devices  4470 us (79%)
  local copies, waits for them, and re-layouts  423 us (7%)
  matrix products  373 us (7%)
  other arithmetic  200 us (4%)
  blocking collectives  166 us (3%)
    unnamed x9, waiting for transfers between devices  2750 us
    psum x2, waiting for transfers between devices, on_device(): lax.psum(jnp.einsum('ruk,rul->ukl', current, current, preferred_element_t...  823 us
    psum x1, waiting for transfers between devices, on_device(): lax.psum(grad_active * silu_slope(condition), ('img', 'strip'))  263 us
    concatenate x1, local copies, waits for them, and re-layouts, on_device(): jnp.concatenate([attention_part, output_part, up_part, down_part], axis=1)  256 us
    all_gather x1, waiting for transfers between devices, on_device(): lax.all_gather(down_shard, ('img', 'strip'), axis=0, tiled=True)  177 us
    all_gather x1, waiting for transfers between devices, on_device(): lax.all_gather(up_shard, ('img', 'strip'), axis=0, tiled=True)  164 us
    all_to_all x1, blocking collectives, on_device(): lax.all_to_all(outgoing, 'img', split_axis=1, concat_axis=0, tiled=True)  145 us
    all_gather x1, waiting for transfers between devices, on_device(): lax.all_gather(matrices[:, :4, :].astype(jnp.bfloat16), ('img', 'strip'),...  144 us
  transfers between devices with their start and end apart: 13, of which 10 were waited for; matrix products, arithmetic and copies ran while one was open for 4% of the time, Pallas kernels for 0%

commit v1 on v0

v1 whole, which is shorter than its diff:
```python
import math

import jax
import jax.numpy as jnp
from jax import lax
from jax.sharding import PartitionSpec as P

HEADS = 16
HD = 128

highest = lax.Precision.HIGHEST
norm_eps = 1e-06
coef_one = 3.4445
coef_two = -4.775
coef_three = 2.0315
matrix_decay = 0.95
vector_decay = 0.9
matrix_rate = 0.5
bias_rate = 0.003
table_rate = 0.02

WORLD = ("img", "strip")
CORE, ALONG_X, ALONG_Y = 1, 2, 4
TEAM = 8
low = jnp.bfloat16
wide = jnp.float32


def dot(spec, left, right):
    return jnp.einsum(spec, left, right, preferred_element_type=wide)


def add(left, right):
    return left.astype(wide) + right.astype(wide)


def normalize(values):
    center = values - jnp.mean(values, axis=-1, keepdims=True)
    inverse = lax.rsqrt(jnp.mean(center * center, axis=-1, keepdims=True) + norm_eps)
    return (center * inverse, inverse)


def norm_back(grad_hat, normed, inverse):
    mean_grad = jnp.mean(grad_hat, axis=-1, keepdims=True)
    mean_cross = jnp.mean(grad_hat * normed, axis=-1, keepdims=True)
    return inverse * (grad_hat - mean_grad - normed * mean_cross)


def gelu_slope(values):
    cumulative = 0.5 * (1.0 + lax.erf(values * 0.7071067811865476))
    density = jnp.exp(-0.5 * values * values) * 0.3989422804014327
    return cumulative + values * density


def silu_slope(values):
    logistic = jax.nn.sigmoid(values)
    return logistic * (1.0 + values * (1.0 - logistic))


class Fabric:
    def __init__(self):
        self.count = lax.axis_size("img") * lax.axis_size("strip")
        self.planes = self.count // TEAM
        self.me = lax.axis_index(WORLD)
        self.plane = self.me // TEAM
        self.seat = self.me % TEAM

    def swap(self, value, bit):
        return lax.ppermute(value, WORLD, [(d, d ^ bit) for d in range(self.count)])

    def hop(self, value, step, first, last):
        pairs = [(d, d + step * TEAM) for d in range(first * TEAM, (last + 1) * TEAM)]
        return lax.ppermute(value, WORLD, pairs)

    def turn(self, value, offset, limit=None):
        pairs = []
        for d in range(self.count):
            target = (d // TEAM + offset) % self.planes
            if limit is None or target < limit:
                pairs.append((d, target * TEAM + d % TEAM))
        return lax.ppermute(value, WORLD, pairs)

    def back(self, value, offset, limit):
        pairs = []
        for d in range(self.count):
            if d // TEAM < limit:
                pairs.append((d, (d // TEAM - offset) % self.planes * TEAM + d % TEAM))
        return lax.ppermute(value, WORLD, pairs)

    def gather_planes(self, shard):
        count = self.planes
        right, left = [shard], [shard]
        for k in range(1, count):
            right.append(self.hop(right[-1], 1, k - 1, count - 2))
            left.append(self.hop(left[-1], -1, 1, count - k))
        slots = [shard]
        for j in range(1, count):
            slots.append(jnp.where(self.plane >= j, right[j], left[count - j]))
        return jnp.concatenate(slots, axis=0)

    def reduce_planes(self, slots):
        count = self.planes
        right = left = None
        for k in range(1, count):
            onward = slots[k] if right is None else add(slots[k], right).astype(low)
            right = self.hop(onward, 1, 0, k - 1)
            onward = slots[count - k] if left is None else add(slots[count - k], left).astype(low)
            left = self.hop(onward, -1, count - k, count - 1)
        return slots[0].astype(wide) + right.astype(wide) + left.astype(wide)

    def share(self, first, second):
        first_x = self.swap(first, ALONG_X)
        second_y = self.swap(second, ALONG_Y)
        first_y = self.swap(first, ALONG_Y)
        second_x = self.swap(second, ALONG_X)
        first_xy = self.swap(first_x, ALONG_Y)
        second_yx = self.swap(second_y, ALONG_X)
        own_first = [first, first_y, first_x, first_xy]
        own_second = [second, second_x, second_y, second_yx]
        far_first = [self.swap(piece, CORE) for piece in own_first]
        far_second = [self.swap(piece, CORE) for piece in own_second]
        return (
            jnp.concatenate(own_first + far_first, axis=0),
            jnp.concatenate(own_second + far_second, axis=0),
        )

    def settle(self, first, second):
        def halves(near, far, bit):
            return add(near, self.swap(far, bit))

        def chain(parts, one, two):
            parts = parts.reshape((2, 2, 2) + (parts.shape[0] // 8,) + parts.shape[1:])
            parts = halves(parts[0], parts[1], CORE).astype(low)
            parts = halves(parts[0], parts[1], one).astype(low)
            return halves(parts[0], parts[1], two)

        return chain(first, ALONG_X, ALONG_Y), chain(second, ALONG_Y, ALONG_X)


def to_images(rows, second):
    inner = rows.shape[0] // 16
    rows = rows.reshape((2, 2, 2, 2, inner) + rows.shape[1:])
    tail = tuple(range(5, rows.ndim))
    order = (1, 3, 0, 2, 4) if second else (2, 3, 0, 1, 4)
    return rows.transpose(order + tail).reshape((4, 4 * inner) + rows.shape[5:])


def to_rows(images, second):
    inner = images.shape[1] // 4
    images = images.reshape((2, 2, 2, 2, inner) + images.shape[2:])
    tail = tuple(range(5, images.ndim))
    order = (2, 0, 3, 1, 4) if second else (2, 3, 0, 1, 4)
    return images.transpose(order + tail).reshape((16 * inner,) + images.shape[5:])


def spread(values, second):
    if second:
        return values[None, :, None, :, None]
    return values[None, None, :, :, None]


def attend(projected):
    query, keys_all, values_all = projected[:, :, 0], projected[:, :, 1], projected[:, :, 2]
    scores = dot("nthe,nshe->nhts", query, keys_all) * HD ** (-0.5)
    summit = jnp.max(scores, axis=-1, keepdims=True)
    exponent = jnp.exp(scores - summit)
    totals = jnp.sum(exponent, axis=-1, keepdims=True)
    probs = exponent / totals
    mixed = dot("nhts,nshe->nthe", probs.astype(low), values_all)
    return mixed.astype(low), probs


def attend_back(projected, probs, grad_heads):
    factor = HD ** (-0.5)
    query, keys_all, values_all = projected[:, :, 0], projected[:, :, 1], projected[:, :, 2]
    grad_probs = dot("nthe,nshe->nhts", grad_heads, values_all)
    grad_scores = (
        probs * (grad_probs - jnp.sum(probs * grad_probs, axis=-1, keepdims=True))
    ).astype(low)
    grad_query = dot("nhts,nshe->nthe", grad_scores, keys_all) * factor
    grad_keys = dot("nhts,nthe->nshe", grad_scores, query) * factor
    grad_values = dot("nhts,nthe->nshe", probs.astype(low), grad_heads)
    return jnp.stack([grad_query, grad_keys, grad_values], axis=2).astype(low)


def on_device(
    tokens,
    cotangent,
    bin_ids,
    level_table,
    table_moment,
    matrices,
    matrix_moment,
    modulation_bias,
    bias_moment,
):
    fabric = Fabric()
    planes, plane, seat = fabric.planes, fabric.plane, fabric.seat
    strips = lax.axis_size("strip")
    here, inner, width = tokens.shape
    shard_rows, units, _ = matrices.shape
    images = bin_ids.shape[0]
    table_rows = level_table.shape[0]
    blocks = (units - 10) // 2
    start_down = 4 + blocks
    start_ada = 4 + 2 * blocks
    slot_rows = planes * shard_rows

    by_unit = matrices.astype(low).transpose(1, 0, 2)

    def gathered(first, last):
        rows = by_unit[first:last].reshape((last - first) * shard_rows, width)
        return fabric.gather_planes(rows)

    attention = gathered(0, 4)
    up_weight = gathered(4, start_down)
    down_weight = gathered(start_down, start_ada)

    def token_halves(values):
        half = here // 2
        return (
            values[:half].reshape(half * inner, width),
            values[half:].reshape(half * inner, width),
        )

    whole_tokens = fabric.share(*token_halves(tokens))
    whole_upstream = fabric.share(*token_halves(cotangent))

    row_ids = fabric.me * table_rows + jnp.arange(table_rows, dtype=jnp.int32)
    selector = (bin_ids[:, None] == row_ids[None, :]).astype(wide)
    active_rows = jax.nn.silu(level_table).astype(low)
    active = jnp.dot(selector.astype(low), active_rows, preferred_element_type=wide).astype(low)
    others = [fabric.turn(active, offset) for offset in range(1, planes)]
    for other in others:
        active = active + other
    for bit in (CORE, ALONG_X, ALONG_Y):
        active = active + fabric.swap(active, bit)
    ada_weight = matrices[:, start_ada:, :].astype(low)
    mod_columns = dot("nk,ruk->nur", active, ada_weight) + modulation_bias[None]
    in_plane = images // planes
    mod_parts = jnp.broadcast_to(
        mod_columns.reshape(planes, 1, in_plane, 6, shard_rows),
        (planes, TEAM, in_plane, 6, shard_rows),
    ).reshape(fabric.count, in_plane, 6, shard_rows)
    mod_parts = lax.all_to_all(mod_parts, WORLD, split_axis=0, concat_axis=0, tiled=True)
    modulation = mod_parts.transpose(1, 2, 0, 3).reshape(2, here, 6, width)
    side = seat // 4
    modulation = jnp.where(side == 0, modulation, modulation[::-1])
    local = modulation[0][:, :, None, :]
    shift_one, scale_one, gate_one = local[:, 0], local[:, 1], local[:, 2]
    shift_two, scale_two, gate_two = local[:, 3], local[:, 4], local[:, 5]

    def half_modulation(which, second):
        half = here // 2
        chosen = modulation[:, half:] if second else modulation[:, :half]
        return spread(chosen[:, :, which], second)

    def open_rows(rows):
        return rows.reshape(2, 2, 2, 2, inner, width)

    first_in = []
    for second in (0, 1):
        normed, _ = normalize(open_rows(whole_tokens[second]).astype(wide))
        value = normed * (1.0 + half_modulation(1, second)) + half_modulation(0, second)
        first_in.append(value.astype(low).reshape(-1, width))
    grad_mlp = [
        (open_rows(whole_upstream[second]).astype(wide) * half_modulation(5, second))
        .astype(low)
        .reshape(-1, width)
        for second in (0, 1)
    ]

    peers = HD // shard_rows
    heads = planes // peers
    attention = attention.reshape(planes, 4, shard_rows, width)
    place = fabric.me % peers

    def mates(offset):
        return [
            (d, d // peers * peers + (d % peers + offset) % peers) for d in range(fabric.count)
        ]

    pieces = [lax.dynamic_slice_in_dim(attention, place * heads, heads, 0)]
    for offset in range(1, peers):
        target = (place + offset) % peers
        payload = lax.dynamic_slice_in_dim(attention, target * heads, heads, 0)
        pieces.append(lax.ppermute(payload, WORLD, mates(offset)))
    attention = jnp.stack(pieces).transpose(2, 1, 0, 3, 4).reshape(4, heads * HD, width)
    weight_in = attention[:3].reshape(3 * heads * HD, width)
    weight_out = attention[3]

    projected, probs, mixed, branch_parts = [], [], [], []
    for second in (0, 1):
        rows = dot("tk,jk->tj", first_in[second], weight_in).astype(low)
        whole = to_images(rows, second).reshape(4, 4 * inner, 3, heads, HD)
        blend, kept = attend(whole)
        blend = to_rows(blend.reshape(4, 4 * inner, heads * HD), second)
        projected.append(whole)
        probs.append(kept)
        mixed.append(blend)
        branch_parts.append(dot("tj,jk->tk", blend, weight_out).astype(low))

    def joined(parts):
        return jnp.concatenate(
            [part.reshape(here // 2, inner, width) for part in fabric.settle(*parts)], axis=0
        )

    branch = joined(branch_parts)
    inputs = tokens.astype(wide)
    middle = inputs + gate_one * branch
    normed_two, inverse_two = normalize(middle)
    second_in = fabric.share(
        *token_halves((normed_two * (1.0 + scale_two) + shift_two).astype(low))
    )
    preact = [dot("tk,jk->tj", rows, up_weight) for rows in second_in]
    hidden = [jax.nn.gelu(rows, approximate=False).astype(low) for rows in preact]
    mlp_parts = [dot("tj,jk->tk", rows, down_weight).astype(low) for rows in hidden]
    mlp_out = joined(mlp_parts)
    block_out = (middle + gate_two * mlp_out).astype(low)

    def over_halves(left, right):
        return dot("tj,tk->jk", jnp.concatenate(left, 0), jnp.concatenate(right, 0)).astype(low)

    down_grad = over_halves(hidden, grad_mlp)
    grad_pre = [
        (dot("tk,jk->tj", grad_mlp[s], down_weight) * gelu_slope(preact[s])).astype(low)
        for s in (0, 1)
    ]
    grad_in = joined([dot("tj,jk->tk", rows, up_weight).astype(low) for rows in grad_pre])
    up_grad = over_halves(grad_pre, second_in)

    grad_total = cotangent.astype(wide)
    grad_gate_two = jnp.sum(grad_total * mlp_out, axis=1)
    grad_shift_two = jnp.sum(grad_in, axis=1)
    grad_scale_two = jnp.sum(grad_in * normed_two, axis=1)
    grad_middle = grad_total + norm_back(grad_in * (1.0 + scale_two), normed_two, inverse_two)
    grad_gate_one = jnp.sum(grad_middle * branch, axis=1)
    grad_branch = fabric.share(*token_halves((grad_middle * gate_one).astype(low)))

    grad_project, grad_first_parts = [], []
    for second in (0, 1):
        grad_mixed = dot("tk,jk->tj", grad_branch[second], weight_out).astype(low)
        grad_heads = to_images(grad_mixed, second).reshape(4, 4 * inner, heads, HD)
        whole = attend_back(projected[second], probs[second], grad_heads)
        whole = to_rows(whole.reshape(4, 4 * inner, 3 * heads * HD), second)
        grad_project.append(whole)
        grad_first_parts.append(dot("tj,jk->tk", whole, weight_in).astype(low))
    in_grad = over_halves(grad_project, first_in).reshape(3, heads * HD, width)
    out_grad = over_halves(mixed, list(grad_branch)).reshape(1, heads * HD, width)
    attention_grad = jnp.concatenate([in_grad, out_grad], axis=0)
    attention_grad = attention_grad.reshape(4, heads, peers, shard_rows, width)
    attention_grad = attention_grad.transpose(2, 1, 0, 3, 4)
    returned = [attention_grad[0]]
    for offset in range(1, peers):
        returned.append(lax.ppermute(attention_grad[offset], WORLD, mates(peers - offset)))
    attention_grad = jnp.concatenate(returned + returned[:-1], axis=0)
    attention_grad = lax.dynamic_slice_in_dim(
        attention_grad, (peers - place) % peers * heads, planes, 0
    ).reshape(planes, 4 * shard_rows, width)

    grad_first = joined(grad_first_parts)
    normed_one, inverse_one = normalize(inputs)
    grad_shift_one = jnp.sum(grad_first, axis=1)
    grad_scale_one = jnp.sum(grad_first * normed_one, axis=1)
    input_grad = (
        grad_middle + norm_back(grad_first * (1.0 + scale_one), normed_one, inverse_one)
    ).astype(low)

    def to_holders(parts):
        stacked = jnp.stack(parts, axis=1).astype(low)
        held = lax.all_to_all(stacked, WORLD, split_axis=2, concat_axis=0, tiled=True)
        held = held.reshape(fabric.count // strips, strips, here, len(parts), shard_rows)
        return jnp.sum(held.astype(wide), axis=1).reshape(images, len(parts), shard_rows)

    late_mod = to_holders([grad_gate_one, grad_shift_two, grad_scale_two, grad_gate_two])
    early_mod = to_holders([grad_shift_one, grad_scale_one])
    grad_mod_all = jnp.concatenate([early_mod, late_mod], axis=1)
    active_wide = active.astype(wide)

    def ada_grad(grads):
        return jnp.einsum("nur,nk->urk", grads, active_wide, precision=highest)

    bias_grad = jnp.sum(grad_mod_all, axis=0)
    grad_active = lax.psum(
        jnp.einsum("nur,ruk->nk", grad_mod_all, ada_weight.astype(wide), precision=highest), WORLD
    )
    table_grad = jnp.dot(selector.T, grad_active, precision=highest) * silu_slope(level_table)

    def summed(grad):
        return fabric.reduce_planes(grad.reshape(planes, -1, width)).reshape(
            -1, shard_rows, width
        )

    moment = matrix_moment.transpose(1, 0, 2)

    def fresh(first, grad):
        return matrix_decay * moment[first : first + grad.shape[0]] + grad

    def orthogonal(batch):
        count = batch.shape[0]
        own = batch.astype(low)
        if count < planes:
            own = jnp.concatenate(
                [own, jnp.zeros((planes - count, shard_rows, width), low)], axis=0
            )
        rows = [lax.dynamic_index_in_dim(own, plane, 0, keepdims=False)]
        for offset in range(1, planes):
            payload = lax.dynamic_index_in_dim(own, (plane + offset) % planes, 0, keepdims=False)
            rows.append(fabric.turn(payload, offset, count))
        rows = jnp.concatenate(rows, axis=0)
        half = slot_rows // 2
        first, second = fabric.share(rows[:half], rows[half:])
        current = jnp.concatenate([first, second], axis=0)
        trace_sum = jnp.sum(jnp.square(current.astype(wide)))
        scaling = 1.0 / (jnp.sqrt(trace_sum) + 1e-07)
        gram_low = (dot("rk,rl->kl", current, current) * scaling * scaling).astype(low)
        product = dot("rk,kl->rl", current, gram_low) * scaling
        square = dot("rk,kl->rl", product.astype(low), gram_low)
        result = (coef_one * scaling) * current.astype(wide) + coef_two * product
        current = (result + coef_three * square).astype(low)
        gram_low = dot("rk,rl->kl", current, current).astype(low)
        mine = jnp.concatenate([current[:half], current[slot_rows * 4 : slot_rows * 4 + half]], 0)
        product = dot("rk,kl->rl", mine, gram_low)
        square = dot("rk,kl->rl", product.astype(low), gram_low)
        result = coef_one * mine.astype(wide) + coef_two * product + coef_three * square
        result = result.astype(low).reshape(planes, shard_rows, width)
        done = [result[0]]
        for offset in range(1, planes):
            done.append(fabric.back(result[offset], offset, count))
        done = jnp.concatenate([jnp.stack(done), jnp.stack(done[:-1])], axis=0)
        start = (planes - plane) % planes
        return lax.dynamic_slice_in_dim(done, start, planes, 0)[:count]

    down_momentum = fresh(start_down, summed(down_grad))
    up_momentum = fresh(4, summed(up_grad))
    late_momentum = fresh(start_ada + 2, ada_grad(late_mod))
    attention_momentum = fresh(0, summed(attention_grad))
    early_momentum = fresh(start_ada, ada_grad(early_mod))
    down_ortho = orthogonal(down_momentum)
    up_ortho = orthogonal(up_momentum)
    late_ortho = orthogonal(late_momentum)
    attention_ortho = orthogonal(attention_momentum)
    early_ortho = orthogonal(early_momentum)
    momentum = jnp.concatenate(
        [attention_momentum, up_momentum, down_momentum, early_momentum, late_momentum], axis=0
    ).transpose(1, 0, 2)
    ortho = jnp.concatenate(
        [attention_ortho, up_ortho, down_ortho, early_ortho, late_ortho], axis=0
    ).transpose(1, 0, 2)
    step_size = matrix_rate * 0.2 * math.sqrt(width)
    matrix_new = matrices - step_size * ortho.astype(wide)
    bias_momentum = vector_decay * bias_moment + bias_grad
    bias_new = modulation_bias - bias_rate * bias_momentum
    table_momentum = vector_decay * table_moment + table_grad
    table_new = level_table - table_rate * table_momentum
    return (
        block_out,
        input_grad,
        table_grad,
        table_momentum,
        table_new,
        momentum,
        matrix_new,
        bias_momentum,
        bias_new,
    )


def solution(mesh):
    whole = P(("img", "strip"), None, None)
    table = P(("img", "strip"), None)
    strip = P("img", "strip", None)
    bias = P(None, ("img", "strip"))
    return jax.shard_map(
        on_device,
        mesh=mesh,
        in_specs=(strip, strip, P(), table, table, whole, whole, bias, bias),
        out_specs=(strip, strip, table, table, table, whole, whole, bias, bias),
        check_vma=False,
    )
```

time: 5680 us -> 2290 us (0.40)
  waiting for transfers between devices: 4470 us -> 765 us
  starting transfers between devices: 21.5 us -> 352 us
  matrix products: 373 us -> 699 us
  blocking collectives: 166 us -> 0 us
  local copies, waits for them, and re-layouts: 423 us -> 266 us
    unnamed x9 -> x1, waiting for transfers between devices: 2750 us -> 0.02 us
    psum x4 -> x1, waiting for transfers between devices: 1210 us -> 124 us  [on_device(): lax.psum(jnp.einsum('nur,ruk->nk', grad_mod_all, ada_weight.astype(wide),...]
    ppermute x0 -> x224, waiting for transfers between devices: none -> 622 us  [the longest x153 372 us: swap(): return lax.ppermute(value, WORLD, [(d, d ^ bit) for d in range(self.count)])]
    all_gather x3 -> x0, waiting for transfers between devices: 485 us -> none  [the longest x1 177 us: on_device(): lax.all_gather(down_shard, ('img', 'strip'), axis=0, tiled=True)]
    ppermute x0 -> x224, starting transfers between devices: none -> 341 us  [the longest x36 110 us: hop(): return lax.ppermute(value, WORLD, pairs)]
    dot_general x29 -> x66, matrix products: 373 us -> 692 us  [the longest x61 684 us: dot(): return jnp.einsum(spec, left, right, preferred_element_type=wide)]
    concatenate x2 -> x22, local copies, waits for them, and re-layouts: 257 us -> 16.3 us  [the longest x5 4.1 us: orthogonal(): current = jnp.concatenate([first, second], axis=0)]
    all_to_all x3 -> x0, blocking collectives: 166 us -> none  [the longest x1 145 us: on_device(): lax.all_to_all(outgoing, 'img', split_axis=1, concat_axis=0, tiled=True)]
  transfers between devices with their start and end apart: 13 -> 228, of which waited for: 10 -> 74; matrix products, arithmetic and copies ran while one was open for 4% -> 40% of each run, Pallas kernels for 0% -> 0%
where the time goes in v1:
time: 2290 us; the launch traced here: 2270 us
  waiting for transfers between devices  765 us (33%)
  matrix products  699 us (31%)
  starting transfers between devices  352 us (15%)
  local copies, waits for them, and re-layouts  266 us (12%)
  other arithmetic  165 us (7%)
    dot_general x61, matrix products, dot(): return jnp.einsum(spec, left, right, preferred_element_type=wide)  684 us
    ppermute x153, waiting for transfers between devices, swap(): return lax.ppermute(value, WORLD, [(d, d ^ bit) for d in range(self.count)])  372 us
    unnamed x454, local copies, waits for them, and re-layouts  163 us
    ppermute x36, waiting for transfers between devices, hop(): return lax.ppermute(value, WORLD, pairs)  156 us
    psum x1, waiting for transfers between devices, on_device(): lax.psum(jnp.einsum('nur,ruk->nk', grad_mod_all, ada_weight.astype(wide),...  124 us
    ppermute x36, starting transfers between devices, hop(): return lax.ppermute(value, WORLD, pairs)  110 us
    ppermute x153, starting transfers between devices, swap(): return lax.ppermute(value, WORLD, [(d, d ^ bit) for d in range(self.count)])  109 us
    ppermute x15, starting transfers between devices, back(): return lax.ppermute(value, WORLD, pairs)  86.5 us
  transfers between devices with their start and end apart: 228, of which 74 were waited for; matrix products, arithmetic and copies ran while one was open for 40% of the time, Pallas kernels for 0%

profile of v1, /device:TPU:0, one launch (start us, length us, event | category | flops | bytes accessed | tf_op | source)
XLA Modules:
  0.0 2268.8 jit_solution(7596515761273299474)
XLA Ops:
  193.4 38.6 %collective-permute-done.15 = bf16[256,2048]{1,0:T(8,128)(2,1)S(1)} collective-permute-done((bf16[256,2048]{1,0:T(8,128)(2,1)}, bf16[256,2048]{1,0:T(8,128)(2,1)S(1)}, u32[]{:S(2)}, u32[]{:S(2)}) %collective-permute-start.15) | collective-permute-done | bytes 1048608 | tf_op jit(solution)/shard_map/ppermute | solution.py:73
  392.7 20.0 collective-permute-done.21
  1041.6 124.5 %all-reduce.3.cloned.1.call-done = f32[32,2048]{1,0:T(8,128)} async-done(((f32[32,2048]{1,0:T(8,128)}), f32[32,2048]{1,0:T(8,128)}) %all-reduce.3.cloned.1.call-update) | async-done | bytes 262160 | tf_op jit(solution)/shard_map/psum | solution.py:384
  1351.0 21.4 collective-permute-done.192
  1556.9 23.0 %multiply_convert_fusion = bf16[2048,2048]{1,0:T(8,128)(2,1)S(1)} fusion(bf16[2048,2048]{1,0:T(8,128)(2,1)} %copy-done.15, f32[]{:T(128)S(6)} %div.120), kind=kOutput, calls=%fused_computation.32 | convolution fusion | flops 17192452096 | bytes 16777220 | tf_op jit(solution)/shard_map/rk,rl->kl/dot_general | solution.py:30
  1583.1 20.6 fusion.279
  1603.7 30.0 %fusion.21 = bf16[2048,2048]{1,0:T(8,128)(2,1)} fusion(bf16[2048,2048]{1,0:T(8,128)(2,1)} %copy-done.15, f32[2048,2048]{1,0:T(8,128)} %fusion.279, bf16[2048,2048]{1,0:T(8,128)(2,1)} %copy-done.122, f32[]{:T(128)S(6)} %div.120, f32[]{:T(128)S(6)} %mul.758), kind=kOutput, calls=%fused_computation.31 | convolution fusion | flops 17221812224 | bytes 41943048 | tf_op jit(solution)/shard_map/rk,kl->rl/dot_general | solution.py:30
  1633.8 22.8 %convolution_convert_fusion = bf16[2048,2048]{1,0:T(8,128)(2,1)S(1)} fusion(bf16[2048,2048]{1,0:T(8,128)(2,1)} %fusion.21), kind=kOutput, calls=%fused_computation.70 | convolution fusion | flops 17184063488 | bytes 16777216 | tf_op jit(solution)/shard_map/rk,rl->kl/dot_general | solution.py:30
  1673.4 23.8 %multiply_convert_fusion.1 = bf16[2048,2048]{1,0:T(8,128)(2,1)} fusion(bf16[2048,2048]{1,0:T(8,128)(2,1)} %copy-done.18, f32[]{:T(128)S(6)} %div.119), kind=kOutput, calls=%fused_computation.33 | convolution fusion | flops 17192452096 | bytes 16777220 | tf_op jit(solution)/shard_map/rk,rl->kl/dot_general | solution.py:30
  1697.2 24.4 %fusion.278 = f32[2048,2048]{1,0:T(8,128)} fusion(bf16[2048,2048]{1,0:T(8,128)(2,1)} %copy-done.18, bf16[2048,2048]{1,0:T(8,128)(2,1)} %multiply_convert_fusion.1), kind=kOutput, calls=%fused_computation.808 | convolution fusion | flops 17179869184 | bytes 33554432 | tf_op jit(solution)/shard_map/rk,kl->rl/dot_general | solution.py:30
  1721.6 29.6 %fusion.17 = bf16[2048,2048]{1,0:T(8,128)(2,1)} fusion(bf16[2048,2048]{1,0:T(8,128)(2,1)} %copy-done.18, f32[2048,2048]{1,0:T(8,128)} %fusion.278, bf16[2048,2048]{1,0:T(8,128)(2,1)} %multiply_convert_fusion.1, f32[]{:T(128)S(6)} %div.119, f32[]{:T(128)S(6)} %mul.746), kind=kOutput, calls=%fused_computation.27 | convolution fusion | flops 17221812224 | bytes 41943048 | tf_op jit(solution)/shard_map/rk,kl->rl/dot_general | solution.py:30
  1751.3 22.6 convolution_convert_fusion.1
  1793.1 24.1 %multiply_convert_fusion.2 = bf16[2048,2048]{1,0:T(8,128)(2,1)} fusion(bf16[2048,2048]{1,0:T(8,128)(2,1)} %constant_dynamic-update-slice_fusion.154, f32[]{:T(128)S(6)} %div.118), kind=kOutput, calls=%fused_computation.34 | convolution fusion | flops 17192452096 | bytes 16777220 | tf_op jit(solution)/shard_map/rk,rl->kl/dot_general | solution.py:30
  1817.2 24.2 %fusion.277 = f32[2048,2048]{1,0:T(8,128)} fusion(bf16[2048,2048]{1,0:T(8,128)(2,1)} %constant_dynamic-update-slice_fusion.154, bf16[2048,2048]{1,0:T(8,128)(2,1)} %multiply_convert_fusion.2), kind=kOutput, calls=%fused_computation.807 | convolution fusion | flops 17179869184 | bytes 33554432 | tf_op jit(solution)/shard_map/rk,kl->rl/dot_general | solution.py:30
  1841.4 30.4 %fusion.13 = bf16[2048,2048]{1,0:T(8,128)(2,1)} fusion(bf16[2048,2048]{1,0:T(8,128)(2,1)} %constant_dynamic-update-slice_fusion.154, f32[2048,2048]{1,0:T(8,128)} %fusion.277, bf16[2048,2048]{1,0:T(8,128)(2,1)} %multiply_convert_fusion.2, f32[]{:T(128)S(6)} %div.118, f32[]{:T(128)S(6)} %mul.734), kind=kOutput, calls=%fused_computation.23 | convolution fusion | flops 17221812224 | bytes 41943048 | tf_op jit(solution)/shard_map/rk,kl->rl/dot_general | solution.py:30
  1871.7 22.5 convolution_convert_fusion.2
  1912.6 23.8 %multiply_convert_fusion.3 = bf16[2048,2048]{1,0:T(8,128)(2,1)} fusion(bf16[2048,2048]{1,0:T(8,128)(2,1)} %copy-done.20, f32[]{:T(128)S(6)} %div.117), kind=kOutput, calls=%fused_computation.35 | convolution fusion | flops 17192452096 | bytes 16777220 | tf_op jit(solution)/shard_map/rk,rl->kl/dot_general | solution.py:30
  1936.4 24.4 %fusion.276 = f32[2048,2048]{1,0:T(8,128)} fusion(bf16[2048,2048]{1,0:T(8,128)(2,1)} %copy-done.20, bf16[2048,2048]{1,0:T(8,128)(2,1)} %multiply_convert_fusion.3), kind=kOutput, calls=%fused_computation.806 | convolution fusion | flops 17179869184 | bytes 33554432 | tf_op jit(solution)/shard_map/rk,kl->rl/dot_general | solution.py:30
  1960.9 30.3 %fusion.9 = bf16[2048,2048]{1,0:T(8,128)(2,1)} fusion(bf16[2048,2048]{1,0:T(8,128)(2,1)} %copy-done.20, f32[2048,2048]{1,0:T(8,128)} %fusion.276, bf16[2048,2048]{1,0:T(8,128)(2,1)} %multiply_convert_fusion.3, f32[]{:T(128)S(6)} %div.117, f32[]{:T(128)S(6)} %mul.722), kind=kOutput, calls=%fused_computation.19 | convolution fusion | flops 17221812224 | bytes 41943048 | tf_op jit(solution)/shard_map/rk,kl->rl/dot_general | solution.py:30
  1991.2 22.7 %convolution_convert_fusion.3 = bf16[2048,2048]{1,0:T(8,128)(2,1)S(1)} fusion(bf16[2048,2048]{1,0:T(8,128)(2,1)} %fusion.9), kind=kOutput, calls=%fused_computation.73 | convolution fusion | flops 17184063488 | bytes 16777216 | tf_op jit(solution)/shard_map/rk,rl->kl/dot_general | solution.py:30
  2032.1 24.0 %multiply_convert_fusion.4 = bf16[2048,2048]{1,0:T(8,128)(2,1)} fusion(bf16[2048,2048]{1,0:T(8,128)(2,1)} %copy-done.22, f32[]{:T(128)S(6)} %div.116), kind=kOutput, calls=%fused_computation.36 | convolution fusion | flops 17192452096 | bytes 16777220 | tf_op jit(solution)/shard_map/rk,rl->kl/dot_general | solution.py:30
  2056.0 24.2 %fusion.275 = f32[2048,2048]{1,0:T(8,128)} fusion(bf16[2048,2048]{1,0:T(8,128)(2,1)} %copy-done.22, bf16[2048,2048]{1,0:T(8,128)(2,1)} %multiply_convert_fusion.4), kind=kOutput, calls=%fused_computation.805 | convolution fusion | flops 17179869184 | bytes 33554432 | tf_op jit(solution)/shard_map/rk,kl->rl/dot_general | solution.py:30
  2080.2 29.9 %fusion.5 = bf16[2048,2048]{1,0:T(8,128)(2,1)} fusion(bf16[2048,2048]{1,0:T(8,128)(2,1)} %copy-done.22, f32[2048,2048]{1,0:T(8,128)} %fusion.275, bf16[2048,2048]{1,0:T(8,128)(2,1)} %multiply_convert_fusion.4, f32[]{:T(128)S(6)} %div.116, f32[]{:T(128)S(6)} %mul.710), kind=kOutput, calls=%fused_computation.15 | convolution fusion | flops 17221812224 | bytes 41943048 | tf_op jit(solution)/shard_map/rk,kl->rl/dot_general | solution.py:30
  2110.2 22.5 convolution_convert_fusion.4
  (1188 shorter events, 1542.0 us)
Async XLA Ops:
  31.5 79.7 %collective-permute-start.9 = (bf16[128,2048]{1,0:T(8,128)(2,1)}, bf16[128,2048]{1,0:T(8,128)(2,1)}, u32[]{:S(2)}, u32[]{:S(2)}) collective-permute-start(bf16[128,2048]{1,0:T(8,128)(2,1)} %bitcast.7), channel_id=1, source_target_pairs={{0,1},{1,0},{2,3},{3,2},{4,5},{5,4},{6,7},{7,6},{8,9},{9,8},{10,11... | collective-permute-start | bytes 1572872 | tf_op jit(solution)/shard_map/ppermute | solution.py:69
  62.0 101.7 %all-to-all-start = ((f32[32,1,3072]{2,1,0:T(1,128)}), f32[32,1,3072]{2,1,0:T(1,128)}, u32[]{:S(2)}, u32[]{:S(2)}) async-start(f32[32,1,3072]{2,1,0:T(1,128)} %reshape.684), calls=%async_computation | async-start | bytes 786432 | tf_op jit(solution)/shard_map/all_to_all | solution.py:245
  88.4 92.3 %collective-permute-start.14 = (bf16[256,2048]{1,0:T(8,128)(2,1)S(1)}, bf16[256,2048]{1,0:T(8,128)(2,1)}, u32[]{:S(2)}, u32[]{:S(2)}) collective-permute-start(bf16[256,2048]{1,0:T(8,128)(2,1)S(1)} %bitcast.693), channel_id=1, source_target_pairs={{8,0},{9,1},{10,2},{11,3},{12,4},{13,5},{14,6},{15,7},{16,8},{17,9... | collective-permute-start | bytes 3145736 | tf_op jit(solution)/shard_map/ppermute | solution.py:73
  97.4 84.7 %collective-permute-start.13 = (bf16[256,2048]{1,0:T(8,128)(2,1)S(1)}, bf16[256,2048]{1,0:T(8,128)(2,1)}, u32[]{:S(2)}, u32[]{:S(2)}) collective-permute-start(bf16[256,2048]{1,0:T(8,128)(2,1)S(1)} %bitcast.694), channel_id=1, source_target_pairs={{0,8},{1,9},{2,10},{3,11},{4,12},{5,13},{6,14},{7,15},{8,16},{9,17... | collective-permute-start | bytes 3145736 | tf_op jit(solution)/shard_map/ppermute | solution.py:73
  159.4 101.7 %collective-permute-start.41 = (bf16[256,2048]{1,0:T(8,128)(2,1)}, bf16[256,2048]{1,0:T(8,128)(2,1)}, u32[]{:S(2)}, u32[]{:S(2)}) collective-permute-start(bf16[256,2048]{1,0:T(8,128)(2,1)} %bitcast.59), channel_id=1, source_target_pairs={{8,0},{9,1},{10,2},{11,3},{12,4},{13,5},{14,6},{15,7},{16,8},{17,9... | collective-permute-start | bytes 3145736 | tf_op jit(solution)/shard_map/ppermute | solution.py:73
  168.5 98.9 %collective-permute-start.40 = (bf16[256,2048]{1,0:T(8,128)(2,1)}, bf16[256,2048]{1,0:T(8,128)(2,1)}, u32[]{:S(2)}, u32[]{:S(2)}) collective-permute-start(bf16[256,2048]{1,0:T(8,128)(2,1)} %bitcast.59), channel_id=1, source_target_pairs={{0,8},{1,9},{2,10},{3,11},{4,12},{5,13},{6,14},{7,15},{8,16},{9,17... | collective-permute-start | bytes 3145736 | tf_op jit(solution)/shard_map/ppermute | solution.py:73
  180.7 88.0 %collective-permute-start.47 = (bf16[256,2048]{1,0:T(8,128)(2,1)}, bf16[256,2048]{1,0:T(8,128)(2,1)}, u32[]{:S(2)}, u32[]{:S(2)}) collective-permute-start(bf16[256,2048]{1,0:T(8,128)(2,1)} %bitcast.60), channel_id=1, source_target_pairs={{8,0},{9,1},{10,2},{11,3},{12,4},{13,5},{14,6},{15,7},{16,8},{17,9... | collective-permute-start | bytes 3145736 | tf_op jit(solution)/shard_map/ppermute | solution.py:73
  261.1 66.6 %collective-permute-start.19 = (bf16[2,4,64,2048]{3,2,1,0:T(8,128)(2,1)}, bf16[2,4,64,2048]{3,2,1,0:T(8,128)(2,1)}, u32[]{:S(2)}, u32[]{:S(2)}) collective-permute-start(bf16[2,4,64,2048]{3,2,1,0:T(8,128)(2,1)} %get-tuple-element.89), channel_id=1, source_target_pairs={{0,1},{1,0},{2,3},{3,2},{4,5},{5,4},{6,7},{7,6},{8,9},{9,8},{10,11... | collective-permute-start | bytes 6291464 | tf_op jit(solution)/shard_map/ppermute | solution.py:287
  270.4 109.3 %collective-permute-start.48 = (bf16[256,2048]{1,0:T(8,128)(2,1)}, bf16[256,2048]{1,0:T(8,128)(2,1)}, u32[]{:S(2)}, u32[]{:S(2)}) collective-permute-start(bf16[256,2048]{1,0:T(8,128)(2,1)} %collective-permute-done.47), channel_id=1, source_target_pairs={{8,0},{9,1},{10,2},{11,3},{12,4},{13,5},{14,6},{15,7},{16,8},{17,9... | collective-permute-start | bytes 3145736 | tf_op jit(solution)/shard_map/ppermute | solution.py:73
  309.9 71.8 %collective-permute-start.45 = (bf16[256,2048]{1,0:T(8,128)(2,1)}, bf16[256,2048]{1,0:T(8,128)(2,1)}, u32[]{:S(2)}, u32[]{:S(2)}) collective-permute-start(bf16[256,2048]{1,0:T(8,128)(2,1)} %collective-permute-done.44), channel_id=1, source_target_pairs={{16,24},{17,25},{18,26},{19,27},{20,28},{21,29},{22,30},{23,31}} | collective-permute-start | bytes 3145736 | tf_op jit(solution)/shard_map/ppermute | solution.py:73
  311.5 79.8 %collective-permute-start.43 = (bf16[256,2048]{1,0:T(8,128)(2,1)}, bf16[256,2048]{1,0:T(8,128)(2,1)}, u32[]{:S(2)}, u32[]{:S(2)}) collective-permute-start(bf16[256,2048]{1,0:T(8,128)(2,1)} %collective-permute-done.42), channel_id=1, source_target_pairs={{8,0},{9,1},{10,2},{11,3},{12,4},{13,5},{14,6},{15,7}} | collective-permute-start | bytes 3145736 | tf_op jit(solution)/shard_map/ppermute | solution.py:73
  323.7 93.3 %collective-permute-start.51 = (bf16[256,2048]{1,0:T(8,128)(2,1)}, bf16[256,2048]{1,0:T(8,128)(2,1)}, u32[]{:S(2)}, u32[]{:S(2)}) collective-permute-start(bf16[256,2048]{1,0:T(8,128)(2,1)} %collective-permute-done.50), channel_id=1, source_target_pairs={{16,24},{17,25},{18,26},{19,27},{20,28},{21,29},{22,30},{23,31}} | collective-permute-start | bytes 3145736 | tf_op jit(solution)/shard_map/ppermute | solution.py:73
  513.0 184.3 %collective-permute-start.72 = (bf16[2,2,128,2048]{3,2,1,0:T(8,128)(2,1)}, bf16[2,2,128,2048]{3,2,1,0:T(8,128)(2,1)}, u32[]{:S(2)}, u32[]{:S(2)}) collective-permute-start(bf16[2,2,128,2048]{3,2,1,0:T(8,128)(2,1)} %bitcast.80), channel_id=1, source_target_pairs={{0,1},{1,0},{2,3},{3,2},{4,5},{5,4},{6,7},{7,6},{8,9},{9,8},{10,11... | collective-permute-start | bytes 6291464 | tf_op jit(solution)/shard_map/ppermute | solution.py:69
  1009.0 157.1 %all-reduce.3.cloned.1.call-start = ((), (), s32[]{:S(2)}) async-start(), calls=%async_computation.3 | async-start | bytes 524288 | tf_op jit(solution)/shard_map/psum | solution.py:384
  1027.6 140.8 %collective-permute-start.108 = (bf16[256,2048]{1,0:T(8,128)(2,1)}, bf16[256,2048]{1,0:T(8,128)(2,1)}, u32[]{:S(2)}, u32[]{:S(2)}) collective-permute-start(bf16[256,2048]{1,0:T(8,128)(2,1)} %add_convert_fusion.7), channel_id=1, source_target_pairs={{0,8},{1,9},{2,10},{3,11},{4,12},{5,13},{6,14},{7,15},{8,16},{9,17... | collective-permute-start | bytes 3145736 | tf_op jit(solution)/shard_map/ppermute | solution.py:73
  1033.7 134.7 %collective-permute-start.111 = (bf16[256,2048]{1,0:T(8,128)(2,1)}, bf16[256,2048]{1,0:T(8,128)(2,1)}, u32[]{:S(2)}, u32[]{:S(2)}) collective-permute-start(bf16[256,2048]{1,0:T(8,128)(2,1)} %add_convert_fusion.6), channel_id=1, source_target_pairs={{8,0},{9,1},{10,2},{11,3},{12,4},{13,5},{14,6},{15,7},{16,8},{17,9... | collective-permute-start | bytes 3145736 | tf_op jit(solution)/shard_map/ppermute | solution.py:73
  1187.2 159.7 %collective-permute-start.212 = (bf16[64,2048]{1,0:T(8,128)(2,1)S(1)}, bf16[64,2048]{1,0:T(8,128)(2,1)S(1)}, u32[]{:S(2)}, u32[]{:S(2)}) collective-permute-start(bf16[64,2048]{1,0:T(8,128)(2,1)S(1)} %get-tuple-element.106), channel_id=1, source_target_pairs={{0,16},{1,17},{2,18},{3,19},{4,20},{5,21},{6,22},{7,23},{8,24},{9,... | collective-permute-start | bytes 786440 | tf_op jit(solution)/shard_map/ppermute | solution.py:81
  1187.3 203.7 %collective-permute-start.213 = (bf16[64,2048]{1,0:T(8,128)(2,1)S(1)}, bf16[64,2048]{1,0:T(8,128)(2,1)S(1)}, u32[]{:S(2)}, u32[]{:S(2)}) collective-permute-start(bf16[64,2048]{1,0:T(8,128)(2,1)S(1)} %get-tuple-element.105), channel_id=1, source_target_pairs={{0,24},{1,25},{2,26},{3,27},{4,28},{5,29},{6,30},{7,31},{8,0},{9,1... | collective-permute-start | bytes 786440 | tf_op jit(solution)/shard_map/ppermute | solution.py:81
  1345.6 69.7 %collective-permute-start.193 = (bf16[64,2048]{1,0:T(8,128)(2,1)S(1)}, bf16[64,2048]{1,0:T(8,128)(2,1)S(1)}, u32[]{:S(2)}, u32[]{:S(2)}) collective-permute-start(bf16[64,2048]{1,0:T(8,128)(2,1)S(1)} %get-tuple-element.142), channel_id=1, source_target_pairs={{8,0},{9,1},{10,2},{11,3},{12,4},{13,5},{14,6},{15,7},{16,8},{17,9... | collective-permute-start | bytes 786440 | tf_op jit(solution)/shard_map/ppermute | solution.py:81
  1428.6 68.8 %collective-permute-start.197 = (bf16[128,2048]{1,0:T(8,128)(2,1)S(1)}, bf16[128,2048]{1,0:T(8,128)(2,1)S(1)}, u32[]{:S(2)}, u32[]{:S(2)}) collective-permute-start(bf16[128,2048]{1,0:T(8,128)(2,1)S(1)} %get-tuple-element.219), channel_id=1, source_target_pairs={{0,1},{1,0},{2,3},{3,2},{4,5},{5,4},{6,7},{7,6},{8,9},{9,8},{10,11... | collective-permute-start | bytes 1572872 | tf_op jit(solution)/shard_map/ppermute | solution.py:69
  1541.9 122.7 %collective-permute-start.200 = (bf16[128,2048]{1,0:T(8,128)(2,1)S(1)}, bf16[128,2048]{1,0:T(8,128)(2,1)S(1)}, u32[]{:S(2)}, u32[]{:S(2)}) collective-permute-start(bf16[128,2048]{1,0:T(8,128)(2,1)S(1)} %collective-permute-done.196), channel_id=1, source_target_pairs={{0,1},{1,0},{2,3},{3,2},{4,5},{5,4},{6,7},{7,6},{8,9},{9,8},{10,11... | collective-permute-start | bytes 1572872 | tf_op jit(solution)/shard_map/ppermute | solution.py:69
  1543.0 239.1 %collective-permute-start.180 = (bf16[128,2048]{1,0:T(8,128)(2,1)}, bf16[128,2048]{1,0:T(8,128)(2,1)}, u32[]{:S(2)}, u32[]{:S(2)}) collective-permute-start(bf16[128,2048]{1,0:T(8,128)(2,1)} %collective-permute-done.176), channel_id=1, source_target_pairs={{0,1},{1,0},{2,3},{3,2},{4,5},{5,4},{6,7},{7,6},{8,9},{9,8},{10,11... | collective-permute-start | bytes 1572872 | tf_op jit(solution)/shard_map/ppermute | solution.py:69
  1543.7 358.7 %collective-permute-start.160 = (bf16[128,2048]{1,0:T(8,128)(2,1)}, bf16[128,2048]{1,0:T(8,128)(2,1)}, u32[]{:S(2)}, u32[]{:S(2)}) collective-permute-start(bf16[128,2048]{1,0:T(8,128)(2,1)} %collective-permute-done.156), channel_id=1, source_target_pairs={{0,1},{1,0},{2,3},{3,2},{4,5},{5,4},{6,7},{7,6},{8,9},{9,8},{10,11... | collective-permute-start | bytes 1572872 | tf_op jit(solution)/shard_map/ppermute | solution.py:69
  1543.8 478.1 %collective-permute-start.140 = (bf16[128,2048]{1,0:T(8,128)(2,1)}, bf16[128,2048]{1,0:T(8,128)(2,1)}, u32[]{:S(2)}, u32[]{:S(2)}) collective-permute-start(bf16[128,2048]{1,0:T(8,128)(2,1)} %collective-permute-done.136), channel_id=1, source_target_pairs={{0,1},{1,0},{2,3},{3,2},{4,5},{5,4},{6,7},{7,6},{8,9},{9,8},{10,11... | collective-permute-start | bytes 1572872 | tf_op jit(solution)/shard_map/ppermute | solution.py:69
  (342 other events, 8306.0 us)
Sparse Core Ops, SparseCore 0:
  1041.1 124.9 all-reduce.2

commit v2 on v1

v2 whole, which is shorter than its diff:
```python
import functools
import math

import jax
import jax.numpy as jnp
from jax import lax
from jax.experimental import pallas as pl
from jax.experimental.pallas import tpu as pltpu
from jax.sharding import PartitionSpec as P

HEADS = 16
HD = 128

highest = lax.Precision.HIGHEST
norm_eps = 1e-06
coef_one = 3.4445
coef_two = -4.775
coef_three = 2.0315
matrix_decay = 0.95
vector_decay = 0.9
matrix_rate = 0.5
bias_rate = 0.003
table_rate = 0.02

WORLD = ("img", "strip")
CORE, ALONG_X, ALONG_Y = 1, 2, 4
TEAM = 8
low = jnp.bfloat16
wide = jnp.float32


def dot(spec, left, right):
    return jnp.einsum(spec, left, right, preferred_element_type=wide)


def after(value, *earlier):
    return lax.optimization_barrier((value, *earlier))[0]


def after_all(values, *earlier):
    return lax.optimization_barrier((*values, *earlier))[: len(values)]


def hold(*values):
    return lax.optimization_barrier(values)


def fence(flag, body, *operands):
    shapes = jax.eval_shape(body, *operands)
    empty = lambda *_: jax.tree.map(lambda leaf: jnp.zeros(leaf.shape, leaf.dtype), shapes)
    return lax.cond(flag, body, empty, *operands)


def add(left, right):
    return left.astype(wide) + right.astype(wide)


def normalize(values):
    center = values - jnp.mean(values, axis=-1, keepdims=True)
    inverse = lax.rsqrt(jnp.mean(center * center, axis=-1, keepdims=True) + norm_eps)
    return (center * inverse, inverse)


def norm_back(grad_hat, normed, inverse):
    mean_grad = jnp.mean(grad_hat, axis=-1, keepdims=True)
    mean_cross = jnp.mean(grad_hat * normed, axis=-1, keepdims=True)
    return inverse * (grad_hat - mean_grad - normed * mean_cross)


def gelu_slope(values):
    cumulative = 0.5 * (1.0 + lax.erf(values * 0.7071067811865476))
    density = jnp.exp(-0.5 * values * values) * 0.3989422804014327
    return cumulative + values * density


def silu_slope(values):
    logistic = jax.nn.sigmoid(values)
    return logistic * (1.0 + values * (1.0 - logistic))


class Fabric:
    def __init__(self):
        self.count = lax.axis_size("img") * lax.axis_size("strip")
        self.planes = self.count // TEAM
        self.me = lax.axis_index(WORLD)
        self.plane = self.me // TEAM
        self.seat = self.me % TEAM
        self.lines = [
            [plane * TEAM + seat for plane in range(self.planes)] for seat in range(TEAM)
        ]

    def swap(self, value, bit):
        return lax.ppermute(value, WORLD, [(d, d ^ bit) for d in range(self.count)])

    def turn(self, value, offset):
        pairs = [(d, (d + offset * TEAM) % self.count) for d in range(self.count)]
        return lax.ppermute(value, WORLD, pairs)

    def gather_planes(self, shard):
        return lax.all_gather(shard, WORLD, axis=0, tiled=True, axis_index_groups=self.lines)

    def reduce_planes(self, parts):
        return lax.psum_scatter(
            parts, WORLD, scatter_dimension=0, tiled=True, axis_index_groups=self.lines
        )

    def trade_planes(self, blocks):
        return lax.all_to_all(
            blocks, WORLD, split_axis=0, concat_axis=0, tiled=True, axis_index_groups=self.lines
        )

    def team_total(self, value):
        for bit in (CORE, ALONG_X, ALONG_Y):
            value = value + self.swap(value, bit)
        return value

    def plane_total(self, value):
        others = [self.turn(value, offset) for offset in range(1, self.planes)]
        for other in others:
            value = value + other
        return value

    def share(self, rows, between=()):
        half = rows.shape[0] // 2
        first, second = rows[:half], rows[half:]
        first_x = self.swap(first, ALONG_X)
        second_y = self.swap(second, ALONG_Y)
        first_y = self.swap(first, ALONG_Y)
        second_x = self.swap(second, ALONG_X)
        first_xy = self.swap(after(first_x, *between), ALONG_Y)
        second_xy = self.swap(after(second_y, *between), ALONG_X)
        return jnp.concatenate(
            [rows, first_x, second_x, first_y, second_y, first_xy, second_xy], axis=0
        )

    def settle(self, near, near_too, beside=None):
        width = near.shape[-1]
        size = near.shape[0] // 8
        near = add(near, near_too).astype(low).reshape(2, 2, 2, size, width)
        first, second = near[:, :, 0], near[:, :, 1]
        first_x = self.swap(first[:, 1], ALONG_X)
        second_y = self.swap(second[1], ALONG_Y)
        done = None
        if beside is not None:
            first, second, first_x, second_y, done = hold(
                first, second, first_x, second_y, beside()
            )
        first = add(first[:, 0], first_x).astype(low)
        second = add(second[0], second_y).astype(low)
        first = add(first[0], self.swap(first[1], ALONG_Y))
        second = add(second[0], self.swap(second[1], ALONG_X))
        total = jnp.concatenate([first, second], axis=0)
        return total if beside is None else (total, done)


VMEM_BYTES = 60 * 2**20
QUICK = pl.CostEstimate(flops=1, bytes_accessed=1, transcendentals=0)


def attend_body(projected_ref, mixed_ref):
    size = mixed_ref.shape[-1]
    shape = mixed_ref.shape[:-1] + (HD,)
    tokens = math.prod(shape[:-1])
    for first in range(0, size, HD):

        def read(unit):
            block = projected_ref[..., unit * size + first : unit * size + first + HD]
            return block.reshape(tokens, HD)

        scores = lax.dot_general(
            read(0), read(1), (((1,), (1,)), ((), ())), preferred_element_type=wide
        ) * HD ** (-0.5)
        exponent = jnp.exp(scores - jnp.max(scores, axis=-1, keepdims=True))
        probs = (exponent / jnp.sum(exponent, axis=-1, keepdims=True)).astype(low)
        mixed = jnp.dot(probs, read(2), preferred_element_type=wide).astype(low)
        mixed_ref[..., first : first + HD] = mixed.reshape(shape)


def attend_back_body(projected_ref, grad_ref, out_ref):
    size = grad_ref.shape[-1]
    shape = grad_ref.shape[:-1] + (HD,)
    tokens = math.prod(shape[:-1])
    factor = HD ** (-0.5)
    across = (((1,), (1,)), ((), ()))
    down = (((0,), (0,)), ((), ()))
    for first in range(0, size, HD):

        def read(unit):
            block = projected_ref[..., unit * size + first : unit * size + first + HD]
            return block.reshape(tokens, HD)

        def write(unit, value):
            part = slice(unit * size + first, unit * size + first + HD)
            out_ref[..., part] = value.astype(low).reshape(shape)

        query, keys_all, values_all = read(0), read(1), read(2)
        grad_heads = grad_ref[..., first : first + HD].reshape(tokens, HD)
        scores = lax.dot_general(query, keys_all, across, preferred_element_type=wide) * factor
        exponent = jnp.exp(scores - jnp.max(scores, axis=-1, keepdims=True))
        probs = exponent / jnp.sum(exponent, axis=-1, keepdims=True)
        grad_probs = lax.dot_general(grad_heads, values_all, across, preferred_element_type=wide)
        cross = jnp.sum(probs * grad_probs, axis=-1, keepdims=True)
        grad_scores = (probs * (grad_probs - cross)).astype(low)
        write(0, jnp.dot(grad_scores, keys_all, preferred_element_type=wide) * factor)
        write(1, lax.dot_general(grad_scores, query, down, preferred_element_type=wide) * factor)
        write(2, lax.dot_general(probs.astype(low), grad_heads, down, preferred_element_type=wide))


def over_images(body, here, inner, arrays, out_features):
    def block(features):
        return pl.BlockSpec(
            (2, 1, 2, 1, inner, features), lambda side, image: (0, side, 0, image, 0, 0)
        )

    arrays = [rows.reshape(2, 2, 2, here, inner, rows.shape[-1]) for rows in arrays]
    result = pl.pallas_call(
        body,
        grid=(2, here),
        in_specs=[block(rows.shape[-1]) for rows in arrays],
        out_specs=block(out_features),
        out_shape=jax.ShapeDtypeStruct((2, 2, 2, here, inner, out_features), low),
        compiler_params=pltpu.CompilerParams(vmem_limit_bytes=32 * 2**20),
        cost_estimate=QUICK,
    )(*arrays)
    return result.reshape(-1, out_features)


def modulate_body(rows_ref, modulation_ref, out_ref):
    values = rows_ref[0, 0].astype(wide)
    center = values - jnp.mean(values, axis=-1, keepdims=True)
    inverse = lax.rsqrt(jnp.mean(center * center, axis=-1, keepdims=True) + norm_eps)
    shift = modulation_ref[0, :, 0:1, :]
    scale = modulation_ref[0, :, 1:2, :]
    out_ref[0, 0] = (center * inverse * (1.0 + scale) + shift).astype(low)


def modulate(rows, modulation):
    sides, seats, here, inner, width = rows.shape
    block = pl.BlockSpec((1, 1, here, inner, width), lambda y, x: (y, x, 0, 0, 0))
    return pl.pallas_call(
        modulate_body,
        grid=(sides, seats),
        in_specs=[
            block,
            pl.BlockSpec((1, here) + modulation.shape[2:], lambda y, x: (y, 0, 0, 0)),
        ],
        out_specs=block,
        out_shape=jax.ShapeDtypeStruct(rows.shape, low),
        compiler_params=pltpu.CompilerParams(vmem_limit_bytes=48 * 2**20),
        cost_estimate=QUICK,
    )(rows, modulation)


def gate_body(hidden_ref, weight_ref, upstream_ref, part_ref, cross_ref):
    part = jnp.dot(hidden_ref[...], weight_ref[...], preferred_element_type=wide)
    part_ref[...] = part.astype(low)
    here, inner, width = upstream_ref.shape[2:]
    cross = upstream_ref[0, 0].astype(wide) * part.reshape(here, inner, width)
    cross = jnp.sum(cross, axis=1)[None]

    @pl.when(pl.program_id(1) == 0)
    def _():
        cross_ref[...] = cross

    @pl.when(pl.program_id(1) > 0)
    def _():
        cross_ref[...] += cross


def gate_sums(hidden, weight, upstream):
    sides, seats, here, inner, width = upstream.shape
    size = here * inner
    return pl.pallas_call(
        gate_body,
        grid=(sides, seats),
        in_specs=[
            pl.BlockSpec((size, hidden.shape[1]), lambda y, x: (y * seats + x, 0)),
            pl.BlockSpec(weight.shape, lambda y, x: (0, 0)),
            pl.BlockSpec((1, 1, here, inner, width), lambda y, x: (y, x, 0, 0, 0)),
        ],
        out_specs=[
            pl.BlockSpec((size, width), lambda y, x: (y * seats + x, 0)),
            pl.BlockSpec((1, here, width), lambda y, x: (y, 0, 0)),
        ],
        out_shape=[
            jax.ShapeDtypeStruct((hidden.shape[0], width), low),
            jax.ShapeDtypeStruct((sides, here, width), wide),
        ],
        compiler_params=pltpu.CompilerParams(vmem_limit_bytes=VMEM_BYTES),
        cost_estimate=QUICK,
    )(hidden, weight, upstream)


GRAM_TILE = 512
ROW_BLOCK = 256
COLUMN_TILE = 512


def gram_body(core_ref, near_ref, far_ref, out_ref, factor_ref, kept_ref, *, scaled):
    half = near_ref.shape[1] // 2
    tile = out_ref.shape[0]
    step = pl.program_id(0)
    if scaled:

        @pl.when(step == 0)
        def _():
            near, far = near_ref[...].astype(wide), far_ref[...].astype(wide)
            trace = jnp.sum(near * near) + jnp.sum(far * far)
            kept_ref[0] = 1.0 / (jnp.sqrt(trace) + 1e-07)

        factor = kept_ref[0]
    else:
        factor = jnp.float32(1.0)
    factor_ref[0] = factor
    start = pl.multiple_of(core_ref[0] * half + step * tile, tile)
    rows = (((0,), (0,)), ((), ()))
    total = lax.dot_general(
        near_ref[:, pl.ds(start, tile)], near_ref[...], rows, preferred_element_type=wide
    )
    total += lax.dot_general(
        far_ref[:, pl.ds(start, tile)], far_ref[...], rows, preferred_element_type=wide
    )
    if scaled:
        total = total * factor * factor
    out_ref[...] = total.astype(low)


def half_gram(core, near, far, scaled):
    rows, width = near.shape
    full = pl.BlockSpec((rows, width), lambda i: (0, 0))
    scalar = pl.BlockSpec(memory_space=pltpu.SMEM)
    return pl.pallas_call(
        functools.partial(gram_body, scaled=scaled),
        grid=(width // 2 // GRAM_TILE,),
        in_specs=[scalar, full, full],
        out_specs=[pl.BlockSpec((GRAM_TILE, width), lambda i: (i, 0)), scalar],
        out_shape=[
            jax.ShapeDtypeStruct((width // 2, width), low),
            jax.ShapeDtypeStruct((1,), wide),
        ],
        scratch_shapes=[pltpu.SMEM((1,), wide)],
        compiler_params=pltpu.CompilerParams(vmem_limit_bytes=VMEM_BYTES),
        cost_estimate=QUICK,
    )(core, near, far)


def polynomial_body(core_ref, factor_ref, rows_ref, mine_ref, other_ref, out_ref, wide_ref, low_ref):
    width = rows_ref.shape[1]
    half = width // 2
    core = core_ref[0]
    factor = factor_ref[0]
    here = pl.ds(pl.multiple_of(core * half, half), half)
    there = pl.ds(pl.multiple_of((1 - core) * half, half), half)

    def times_gram(left_ref, part):
        result = jnp.dot(left_ref[:, here], mine_ref[:, part], preferred_element_type=wide)
        return result + jnp.dot(left_ref[:, there], other_ref[:, part], preferred_element_type=wide)

    tiles = [slice(start, start + COLUMN_TILE) for start in range(0, width, COLUMN_TILE)]
    for part in tiles:
        product = times_gram(rows_ref, part) * factor
        wide_ref[:, part] = product
        low_ref[:, part] = product.astype(low)
    for part in tiles:
        square = times_gram(low_ref, part)
        lead = (coef_one * factor) * rows_ref[:, part].astype(wide)
        out_ref[:, part] = (lead + coef_two * wide_ref[:, part] + coef_three * square).astype(low)


def polynomial(core, factor, rows, mine, other):
    count, width = rows.shape
    full = pl.BlockSpec((width // 2, width), lambda i: (0, 0))
    block = pl.BlockSpec((ROW_BLOCK, width), lambda i: (i, 0))
    scalar = pl.BlockSpec(memory_space=pltpu.SMEM)
    return pl.pallas_call(
        polynomial_body,
        grid=(count // ROW_BLOCK,),
        in_specs=[scalar, scalar, block, full, full],
        out_specs=block,
        out_shape=jax.ShapeDtypeStruct((count, width), low),
        scratch_shapes=[pltpu.VMEM((ROW_BLOCK, width), wide), pltpu.VMEM((ROW_BLOCK, width), low)],
        compiler_params=pltpu.CompilerParams(vmem_limit_bytes=VMEM_BYTES),
        cost_estimate=QUICK,
    )(core, factor, rows, mine, other)


def on_device(
    tokens,
    cotangent,
    bin_ids,
    level_table,
    table_moment,
    matrices,
    matrix_moment,
    modulation_bias,
    bias_moment,
):
    fabric = Fabric()
    planes, plane, seat = fabric.planes, fabric.plane, fabric.seat
    strips = lax.axis_size("strip")
    here, inner, width = tokens.shape
    shard_rows, units, _ = matrices.shape
    images = bin_ids.shape[0]
    table_rows = level_table.shape[0]
    blocks = (units - 10) // 2
    start_down = 4 + blocks
    start_ada = 4 + 2 * blocks
    slot_rows = planes * shard_rows
    valid = bin_ids[0] >= 0
    core = (fabric.me % 2).astype(jnp.int32).reshape(1)
    side = seat // 2 % 2
    peers = HD // shard_rows
    heads = planes // peers
    place = fabric.me % peers

    def flat(values):
        return values.reshape(here * inner, width)

    def whole(pair):
        return jnp.concatenate(pair, axis=0)

    def halves(rows):
        return [rows[: rows.shape[0] // 2], rows[rows.shape[0] // 2 :]]

    def parts(rows, weight):
        near, far = [dot("tj,jk->tk", piece, weight).astype(low) for piece in rows]
        return near, fabric.swap(far, CORE)

    def settled(pair):
        return fabric.settle(*pair).reshape(here, inner, width)

    def both(near):
        return [near, fabric.swap(near, CORE)]

    def over_tokens(left, right):
        return dot("tj,tk->jk", whole(left), whole(right)).astype(low)

    row_ids = fabric.me * table_rows + jnp.arange(table_rows, dtype=jnp.int32)
    selector = (bin_ids[:, None] == row_ids[None, :]).astype(wide)
    in_plane = images // planes
    ada_weight = matrices[:, start_ada:, :].astype(low)

    def modulated(modulation, which):
        return modulation[None, :, None, :, None, which]

    def open_rows(rows):
        return rows.reshape(1, 2, 2, here, inner, width).astype(wide)

    active_rows = jax.nn.silu(level_table).astype(low)
    active = jnp.dot(selector.astype(low), active_rows, preferred_element_type=wide)
    active = fabric.plane_total(active.astype(low))

    def gathered(first, last):
        rows = matrices[:, first:last].astype(low).transpose(1, 0, 2)
        rows = after(rows.reshape((last - first) * shard_rows, width), active)
        return fabric.gather_planes(rows)

    attention = gathered(0, 4)
    up_weight = gathered(4, start_down)
    down_weight = gathered(start_down, start_ada)

    def begin(active):
        active = fabric.team_total(active)
        rows, active = hold(flat(tokens), active)
        half = rows.shape[0] // 2
        first, second = rows[:half], rows[half:]
        mod_columns = dot("nk,ruk->nur", active, ada_weight) + modulation_bias[None]
        mod_parts = jnp.broadcast_to(
            mod_columns.reshape(planes, 1, in_plane, 6, shard_rows),
            (planes, TEAM, in_plane, 6, shard_rows),
        ).reshape(fabric.count, in_plane, 6, shard_rows)
        mod_parts = lax.all_to_all(mod_parts, WORLD, split_axis=0, concat_axis=0, tiled=True)
        first_x, second_y, mod_parts = hold(
            fabric.swap(first, ALONG_X), fabric.swap(second, ALONG_Y), mod_parts
        )
        modulation = mod_parts.transpose(1, 2, 0, 3).reshape(2, here, 6, width)
        modulation = jnp.where(seat // 4 == 0, modulation, modulation[::-1])
        first_y, second_x, first_xy, second_xy, modulation = hold(
            fabric.swap(first, ALONG_Y),
            fabric.swap(second, ALONG_X),
            fabric.swap(first_x, ALONG_Y),
            fabric.swap(second_y, ALONG_X),
            modulation,
        )
        near = jnp.concatenate(
            [rows, first_x, second_x, first_y, second_y, first_xy, second_xy], axis=0
        )
        first_in = modulate(near.reshape(2, 2, here, inner, width), modulation)
        return active, modulation, first_in.reshape(-1, width)

    active, modulation, first_in = fence(valid, begin, active)
    local = modulation[0][:, :, None, :]
    shift_one, scale_one, gate_one = local[:, 0], local[:, 1], local[:, 2]
    shift_two, scale_two, gate_two = local[:, 3], local[:, 4], local[:, 5]

    def mates(offset):
        return [
            (d, d // peers * peers + (d % peers + offset) % peers) for d in range(fabric.count)
        ]

    def attention_forward(attention, first_in):
        first_in = both(first_in)
        attention = attention.reshape(planes, 4, shard_rows, width)
        pieces = [lax.dynamic_slice_in_dim(attention, place * heads, heads, 0)]
        for offset in range(1, peers):
            target = (place + offset) % peers
            payload = lax.dynamic_slice_in_dim(attention, target * heads, heads, 0)
            pieces.append(lax.ppermute(payload, WORLD, mates(offset)))
        attention = jnp.stack(pieces).transpose(2, 1, 0, 3, 4).reshape(4, heads * HD, width)
        weight_in = attention[:3].reshape(3 * heads * HD, width)
        weight_out = attention[3]
        projected = whole([dot("tk,jk->tj", rows, weight_in).astype(low) for rows in first_in])
        upstream = fabric.share(flat(cotangent), (projected,))
        mixed = over_images(attend_body, here, inner, [projected], heads * HD)
        return weight_in, weight_out, first_in, projected, mixed, upstream

    weight_in, weight_out, first_in, projected, mixed, upstream = fence(
        valid, attention_forward, attention, first_in
    )

    moment = matrix_moment.transpose(1, 0, 2)

    def padded(batch, count):
        spare = count - batch.shape[0]
        if spare == 0:
            return batch
        return jnp.concatenate([batch, jnp.zeros((spare,) + batch.shape[1:], batch.dtype)], axis=0)

    def to_owner(batch, each):
        batch = padded(batch, planes * each)
        return fabric.trade_planes(batch.reshape(planes, each * shard_rows, width))

    def to_rows(batch, count):
        return fabric.trade_planes(batch).reshape(-1, shard_rows, width)[:count]

    def middle_forward(mixed, upstream):
        def gated():
            grad_mlp = open_rows(upstream) * modulated(modulation, 5)
            return grad_mlp.astype(low).reshape(-1, width)

        branch, grad_mlp = fabric.settle(*parts(halves(mixed), weight_out), gated)
        branch = branch.reshape(here, inner, width)
        middle = tokens.astype(wide) + gate_one * branch
        normed_two, inverse_two = normalize(middle)
        second_in = flat((normed_two * (1.0 + scale_two) + shift_two).astype(low))
        second_in = fabric.share(second_in)
        return (
            branch, middle, normed_two, inverse_two, both(upstream), both(grad_mlp), second_in,
        )

    (
        branch, middle, normed_two, inverse_two, upstream, grad_mlp, second_in,
    ) = fence(valid, middle_forward, mixed, upstream)

    second_in = both(after(second_in, down_weight))
    hidden, slope = [], []
    for rows in second_in:
        preact = dot("tk,jk->tj", rows, up_weight)
        cumulative = 0.5 * (1.0 + lax.erf(preact * 0.7071067811865476))
        density = jnp.exp(-0.5 * preact * preact) * 0.3989422804014327
        hidden.append((preact * cumulative).astype(low))
        slope.append(cumulative + preact * density)
    down_grad = over_tokens(hidden, grad_mlp)
    down_sum = fabric.reduce_planes(down_grad)
    grad_pre = [
        (dot("tk,jk->tj", after(grad_mlp[s], down_grad), down_weight) * slope[s]).astype(low)
        for s in (0, 1)
    ]
    grad_pre = list(lax.optimization_barrier(grad_pre))
    up_grad = over_tokens(grad_pre, second_in)
    up_sum = fabric.reduce_planes(up_grad)
    grad_total = cotangent.astype(wide)
    grad_in_parts = parts(
        [after(rows, up_grad) for rows in grad_pre], up_weight
    )

    def middle_back(grad_in_parts):
        def gate():
            sums = [
                gate_sums(hidden[s], down_weight, upstream[s].reshape(2, 2, here, inner, width))
                for s in (0, 1)
            ]
            return [part for part, _ in sums], sums[0][1] + sums[1][1]

        grad_in, (mlp_parts, grad_gate_two) = fabric.settle(*grad_in_parts, gate)
        grad_in = grad_in.reshape(here, inner, width)
        grad_gate_two = grad_gate_two[0] + fabric.swap(grad_gate_two[1], ALONG_Y)
        grad_gate_two += fabric.swap(grad_gate_two, ALONG_X)
        grad_gate_two += fabric.swap(grad_gate_two, CORE)
        grad_shift_two = jnp.sum(grad_in, axis=1)
        grad_scale_two = jnp.sum(grad_in * normed_two, axis=1)
        grad_middle = grad_total + norm_back(grad_in * (1.0 + scale_two), normed_two, inverse_two)
        grad_gate_one = jnp.sum(grad_middle * branch, axis=1)
        grad_branch = fabric.share(flat((grad_middle * gate_one).astype(low)))
        return (
            mlp_parts, grad_shift_two, grad_scale_two, grad_middle, grad_gate_one,
            grad_gate_two / strips, grad_branch,
        )

    (
        mlp_parts, grad_shift_two, grad_scale_two, grad_middle, grad_gate_one, grad_gate_two,
        grad_branch,
    ) = fence(valid, middle_back, grad_in_parts)

    ada_moment = to_owner(after(moment[start_ada:].astype(low), up_grad), 2)
    grad_branch, ada_moment = hold(grad_branch, ada_moment)

    def attention_back(grad_branch, down_sum):
        grad_branch = both(grad_branch)
        grad_mixed = whole([dot("tk,jk->tj", rows, weight_out).astype(low) for rows in grad_branch])
        grad_project = over_images(
            attend_back_body, here, inner, [projected, grad_mixed], 3 * heads * HD
        )
        return grad_branch, grad_project

    grad_branch, grad_project = fence(valid, attention_back, grad_branch, down_sum)

    def fresh(first, grad):
        grad = grad.astype(wide).reshape(-1, shard_rows, width)
        return matrix_decay * moment[first : first + grad.shape[0]] + grad

    def attention_grads(grad_branch, grad_project, up_sum):
        dense_momentum = jnp.concatenate([fresh(4, up_sum), fresh(start_down, down_sum)], axis=0)
        dense_rows = to_owner(dense_momentum.astype(low), 2)
        grad_first_parts = hold(*parts(halves(grad_project), weight_in))

        def weights():
            in_grad = over_tokens([grad_project], first_in).reshape(3, heads * HD, width)
            out_grad = over_tokens([mixed], grad_branch).reshape(1, heads * HD, width)
            attention_grad = jnp.concatenate([in_grad, out_grad], axis=0)
            attention_grad = attention_grad.reshape(4, heads, peers, shard_rows, width)
            return attention_grad.transpose(2, 1, 0, 3, 4)

        grad_first, attention_grad = fabric.settle(*grad_first_parts, weights)
        returned = [attention_grad[0]]
        for offset in range(1, peers):
            returned.append(lax.ppermute(attention_grad[offset], WORLD, mates(peers - offset)))
        attention_grad = jnp.concatenate(returned + returned[:-1], axis=0)
        attention_grad = lax.dynamic_slice_in_dim(
            attention_grad, (peers - place) % peers * heads, planes, 0
        )
        attention_grad = attention_grad.reshape(planes * 4 * shard_rows, width)
        return attention_grad, dense_momentum, dense_rows, grad_first

    attention_grad, dense_momentum, dense_rows, grad_first = fence(
        valid, attention_grads, grad_branch, grad_project, up_sum
    )
    attention_sum = fabric.reduce_planes(attention_grad)

    def two_of(rows):
        rows = rows.reshape(planes, 2, shard_rows, width)
        mine = lax.dynamic_index_in_dim(rows, side, 1, keepdims=False)
        other = lax.dynamic_index_in_dim(rows, 1 - side, 1, keepdims=False)
        return mine.reshape(slot_rows, width), other.reshape(slot_rows, width)

    def two_back(mine, other):
        mine = mine.reshape(planes, 1, shard_rows, width)
        other = other.reshape(planes, 1, shard_rows, width)
        both_sides = jnp.where(
            side == 0,
            jnp.concatenate([mine, other], axis=1),
            jnp.concatenate([other, mine], axis=1),
        )
        return both_sides.reshape(planes, 2 * shard_rows, width)

    def to_holders(stacked):
        held = lax.all_to_all(stacked, WORLD, split_axis=2, concat_axis=0, tiled=True)
        held = held.reshape(fabric.count // strips, strips, here, 6, shard_rows)
        return jnp.sum(held.astype(wide), axis=1).reshape(images, 6, shard_rows)

    def to_owners(stacked):
        spare = 2 * planes - 6
        stacked = jnp.concatenate(
            [stacked, jnp.zeros((here, spare, width), stacked.dtype)], axis=1
        ).reshape(here, planes, 2, planes, TEAM, shard_rows)
        stacked = stacked.transpose(1, 4, 0, 2, 3, 5)
        stacked = stacked.reshape(fabric.count, here, 2, planes, shard_rows)
        held = lax.all_to_all(stacked, WORLD, split_axis=0, concat_axis=0, tiled=True)
        held = held.reshape(fabric.count // strips, strips, here, 2, planes, shard_rows)
        return jnp.sum(held.astype(wide), axis=1).reshape(images, 2, planes, shard_rows)

    def enter(dense_rows, grad_first):
        normed_one, inverse_one = normalize(tokens.astype(wide))
        grad_first = grad_first.reshape(here, inner, width)
        grad_shift_one = jnp.sum(grad_first, axis=1)
        grad_scale_one = jnp.sum(grad_first * normed_one, axis=1)
        stacked = jnp.stack(
            [
                grad_shift_one,
                grad_scale_one,
                grad_gate_one,
                grad_shift_two,
                grad_scale_two,
                grad_gate_two,
            ],
            axis=1,
        ).astype(low)
        mine, other = two_of(dense_rows)
        mine, mine_x, mine_y, owned = hold(
            mine, fabric.swap(other, ALONG_X), fabric.swap(mine, ALONG_Y), to_owners(stacked)
        )
        ada = jnp.einsum("nuzr,nk->zurk", owned, active.astype(wide), precision=highest)
        ada += matrix_decay * ada_moment.astype(wide).reshape(ada.shape)
        ada_mine, ada_other = two_of(ada.astype(low))
        mine_xy, ada_mine, ada_other = hold(fabric.swap(mine_x, ALONG_Y), ada_mine, ada_other)
        near = jnp.concatenate([mine, mine_x, mine_y, mine_xy], axis=0)
        return near, ada_mine, ada_other, stacked

    dense_near, ada_mine, ada_other, stacked = fence(valid, enter, dense_rows, grad_first)

    d, d_far, ada_mine = hold(dense_near, fabric.swap(dense_near, CORE), ada_mine)
    a_x = fabric.swap(ada_other, ALONG_X)
    d_half, d_factor = half_gram(core, d, d_far, True)
    d, d_half, d_factor, a_x, attention_sum = hold(d, d_half, d_factor, a_x, attention_sum)
    attention_momentum = fresh(0, attention_sum)
    a_y = fabric.swap(ada_mine, ALONG_Y)
    t_rows = to_owner(attention_momentum.astype(low), 1)
    d, d_half, d_other = hold(d, d_half, fabric.swap(d_half, CORE))
    d = polynomial(core, d_factor, d, d_half, d_other)
    d, a_y, a_x = hold(d, a_y, a_x)
    a_xy = fabric.swap(a_x, ALONG_Y)
    d, d_far = hold(d, fabric.swap(d, CORE))
    d_half, one = half_gram(core, d, d_far, False)
    d, d_half, a_xy, t_rows = hold(d, d_half, a_xy, t_rows)
    a = jnp.concatenate([ada_mine, a_x, a_y, a_xy], axis=0)
    t_rows = t_rows.reshape(slot_rows, width)
    t_first, t_second = halves(t_rows)
    t_first_x, t_second_y = fabric.swap(t_first, ALONG_X), fabric.swap(t_second, ALONG_Y)
    a, a_far, d_other = hold(a, fabric.swap(a, CORE), fabric.swap(d_half, CORE))
    d_rows = polynomial(core, one, d[: 2 * slot_rows], d_half, d_other)
    d_rows, a, a_far, t_first_x, t_second_y = hold(d_rows, a, a_far, t_first_x, t_second_y)
    t_first_y, t_second_x = fabric.swap(t_first, ALONG_Y), fabric.swap(t_second, ALONG_X)
    t_first_xy, t_second_xy = fabric.swap(t_first_x, ALONG_Y), fabric.swap(t_second_y, ALONG_X)
    a_half, a_factor = half_gram(core, a, a_far, True)
    d_rows, a, a_half, a_factor, t_first_y, t_second_x, t_first_xy, t_second_xy = hold(
        d_rows, a, a_half, a_factor, t_first_y, t_second_x, t_first_xy, t_second_xy
    )
    t = jnp.concatenate(
        [t_rows, t_first_x, t_second_x, t_first_y, t_second_y, t_first_xy, t_second_xy], axis=0
    )
    d_x = fabric.swap(d_rows[slot_rows:], ALONG_X)
    a_half, a_other, t, t_far = hold(
        a_half, fabric.swap(a_half, CORE), t, fabric.swap(t, CORE)
    )
    t_half, t_factor = half_gram(core, t, t_far, True)
    a_half, a_other, t, t_half, d_x = hold(a_half, a_other, t, t_half, d_x)
    dense_ortho = fabric.trade_planes(two_back(d_rows[:slot_rows], d_x))
    t_other = fabric.swap(t_half, CORE)
    a = polynomial(core, a_factor, a, a_half, a_other)
    a, t, t_half, t_other = hold(a, t, t_half, t_other)
    a_far = fabric.swap(a, CORE)
    t = polynomial(core, t_factor, t, t_half, t_other)
    a, a_far, t = hold(a, a_far, t)
    t_far = fabric.swap(t, CORE)
    a_half, one = half_gram(core, a, a_far, False)
    a, a_half, t, t_far = hold(a, a_half, t, t_far)
    a_other = fabric.swap(a_half, CORE)
    t_half, one = half_gram(core, t, t_far, False)
    a, a_half, a_other, t, t_half, dense_ortho = hold(a, a_half, a_other, t, t_half, dense_ortho)
    t_other = fabric.swap(t_half, CORE)
    a_rows = polynomial(core, one, a[: 2 * slot_rows], a_half, a_other)
    a_rows, t, t_half, t_other = hold(a_rows, t, t_half, t_other)
    a_x = fabric.swap(a_rows[slot_rows:], ALONG_X)
    t_rows = polynomial(core, one, t[:slot_rows], t_half, t_other)
    a_rows, a_x, t_rows = hold(a_rows, a_x, t_rows)
    attention_ortho = fabric.trade_planes(t_rows.reshape(planes, shard_rows, width))
    ada_ortho = fabric.trade_planes(two_back(a_rows[:slot_rows], a_x))

    near, far = mlp_parts
    near, far, grad_first, stacked = after_all((near, far, grad_first, stacked), a)
    mlp_out = settled((near, fabric.swap(far, CORE)))
    block_out = (middle + gate_two * mlp_out).astype(low)
    normed_one, inverse_one = normalize(tokens.astype(wide))
    input_grad = grad_middle + norm_back(
        grad_first.reshape(here, inner, width) * (1.0 + scale_one), normed_one, inverse_one
    )
    input_grad = input_grad.astype(low)
    grad_mod_all = to_holders(stacked)
    grad_active = jnp.einsum(
        "nur,ruk->nk", grad_mod_all, ada_weight.astype(wide), precision=highest
    )
    grad_active = fabric.plane_total(fabric.team_total(grad_active))
    dense_ortho = dense_ortho.reshape(-1, shard_rows, width)[: 2 * blocks]
    ada_ortho = ada_ortho.reshape(-1, shard_rows, width)[:6]
    attention_ortho = attention_ortho.reshape(-1, shard_rows, width)[:4]

    active_wide = active.astype(wide)
    ada_grad = jnp.einsum("nur,nk->urk", grad_mod_all, active_wide, precision=highest)
    bias_grad = jnp.sum(grad_mod_all, axis=0)
    table_grad = jnp.dot(selector.T, grad_active, precision=highest) * silu_slope(level_table)
    momentum = jnp.concatenate(
        [
            attention_momentum,
            dense_momentum,
            matrix_decay * moment[start_ada:] + ada_grad,
        ],
        axis=0,
    ).transpose(1, 0, 2)
    ortho = jnp.concatenate([attention_ortho, dense_ortho, ada_ortho], axis=0).transpose(1, 0, 2)
    step_size = matrix_rate * 0.2 * math.sqrt(width)
    matrix_new = matrices - step_size * ortho.astype(wide)
    bias_momentum = vector_decay * bias_moment + bias_grad
    bias_new = modulation_bias - bias_rate * bias_momentum
    table_momentum = vector_decay * table_moment + table_grad
    table_new = level_table - table_rate * table_momentum
    return (
        block_out,
        input_grad,
        table_grad,
        table_momentum,
        table_new,
        momentum,
        matrix_new,
        bias_momentum,
        bias_new,
    )


def solution(mesh):
    whole = P(("img", "strip"), None, None)
    table = P(("img", "strip"), None)
    strip = P("img", "strip", None)
    bias = P(None, ("img", "strip"))
    return jax.shard_map(
        on_device,
        mesh=mesh,
        in_specs=(strip, strip, P(), table, table, whole, whole, bias, bias),
        out_specs=(strip, strip, table, table, table, whole, whole, bias, bias),
        check_vma=False,
    )
```

time: 2290 us -> 1210 us (0.53)
  matrix products: 699 us -> 149 us
  waiting for transfers between devices: 765 us -> 372 us
  Pallas kernels: 0 us -> 248 us
  starting transfers between devices: 352 us -> 121 us
  local copies, waits for them, and re-layouts: 266 us -> 158 us
  other arithmetic: 165 us -> 112 us
    dot_general x61 -> x19, matrix products: 684 us -> 139 us  [dot(): return jnp.einsum(spec, left, right, preferred_element_type=wide)]
    pallas_call x0 -> x17, Pallas kernels: none -> 248 us  [the longest x6 112 us: polynomial(): pl.pallas_call(polynomial_body, grid=(count // ROW_BLOCK,), in_specs=[sca...]
    ppermute x53 -> x2, starting transfers between devices: 197 us -> 0.61 us  [the longest x1 0.53 us: attention_forward(): pieces.append(lax.ppermute(payload, WORLD, mates(offset)))]
    ppermute x153 -> x84, waiting for transfers between devices: 372 us -> 197 us  [swap(): return lax.ppermute(value, WORLD, [(d, d ^ bit) for d in range(self.count)])]
    ppermute x53 -> x2, waiting for transfers between devices: 170 us -> 0.01 us  [the longest x1 0.01 us: attention_forward(): pieces.append(lax.ppermute(payload, WORLD, mates(offset)))]
    unnamed x454 -> x78, local copies, waits for them, and re-layouts: 163 us -> 36.1 us
    psum x1 -> x0, waiting for transfers between devices: 124 us -> none  [on_device(): lax.psum(jnp.einsum('nur,ruk->nk', grad_mod_all, ada_weight.astype(wide),...]
    all_to_all x1 -> x7, waiting for transfers between devices: 0.01 us -> 75.3 us  [the longest x6 56.6 us: trade_planes(): lax.all_to_all(blocks, WORLD, split_axis=0, concat_axis=0, tiled=True, ax...]
  transfers between devices with their start and end apart: 228 -> 106, of which waited for: 74 -> 47; matrix products, arithmetic and copies ran while one was open for 40% -> 28% of each run, Pallas kernels for 0% -> 21%
where the time goes in v2:
time: 1210 us; the launch traced here: 1200 us
  waiting for transfers between devices  372 us (31%)
  Pallas kernels  248 us (20%)
  local copies, waits for them, and re-layouts  158 us (13%)
  matrix products  149 us (12%)
  starting transfers between devices  121 us (10%)
  other arithmetic  112 us (9%)
  blocking collectives  19.3 us (2%)
  between operations  15.1 us (1%)
    ppermute x84, waiting for transfers between devices, swap(): return lax.ppermute(value, WORLD, [(d, d ^ bit) for d in range(self.count)])  197 us
    dot_general x19, matrix products, dot(): return jnp.einsum(spec, left, right, preferred_element_type=wide)  139 us
    pallas_call x6, Pallas kernels, polynomial(): pl.pallas_call(polynomial_body, grid=(count // ROW_BLOCK,), in_specs=[sca...  112 us
    pallas_call x6, Pallas kernels, half_gram(): pl.pallas_call(functools.partial(gram_body, scaled=scaled), grid=(width /...  91.2 us
    ppermute x84, starting transfers between devices, swap(): return lax.ppermute(value, WORLD, [(d, d ^ bit) for d in range(self.count)])  74 us
    all_to_all x6, waiting for transfers between devices, trade_planes(): lax.all_to_all(blocks, WORLD, split_axis=0, concat_axis=0, tiled=True, ax...  56.6 us
    cond x75, local copies, waits for them, and re-layouts  49.5 us
    reduce_scatter x3, waiting for transfers between devices, reduce_planes(): lax.psum_scatter(parts, WORLD, scatter_dimension=0, tiled=True, axis_inde...  46.3 us
  transfers between devices with their start and end apart: 106, of which 47 were waited for; matrix products, arithmetic and copies ran while one was open for 28% of the time, Pallas kernels for 21%

profile of v2, /device:TPU:0, one launch (start us, length us, event | category | flops | bytes accessed | tf_op | source)
XLA Modules:
  0.0 1197.5 jit_solution(4709928883915293926)
XLA Ops:
  26.4 77.6 %conditional.7 = (bf16[32,2048]{1,0:T(8,128)(2,1)S(1)}, f32[2,4,6,2048]{3,2,1,0:T(8,128)}, bf16[1024,2048]{1,0:T(8,128)(2,1)}) conditional(s32[]{:T(128)} %bitcast.109, () %tuple.107, (bf16[4,64,2048]{2,1,0:T(8,128)(2,1)S(1)}, bf16[32,2048]{1,0:T(8,128)(2,1)S(1)}, bf16[64,6,2048]{2,0,1:T(8,128)(2,1)S(1)}, f32[6,64]{1,0:T(8,128)S(1)}, s32[]{:T(128)}) %tuple.234), branch_computations={%region_0.1_spmd, %region_1.2_spmd} | conditional | flops 50638848 | bytes 51841184 | solution.py:51
  51.8 18.7 %all-to-all-done.2 = f32[32,1,3072]{2,1,0:T(1,128)S(1)} async-done(((f32[32,1,3072]{2,1,0:T(1,128)}), f32[32,1,3072]{2,1,0:T(1,128)S(1)}, u32[]{:S(2)}, u32[]{:S(2)}) %all-to-all-start.2) | async-done | bytes 393248 | tf_op jit(solution)/shard_map/cond/branch_1_fun/all_to_all | solution.py:472
  114.3 62.1 %conditional.8 = (bf16[768,2048]{1,0:T(8,128)(2,1)}, bf16[256,2048]{1,0:T(8,128)(2,1)}, bf16[1024,2048]{1,0:T(8,128)(2,1)}, bf16[1024,2048]{1,0:T(8,128)(2,1)}, ...) conditional(s32[]{:T(128)} %bitcast.109, () %tuple.105, ...), branch_computations={%region_2.3_spmd, %region_3.4_spmd} | conditional | flops 6452412416 | bytes 124781168 | solution.py:51
  176.4 98.8 %conditional.9 = (f32[4,64,2048]{2,1,0:T(8,128)S(1)}, f32[4,64,2048]{2,1,0:T(8,128)}, f32[4,64,2048]{2,1,0:T(8,128)}, f32[4,64,1]{1,0,2:T(4,128)S(1)}, bf16[1024...) conditional(s32[]{:T(128)} %bitcast.109, () %tuple.104, ...), branch_computations={%region_4.5_spmd, %region_5.8_spmd} | conditional | flops 2178949376 | bytes 186821248 | solution.py:51
  199.3 16.2 %collective-permute-done.22 = bf16[2,128,2048]{2,1,0:T(8,128)(2,1)S(1)} collective-permute-done((bf16[2,128,2048]{2,1,0:T(8,128)(2,1)S(1)}, bf16[2,128,2048]{2,1,0:T(8,128)(2,1)S(1)}, u32[]{:S(2)}, u32[]{:S(2)}) %collective-permute-start.22) | collective-permute-done | bytes 1048608 | tf_op jit(solution)/shard_map/cond/branch_1_fun/ppermute | solution.py:93
  370.7 97.8 %conditional.10 = (bf16[1024,2048]{1,0:T(8,128)(2,1)}, bf16[1024,2048]{1,0:T(8,128)(2,1)}, bf16[4,2048]{1,0:T(4,128)(2,1)S(1)}, bf16[4,2048]{1,0:T(4,128)(2,1)S(...) conditional(s32[]{:T(128)} %bitcast.109, () %tuple.111, ...), branch_computations={%region_8.9_spmd, %region_9.0_spmd} | conditional | flops 24682498 | bytes 128296640 | solution.py:51
  468.5 27.4 %conditional.11 = (bf16[1024,2048]{1,0:T(8,128)(2,1)}, bf16[1024,2048]{1,0:T(8,128)(2,1)}, bf16[2048,768]{1,0:T(8,128)(2,1)}) conditional(s32[]{:T(128)} %bitcast.109, () %tuple.122, (bf16[1024,2048]{1,0:T(8,128)(2,1)}, bf16[2048,768]{0,1:T(8,128)(2,1)}, bf16[256,2048]{1,0:T(8,128)(2,1)}) %tuple.125), branch_computations={%region_17.18_spmd, %region_18.19_spmd} | conditional | flops 2150105088 | bytes 45088832 | solution.py:51
  495.8 46.3 %reduce-scatter.6.cloned.1.call-done = bf16[256,2048]{1,0:T(8,128)(2,1)} async-done(((bf16[1024,2048]{1,0:T(8,128)(2,1)}), bf16[256,2048]{1,0:T(8,128)(2,1)}) %reduce-scatter.6.cloned.1.call-update) | async-done | bytes 1048592 | tf_op jit(solution)/shard_map/reduce_scatter | solution.py:103
  542.1 81.8 %conditional.12 = (bf16[1024,2048]{1,0:T(8,128)(2,1)}, f32[8,64,2048]{2,1,0:T(8,128)}, bf16[4,128,2048]{2,1,0:T(8,128)(2,1)}, f32[256,2048]{1,0:T(8,128)S(1)}) conditional(s32[]{:T(128)} %bitcast.109, () %tuple.121, (bf16[2048,768]{1,0:T(8,128)(2,1)}, bf16[768,2048]{1,0:T(8,128)(2,1)}, bf16[1024,2048]{1,0:T(8,128)(2,1)}, ...), branch_computations={%region_19.20_spmd, %region_20.21_spmd} | conditional | flops 15098445824 | bytes 217055808 | solution.py:51
  625.1 61.0 %conditional.13 = (bf16[1024,2048]{1,0:T(8,128)(2,1)}, bf16[256,2048]{1,0:T(8,128)(2,1)}, bf16[256,2048]{1,0:T(8,128)(2,1)}, bf16[4,6,2048]{2,0,1:T(4,128)(2,1)S(1)}) conditional(s32[]{:T(128)} %bitcast.109, () %tuple.127, (bf16[4,128,2048]{2,1,0:T(8,128)(2,1)}, s32[]{:T(128)}, f32[256,2048]{1,0:T(8,128)S(1)}, bf16[4,64,2048]{2,1,0:T(8,128)(2,1)S(1)}, ...), branch_computations={%region_21.22_spmd, %region_22.0_spmd} | conditional | flops 430014720 | bytes 50734384 | solution.py:51
  636.3 19.3 %all_to_all.46 = bf16[32,2,1024]{2,1,0:T(2,128)(2,1)} all-to-all(bf16[32,2,1024]{2,1,0:T(2,128)(2,1)} %reshape.445), channel_id=1, replica_groups=mesh['img'=8,'strip'=4] {'img','strip'}, dimensions={0} | all-to-all | bytes 262144 | tf_op jit(solution)/shard_map/cond/branch_1_fun/all_to_all | solution.py:678
  664.2 18.2 %collective-permute-done.37 = bf16[256,2048]{1,0:T(8,128)(2,1)S(1)} collective-permute-done((bf16[256,2048]{1,0:T(8,128)(2,1)}, bf16[256,2048]{1,0:T(8,128)(2,1)S(1)}, u32[]{:S(2)}, u32[]{:S(2)}) %collective-permute-start.37) | collective-permute-done | bytes 1048608 | tf_op jit(solution)/shard_map/cond/branch_1_fun/ppermute | solution.py:93
  693.7 16.3 %shard_map.160 = (bf16[1024,2048]{1,0:T(8,128)(2,1)}, f32[1]{0:T(128)}) custom-call(s32[1]{0:T(128)} %bitcast.122.core_ref, bf16[1024,2048]{1,0:T(8,128)(2,1)} %get-tuple-element.406.near_ref.rows_ref, bf16[1024,2048]{1,0:T(8,128)(2,1)} %collective-permute-done.58.far_ref), custom_call_target="tpu_custom_call" | custom-call | flops 1 | bytes 1 | tf_op jit(solution)/shard_map/pallas_call | solution.py:332
  719.6 24.1 %shard_map.161.near_ref = bf16[1024,2048]{1,0:T(8,128)(2,1)} custom-call(s32[1]{0:T(128)} %bitcast.122.core_ref, f32[1]{0:T(128)} %get-tuple-element.403.factor_ref, bf16[1024,2048]{1,0:T(8,128)(2,1)} %get-tuple-element.406.near_ref.rows_ref, bf16[1024,2048]{1,0:T(8,128)(2,1)} %get-tuple-element.407.mine_ref, ...), custom_call_target="tpu_custom_call" | custom-call | flops 1 | bytes 1 | tf_op jit(solution)/shard_map/pallas_call | solution.py:375
  795.3 14.7 %shard_map.163 = bf16[512,2048]{1,0:T(8,128)(2,1)} custom-call(s32[1]{0:T(128)} %bitcast.122.core_ref, f32[1]{0:T(128)} %get-tuple-element.414.factor_ref, bf16[512,2048]{1,0:T(8,128)(2,1)} %slice.306.rows_ref, bf16[1024,2048]{1,0:T(8,128)(2,1)} %get-tuple-element.419.mine_ref, bf16[1024,2048]{1,0:T(8,128)(2,1)} %collective-permute-done.65.other_ref), custom_call_target="tpu_custom_call" | custom-call | flops 1 | bytes 1 | tf_op jit(solution)/shard_map/pallas_call | solution.py:375
  814.4 16.8 %shard_map.164 = (bf16[1024,2048]{1,0:T(8,128)(2,1)}, f32[1]{0:T(128)}) custom-call(s32[1]{0:T(128)} %bitcast.122.core_ref, bf16[1024,2048]{1,0:T(8,128)(2,1)} %constant_dynamic-update-slice_fusion.28.near_ref.rows_ref, bf16[1024,2048]{1,0:T(8,128)(2,1)} %collective-permute-done.64.far_ref), custom_call_target="tpu_custom_call" | custom-call | flops 1 | bytes 1 | tf_op jit(solution)/shard_map/pallas_call | solution.py:332
  849.3 16.3 %shard_map.165 = (bf16[1024,2048]{1,0:T(8,128)(2,1)}, f32[1]{0:T(128)}) custom-call(s32[1]{0:T(128)} %bitcast.122.core_ref, bf16[1024,2048]{1,0:T(8,128)(2,1)} %constant_dynamic-update-slice_fusion.32.near_ref.rows_ref, bf16[1024,2048]{1,0:T(8,128)(2,1)} %collective-permute-done.73.far_ref), custom_call_target="tpu_custom_call" | custom-call | flops 1 | bytes 1 | tf_op jit(solution)/shard_map/pallas_call | solution.py:332
  869.0 24.2 %shard_map.166.near_ref = bf16[1024,2048]{1,0:T(8,128)(2,1)} custom-call(s32[1]{0:T(128)} %bitcast.122.core_ref, f32[1]{0:T(128)} %get-tuple-element.433.factor_ref, bf16[1024,2048]{1,0:T(8,128)(2,1)} %constant_dynamic-update-slice_fusion.28.near_ref.rows_ref, bf16[1024,2048]{1,0:T(8,128)(2,1)} %get-tuple-element.446.mine_ref, ...), custom_call_target="tpu_custom_call" | custom-call | flops 1 | bytes 1 | tf_op jit(solution)/shard_map/pallas_call | solution.py:375
  893.8 24.1 %shard_map.167.near_ref = bf16[1024,2048]{1,0:T(8,128)(2,1)} custom-call(s32[1]{0:T(128)} %bitcast.122.core_ref, f32[1]{0:T(128)} %get-tuple-element.451.factor_ref, bf16[1024,2048]{1,0:T(8,128)(2,1)} %constant_dynamic-update-slice_fusion.32.near_ref.rows_ref, bf16[1024,2048]{1,0:T(8,128)(2,1)} %get-tuple-element.453.mine_ref, ...), custom_call_target="tpu_custom_call" | custom-call | flops 1 | bytes 1 | tf_op jit(solution)/shard_map/pallas_call | solution.py:375
  954.9 34.8 %all-to-all-done.5 = bf16[4,128,2048]{2,1,0:T(8,128)(2,1)} async-done(((bf16[4,128,2048]{2,1,0:T(8,128)(2,1)}), bf16[4,128,2048]{2,1,0:T(8,128)(2,1)}, u32[]{:S(2)}, u32[]{:S(2)}) %all-to-all-start.5) | async-done | bytes 2097184 | tf_op jit(solution)/shard_map/all_to_all | solution.py:108
  1007.2 14.7 %shard_map.170 = bf16[512,2048]{1,0:T(8,128)(2,1)} custom-call(s32[1]{0:T(128)} %bitcast.122.core_ref, f32[1]{0:T(128)} %get-tuple-element.472.factor_ref, bf16[512,2048]{1,0:T(8,128)(2,1)} %slice.323.rows_ref, bf16[1024,2048]{1,0:T(8,128)(2,1)} %get-tuple-element.473.mine_ref, bf16[1024,2048]{1,0:T(8,128)(2,1)} %collective-permute-done.78.other_ref), custom_call_target="tpu_custom_call" | custom-call | flops 1 | bytes 1 | tf_op jit(solution)/shard_map/pallas_call | solution.py:375
  1095.8 14.8 %collective-permute-done.80 = bf16[2,128,2048]{2,1,0:T(8,128)(2,1)S(1)} collective-permute-done((bf16[2,128,2048]{2,1,0:T(8,128)(2,1)S(1)}, bf16[2,128,2048]{2,1,0:T(8,128)(2,1)S(1)}, u32[]{:S(2)}, u32[]{:S(2)}) %collective-permute-start.80) | collective-permute-done | bytes 1048608 | tf_op jit(solution)/shard_map/ppermute | solution.py:93
  1123.3 29.0 %collective-permute-done.88 = f32[32,2048]{1,0:T(8,128)S(1)} collective-permute-done((f32[32,2048]{1,0:T(8,128)S(1)}, f32[32,2048]{1,0:T(8,128)S(1)}, u32[]{:S(2)}, u32[]{:S(2)}) %collective-permute-start.88) | collective-permute-done | bytes 262176 | tf_op jit(solution)/shard_map/ppermute | solution.py:97
  1164.4 18.0 %all-to-all-done.7 = bf16[4,64,2048]{2,1,0:T(8,128)(2,1)S(1)} async-done(((bf16[4,64,2048]{2,1,0:T(8,128)(2,1)}), bf16[4,64,2048]{2,1,0:T(8,128)(2,1)S(1)}, u32[]{:S(2)}, u32[]{:S(2)}) %all-to-all-start.7) | async-done | bytes 1048608 | tf_op jit(solution)/shard_map/all_to_all | solution.py:108
  (560 shorter events, 812.9 us)
Async XLA Ops:
  7.2 107.1 %all-gather.4.cloned.1.call-start = ((), (), s32[]{:S(2)}) async-start(), calls=%async_computation.12 | async-start | bytes 5242880 | tf_op jit(solution)/shard_map/all_gather | solution.py:100
  24.8 250.4 %all-gather.6.cloned.1.call-start = ((), (), s32[]{:S(2)}) async-start(), calls=%async_computation.13 | async-start | bytes 5242880 | tf_op jit(solution)/shard_map/all_gather | solution.py:100
  25.6 251.6 %all-gather.8.cloned.1.call-start = ((), (), s32[]{:S(2)}) async-start(), calls=%async_computation.14 | async-start | bytes 5242880 | tf_op jit(solution)/shard_map/all_gather | solution.py:100
  26.3 469.5 %reduce-scatter.4.cloned.1.call-start = ((), (), s32[]{:S(2)}) async-start(), calls=%async_computation.15 | async-start | bytes 5242880 | tf_op jit(solution)/shard_map/reduce_scatter | solution.py:103
  120.2 37.1 %collective-permute-start.17 = (bf16[128,2048]{1,0:T(8,128)(2,1)S(1)}, bf16[128,2048]{1,0:T(8,128)(2,1)S(1)}, u32[]{:S(2)}, u32[]{:S(2)}) collective-permute-start(bf16[128,2048]{1,0:T(8,128)(2,1)S(1)} %bitcast.441), channel_id=1, source_target_pairs={{0,4},{1,5},{2,6},{3,7},{4,0},{5,1},{6,2},{7,3},{8,12},{9,13},{10,... | collective-permute-start | bytes 1572872 | tf_op jit(solution)/shard_map/cond/branch_1_fun/ppermute | solution.py:93
  192.4 82.8 %collective-permute-start.26 = (bf16[1024,2048]{1,0:T(8,128)(2,1)}, bf16[1024,2048]{1,0:T(8,128)(2,1)}, u32[]{:S(2)}, u32[]{:S(2)}) collective-permute-start(bf16[1024,2048]{1,0:T(8,128)(2,1)} %get-tuple-element.688), channel_id=1, source_target_pairs={{0,1},{1,0},{2,3},{3,2},{4,5},{5,4},{6,7},{7,6},{8,9},{9,8},{10,11... | collective-permute-start | bytes 12582920 | tf_op jit(solution)/shard_map/cond/branch_1_fun/ppermute | solution.py:93
  219.8 55.4 %collective-permute-start.27 = (bf16[1024,2048]{1,0:T(8,128)(2,1)}, bf16[1024,2048]{1,0:T(8,128)(2,1)}, u32[]{:S(2)}, u32[]{:S(2)}) collective-permute-start(bf16[1024,2048]{1,0:T(8,128)(2,1)} %fusion.5), channel_id=1, source_target_pairs={{0,1},{1,0},{2,3},{3,2},{4,5},{5,4},{6,7},{7,6},{8,9},{9,8},{10,11... | collective-permute-start | bytes 12582920 | tf_op jit(solution)/shard_map/cond/branch_1_fun/ppermute | solution.py:93
  343.6 198.5 %reduce-scatter.6.cloned.1.call-start = ((), (), s32[]{:S(2)}) async-start(), calls=%async_computation.16 | async-start | bytes 5242880 | tf_op jit(solution)/shard_map/reduce_scatter | solution.py:103
  357.3 111.2 %all-to-all-start.3 = ((bf16[4,128,2048]{2,1,0:T(8,128)(2,1)}), bf16[4,128,2048]{2,1,0:T(8,128)(2,1)}, u32[]{:S(2)}, u32[]{:S(2)}) async-start(bf16[4,128,2048]{2,1,0:T(8,128)(2,1)} %bitcast.413), calls=%async_computation.3 | async-start | bytes 4194304 | tf_op jit(solution)/shard_map/all_to_all | solution.py:108
  361.8 350.3 %reduce-scatter.8.cloned.1.call-start = ((), (), s32[]{:S(2)}) async-start(), calls=%async_computation.17 | async-start | bytes 5242880 | tf_op jit(solution)/shard_map/reduce_scatter | solution.py:103
  556.3 67.2 %all-to-all-start.1 = ((bf16[4,128,2048]{2,1,0:T(8,128)(2,1)}), bf16[4,128,2048]{2,1,0:T(8,128)(2,1)}, u32[]{:S(2)}, u32[]{:S(2)}) async-start(bf16[4,128,2048]{2,1,0:T(8,128)(2,1)} %bitcast.82), calls=%async_computation.1 | async-start | bytes 4194304 | tf_op jit(solution)/shard_map/cond/branch_1_fun/all_to_all | solution.py:108
  786.6 46.6 %collective-permute-start.68 = (bf16[128,2048]{1,0:T(8,128)(2,1)}, bf16[128,2048]{1,0:T(8,128)(2,1)}, u32[]{:S(2)}, u32[]{:S(2)}) collective-permute-start(bf16[128,2048]{1,0:T(8,128)(2,1)} %bitcast.124), channel_id=1, source_target_pairs={{0,4},{1,5},{2,6},{3,7},{4,0},{5,1},{6,2},{7,3},{8,12},{9,13},{10,... | collective-permute-start | bytes 1572872 | tf_op jit(solution)/shard_map/ppermute | solution.py:93
  789.3 44.0 %collective-permute-start.69 = (bf16[128,2048]{1,0:T(8,128)(2,1)}, bf16[128,2048]{1,0:T(8,128)(2,1)}, u32[]{:S(2)}, u32[]{:S(2)}) collective-permute-start(bf16[128,2048]{1,0:T(8,128)(2,1)} %bitcast.125), channel_id=1, source_target_pairs={{0,2},{1,3},{2,0},{3,1},{4,6},{5,7},{6,4},{7,5},{8,10},{9,11},{10,... | collective-permute-start | bytes 1572872 | tf_op jit(solution)/shard_map/ppermute | solution.py:93
  931.8 57.8 %collective-permute-start.78 = (bf16[1024,2048]{1,0:T(8,128)(2,1)}, bf16[1024,2048]{1,0:T(8,128)(2,1)}, u32[]{:S(2)}, u32[]{:S(2)}) collective-permute-start(bf16[1024,2048]{1,0:T(8,128)(2,1)} %get-tuple-element.473.mine_ref), channel_id=1, source_target_pairs={{0,1},{1,0},{2,3},{3,2},{4,5},{5,4},{6,7},{7,6},{8,9},{9,8},{10,11... | collective-permute-start | bytes 12582920 | tf_op jit(solution)/shard_map/ppermute | solution.py:93
  936.2 53.4 %all-to-all-start.5 = ((bf16[4,128,2048]{2,1,0:T(8,128)(2,1)}), bf16[4,128,2048]{2,1,0:T(8,128)(2,1)}, u32[]{:S(2)}, u32[]{:S(2)}) async-start(bf16[4,128,2048]{2,1,0:T(8,128)(2,1)} %bitcast.414), calls=%async_computation.8 | async-start | bytes 4194304 | tf_op jit(solution)/shard_map/all_to_all | solution.py:108
  989.6 59.3 %collective-permute-start.90 = (bf16[1024,2048]{1,0:T(8,128)(2,1)}, bf16[1024,2048]{1,0:T(8,128)(2,1)}, u32[]{:S(2)}, u32[]{:S(2)}) collective-permute-start(bf16[1024,2048]{1,0:T(8,128)(2,1)} %get-tuple-element.479.mine_ref), channel_id=1, source_target_pairs={{0,1},{1,0},{2,3},{3,2},{4,5},{5,4},{6,7},{7,6},{8,9},{9,8},{10,11... | collective-permute-start | bytes 12582920 | tf_op jit(solution)/shard_map/ppermute | solution.py:93
  989.6 62.5 %collective-permute-start.79 = (bf16[1024,2048]{1,0:T(8,128)(2,1)}, bf16[1024,2048]{1,0:T(8,128)(2,1)}, u32[]{:S(2)}, u32[]{:S(2)}) collective-permute-start(bf16[1024,2048]{1,0:T(8,128)(2,1)} %get-tuple-element.467), channel_id=1, source_target_pairs={{0,1},{1,0},{2,3},{3,2},{4,5},{5,4},{6,7},{7,6},{8,9},{9,8},{10,11... | collective-permute-start | bytes 12582920 | tf_op jit(solution)/shard_map/ppermute | solution.py:93
  1047.4 38.2 %collective-permute-start.86 = (f32[32,2048]{1,0:T(8,128)S(1)}, f32[32,2048]{1,0:T(8,128)}, u32[]{:S(2)}, u32[]{:S(2)}) collective-permute-start(f32[32,2048]{1,0:T(8,128)S(1)} %add.315), channel_id=1, source_target_pairs={{0,4},{1,5},{2,6},{3,7},{4,0},{5,1},{6,2},{7,3},{8,12},{9,13},{10,... | collective-permute-start | bytes 786440 | tf_op jit(solution)/shard_map/ppermute | solution.py:93
  1077.9 75.8 %all-to-all-start.8 = ((bf16[4,128,2048]{2,1,0:T(8,128)(2,1)}), bf16[4,128,2048]{2,1,0:T(8,128)(2,1)S(1)}, u32[]{:S(2)}, u32[]{:S(2)}) async-start(bf16[4,128,2048]{2,1,0:T(8,128)(2,1)} %bitcast.162), calls=%async_computation.11 | async-start | bytes 4194304 | tf_op jit(solution)/shard_map/all_to_all | solution.py:108
  1086.7 36.6 %collective-permute-start.89 = (f32[32,2048]{1,0:T(8,128)S(1)}, f32[32,2048]{1,0:T(8,128)S(1)}, u32[]{:S(2)}, u32[]{:S(2)}) collective-permute-start(f32[32,2048]{1,0:T(8,128)S(1)} %add.316), channel_id=1, source_target_pairs={{0,24},{1,25},{2,26},{3,27},{4,28},{5,29},{6,30},{7,31},{8,0},{9,1... | collective-permute-start | bytes 786440 | tf_op jit(solution)/shard_map/ppermute | solution.py:97
  1090.6 61.7 %collective-permute-start.88 = (f32[32,2048]{1,0:T(8,128)S(1)}, f32[32,2048]{1,0:T(8,128)S(1)}, u32[]{:S(2)}, u32[]{:S(2)}) collective-permute-start(f32[32,2048]{1,0:T(8,128)S(1)} %add.316), channel_id=1, source_target_pairs={{0,16},{1,17},{2,18},{3,19},{4,20},{5,21},{6,22},{7,23},{8,24},{9,... | collective-permute-start | bytes 786440 | tf_op jit(solution)/shard_map/ppermute | solution.py:97
  1090.6 61.7 %collective-permute-start.87 = (f32[32,2048]{1,0:T(8,128)S(1)}, f32[32,2048]{1,0:T(8,128)S(1)}, u32[]{:S(2)}, u32[]{:S(2)}) collective-permute-start(f32[32,2048]{1,0:T(8,128)S(1)} %add.316), channel_id=1, source_target_pairs={{0,8},{1,9},{2,10},{3,11},{4,12},{5,13},{6,14},{7,15},{8,16},{9,17... | collective-permute-start | bytes 786440 | tf_op jit(solution)/shard_map/ppermute | solution.py:97
  1094.4 62.9 %collective-permute-start.83 = (bf16[128,2048]{1,0:T(8,128)(2,1)}, bf16[128,2048]{1,0:T(8,128)(2,1)}, u32[]{:S(2)}, u32[]{:S(2)}) collective-permute-start(bf16[128,2048]{1,0:T(8,128)(2,1)} %slice_bitcast_fusion.30), channel_id=1, source_target_pairs={{0,2},{1,3},{2,0},{3,1},{4,6},{5,7},{6,4},{7,5},{8,10},{9,11},{10,... | collective-permute-start | bytes 1572872 | tf_op jit(solution)/shard_map/ppermute | solution.py:93
  1111.9 46.6 %collective-permute-start.81 = (bf16[128,2048]{1,0:T(8,128)(2,1)}, bf16[128,2048]{1,0:T(8,128)(2,1)}, u32[]{:S(2)}, u32[]{:S(2)}) collective-permute-start(bf16[128,2048]{1,0:T(8,128)(2,1)} %slice_bitcast_fusion.32), channel_id=1, source_target_pairs={{0,4},{1,5},{2,6},{3,7},{4,0},{5,1},{6,2},{7,3},{8,12},{9,13},{10,... | collective-permute-start | bytes 1572872 | tf_op jit(solution)/shard_map/ppermute | solution.py:93
  (134 other events, 2216.1 us)
Sparse Core Ops, SparseCore 0:
  24.9 89.3 all-gather.3
  116.5 79.2 all-gather.5
  197.9 79.2 all-gather.7
  343.8 110.1 reduce-scatter.3
  456.2 85.8 reduce-scatter.5
  624.1 79.9 reduce-scatter.7

commit v3 on v2

--- a/solution.py
+++ b/solution.py
@@ -108,6 +108,39 @@
         return lax.all_to_all(
             blocks, WORLD, split_axis=0, concat_axis=0, tiled=True, axis_index_groups=self.lines
         )
+
+    def pieces(self):
+        distances = list(range(1, self.planes))
+        return [distances[:1], distances[-1:], distances[1:-1]]
+
+    def to_owners(self, blocks, group):
+        return {
+            distance: self.turn(
+                lax.dynamic_index_in_dim(
+                    blocks, (self.plane + distance) % self.planes, 0, keepdims=False
+                ),
+                distance,
+            )
+            for distance in self.pieces()[group]
+        }
+
+    def from_owners(self, slots, group):
+        return {distance: self.turn(slots[distance], -distance) for distance in self.pieces()[group]}
+
+    def slots_of(self, blocks):
+        return [
+            lax.dynamic_index_in_dim(blocks, (self.plane - j) % self.planes, 0, keepdims=False)
+            for j in range(self.planes)
+        ]
+
+    def by_plane(self, own, came):
+        came = {0: own, **came}
+        result = jnp.zeros((self.planes,) + own.shape, own.dtype)
+        for distance, block in came.items():
+            result = lax.dynamic_update_index_in_dim(
+                result, block, (self.plane + distance) % self.planes, 0
+            )
+        return result
 
     def team_total(self, value):
         for bit in (CORE, ALONG_X, ALONG_Y):
@@ -134,23 +167,28 @@
         )
 
     def settle(self, near, near_too, beside=None):
+        if beside is None:
+            return self.settle_end(self.settle_begin(near, near_too))
+        parts = self.settle_begin(near, near_too)
+        *parts, done = hold(*parts, beside())
+        return self.settle_end(parts), done
+
+    def settle_begin(self, near, near_too):
         width = near.shape[-1]
         size = near.shape[0] // 8
         near = add(near, near_too).astype(low).reshape(2, 2, 2, size, width)
         first, second = near[:, :, 0], near[:, :, 1]
         first_x = self.swap(first[:, 1], ALONG_X)
         second_y = self.swap(second[1], ALONG_Y)
-        done = None
-        if beside is not None:
-            first, second, first_x, second_y, done = hold(
-                first, second, first_x, second_y, beside()
-            )
-        first = add(first[:, 0], first_x).astype(low)
-        second = add(second[0], second_y).astype(low)
+        return first[:, 0], second[0], first_x, second_y
+
+    def settle_end(self, parts):
+        first, second, first_x, second_y = parts
+        first = add(first, first_x).astype(low)
+        second = add(second, second_y).astype(low)
         first = add(first[0], self.swap(first[1], ALONG_Y))
         second = add(second[0], self.swap(second[1], ALONG_X))
-        total = jnp.concatenate([first, second], axis=0)
-        return total if beside is None else (total, done)
+        return jnp.concatenate([first, second], axis=0)
 
 
 VMEM_BYTES = 60 * 2**20
@@ -291,97 +329,235 @@
     )(hidden, weight, upstream)
 
 
-GRAM_TILE = 512
+def norm_sums_body(grad_ref, weight_ref, rows_ref, part_ref, sums_ref):
+    part = jnp.dot(grad_ref[...], weight_ref[...], preferred_element_type=wide)
+    part_ref[...] = part.astype(low)
+    here, inner, width = rows_ref.shape[2:]
+    part = part.reshape(here, inner, width)
+    values = rows_ref[0, 0].astype(wide)
+    center = values - jnp.mean(values, axis=-1, keepdims=True)
+    inverse = lax.rsqrt(jnp.mean(center * center, axis=-1, keepdims=True) + norm_eps)
+    shift = jnp.sum(part, axis=1)[None, None]
+    scale = jnp.sum(part * (center * inverse), axis=1)[None, None]
+
+    @pl.when(pl.program_id(1) == 0)
+    def _():
+        sums_ref[0:1] = shift
+        sums_ref[1:2] = scale
+
+    @pl.when(pl.program_id(1) > 0)
+    def _():
+        sums_ref[0:1] += shift
+        sums_ref[1:2] += scale
+
+
+def norm_sums(grads, weight, rows):
+    sides, seats, here, inner, width = rows.shape
+    size = here * inner
+    return pl.pallas_call(
+        norm_sums_body,
+        grid=(sides, seats),
+        in_specs=[
+            pl.BlockSpec((size, grads.shape[1]), lambda y, x: (y * seats + x, 0)),
+            pl.BlockSpec(weight.shape, lambda y, x: (0, 0)),
+            pl.BlockSpec((1, 1, here, inner, width), lambda y, x: (y, x, 0, 0, 0)),
+        ],
+        out_specs=[
+            pl.BlockSpec((size, width), lambda y, x: (y * seats + x, 0)),
+            pl.BlockSpec((2, 1, here, width), lambda y, x: (0, y, 0, 0)),
+        ],
+        out_shape=[
+            jax.ShapeDtypeStruct((grads.shape[0], width), low),
+            jax.ShapeDtypeStruct((2, sides, here, width), wide),
+        ],
+        compiler_params=pltpu.CompilerParams(vmem_limit_bytes=VMEM_BYTES),
+        cost_estimate=QUICK,
+    )(grads, weight, rows)
+
+
+CHUNK = 512
 ROW_BLOCK = 256
-COLUMN_TILE = 512
-
-
-def gram_body(core_ref, near_ref, far_ref, out_ref, factor_ref, kept_ref, *, scaled):
-    half = near_ref.shape[1] // 2
+
+
+def gram_body(core_ref, *refs, near_count, far_count):
+    pieces = refs[: near_count + far_count]
+    out_ref, near_ref, x_ref, sem, near_sem = refs[near_count + far_count :]
+    width = x_ref.shape[1]
+    half = width // 2
     tile = out_ref.shape[0]
     step = pl.program_id(0)
-    if scaled:
+    start = core_ref[0] * half
+
+    def column(j):
+        return pl.multiple_of((start + j * CHUNK) % width, CHUNK)
+
+    def copies(j):
+        part = pl.ds(column(j), CHUNK)
+        result, row = [], 0
+        for k, piece in enumerate(pieces):
+            rows = pl.ds(row, piece.shape[0])
+            result.append(
+                pltpu.make_async_copy(piece.at[:, part], x_ref.at[rows, part], sem.at[j, k])
+            )
+            row += piece.shape[0]
+        return result
+
+    joined = pltpu.make_async_copy(x_ref.at[pl.ds(0, near_ref.shape[0])], near_ref, near_sem)
+
+    @pl.when(step == 0)
+    def _():
+        for j in range(width // CHUNK):
+            for copy in copies(j):
+                copy.start()
+
+    left = pl.ds(pl.multiple_of(start + step * tile, tile), tile)
+    for j in range(width // CHUNK):
 
         @pl.when(step == 0)
         def _():
-            near, far = near_ref[...].astype(wide), far_ref[...].astype(wide)
-            trace = jnp.sum(near * near) + jnp.sum(far * far)
-            kept_ref[0] = 1.0 / (jnp.sqrt(trace) + 1e-07)
-
-        factor = kept_ref[0]
-    else:
-        factor = jnp.float32(1.0)
-    factor_ref[0] = factor
-    start = pl.multiple_of(core_ref[0] * half + step * tile, tile)
-    rows = (((0,), (0,)), ((), ()))
-    total = lax.dot_general(
-        near_ref[:, pl.ds(start, tile)], near_ref[...], rows, preferred_element_type=wide
-    )
-    total += lax.dot_general(
-        far_ref[:, pl.ds(start, tile)], far_ref[...], rows, preferred_element_type=wide
-    )
-    if scaled:
-        total = total * factor * factor
-    out_ref[...] = total.astype(low)
-
-
-def half_gram(core, near, far, scaled):
-    rows, width = near.shape
-    full = pl.BlockSpec((rows, width), lambda i: (0, 0))
-    scalar = pl.BlockSpec(memory_space=pltpu.SMEM)
-    return pl.pallas_call(
-        functools.partial(gram_body, scaled=scaled),
-        grid=(width // 2 // GRAM_TILE,),
-        in_specs=[scalar, full, full],
-        out_specs=[pl.BlockSpec((GRAM_TILE, width), lambda i: (i, 0)), scalar],
+            for copy in copies(j):
+                copy.wait()
+            if j == width // CHUNK - 1 and near_count > 1:
+                joined.start()
+
+        part = pl.ds(column(j), CHUNK)
+        total = lax.dot_general(
+            x_ref[:, left], x_ref[:, part], (((0,), (0,)), ((), ())), preferred_element_type=wide
+        )
+        out_ref[:, part] = total.astype(low)
+
+    if near_count > 1:
+
+        @pl.when(step == pl.num_programs(0) - 1)
+        def _():
+            joined.wait()
+
+
+def half_gram(core, near, far):
+    width = near[0].shape[1]
+    near_rows = sum(piece.shape[0] for piece in near)
+    far_rows = sum(piece.shape[0] for piece in far)
+    anywhere = pl.BlockSpec(memory_space=pl.ANY)
+    kept = near_rows if len(near) > 1 else 16
+    half, joined = pl.pallas_call(
+        functools.partial(gram_body, near_count=len(near), far_count=len(far)),
+        grid=(width // 2 // CHUNK,),
+        in_specs=[pl.BlockSpec(memory_space=pltpu.SMEM)] + [anywhere] * (len(near) + len(far)),
+        out_specs=[pl.BlockSpec((CHUNK, width), lambda i: (i, 0)), anywhere],
         out_shape=[
             jax.ShapeDtypeStruct((width // 2, width), low),
-            jax.ShapeDtypeStruct((1,), wide),
+            jax.ShapeDtypeStruct((kept, width), low),
         ],
-        scratch_shapes=[pltpu.SMEM((1,), wide)],
+        scratch_shapes=[
+            pltpu.VMEM((near_rows + far_rows, width), low),
+            pltpu.SemaphoreType.DMA((width // CHUNK, len(near) + len(far))),
+            pltpu.SemaphoreType.DMA,
+        ],
         compiler_params=pltpu.CompilerParams(vmem_limit_bytes=VMEM_BYTES),
         cost_estimate=QUICK,
-    )(core, near, far)
-
-
-def polynomial_body(core_ref, factor_ref, rows_ref, mine_ref, other_ref, out_ref, wide_ref, low_ref):
+    )(core, *near, *far)
+    return half, joined if len(near) > 1 else near[0]
+
+
+def polynomial_body(core_ref, rows_ref, mine_ref, other_ref, *refs, scaled):
+    *outs, gram_ref, wide_ref, low_ref, factor_ref, sem = refs
     width = rows_ref.shape[1]
     half = width // 2
+    first = pl.program_id(0) == 0
     core = core_ref[0]
-    factor = factor_ref[0]
-    here = pl.ds(pl.multiple_of(core * half, half), half)
-    there = pl.ds(pl.multiple_of((1 - core) * half, half), half)
-
-    def times_gram(left_ref, part):
-        result = jnp.dot(left_ref[:, here], mine_ref[:, part], preferred_element_type=wide)
-        return result + jnp.dot(left_ref[:, there], other_ref[:, part], preferred_element_type=wide)
-
-    tiles = [slice(start, start + COLUMN_TILE) for start in range(0, width, COLUMN_TILE)]
+    places = [pl.multiple_of(core * half, half), pl.multiple_of((1 - core) * half, half)]
+
+    def copies(j):
+        part = pl.ds(j * CHUNK, CHUNK)
+        return [
+            pltpu.make_async_copy(
+                source.at[:, part], gram_ref.at[pl.ds(places[k], half), part], sem.at[j, k]
+            )
+            for k, source in enumerate((mine_ref, other_ref))
+        ]
+
+    @pl.when(first)
+    def _():
+        for j in range(width // CHUNK):
+            for copy in copies(j):
+                copy.start()
+
+    tiles = [slice(start, start + CHUNK) for start in range(0, width, CHUNK)]
+    for j, part in enumerate(tiles):
+
+        @pl.when(first)
+        def _():
+            for copy in copies(j):
+                copy.wait()
+
+        wide_ref[:, part] = jnp.dot(
+            rows_ref[...], gram_ref[:, part], preferred_element_type=wide
+        )
+        if not scaled:
+            low_ref[:, part] = wide_ref[:, part].astype(low)
+
+    if scaled:
+
+        @pl.when(first)
+        def _():
+            trace = jnp.float32(0.0)
+            size = 256
+            row = lax.broadcasted_iota(jnp.int32, (size, size), 0)
+            column = lax.broadcasted_iota(jnp.int32, (size, size), 1)
+            for start in range(0, width, size):
+                block = gram_ref[start : start + size, start : start + size].astype(wide)
+                trace += jnp.sum(jnp.where(row == column, block, 0.0))
+            factor_ref[0] = 1.0 / (jnp.sqrt(trace) + 1e-07)
+
+        factor = factor_ref[0]
+        cube, squared = factor * factor * factor, factor * factor
+        for part in tiles:
+            product = wide_ref[:, part] * cube
+            wide_ref[:, part] = product
+            low_ref[:, part] = product.astype(low)
+    else:
+        factor = squared = jnp.float32(1.0)
     for part in tiles:
-        product = times_gram(rows_ref, part) * factor
-        wide_ref[:, part] = product
-        low_ref[:, part] = product.astype(low)
-    for part in tiles:
-        square = times_gram(low_ref, part)
+        square = jnp.dot(low_ref[...], gram_ref[:, part], preferred_element_type=wide) * squared
         lead = (coef_one * factor) * rows_ref[:, part].astype(wide)
-        out_ref[:, part] = (lead + coef_two * wide_ref[:, part] + coef_three * square).astype(low)
-
-
-def polynomial(core, factor, rows, mine, other):
+        result = (lead + coef_two * wide_ref[:, part] + coef_three * square).astype(low)
+        if len(outs) == 1:
+            outs[0][:, part] = result
+        else:
+            for k, out_ref in enumerate(outs):
+
+                @pl.when(pl.program_id(0) == k)
+                def _():
+                    out_ref[:, part] = result
+
+
+def polynomial(core, rows, mine, other, scaled, blocks=None):
     count, width = rows.shape
-    full = pl.BlockSpec((width // 2, width), lambda i: (0, 0))
+    if blocks is not None:
+        count = blocks * ROW_BLOCK
+    anywhere = pl.BlockSpec(memory_space=pl.ANY)
     block = pl.BlockSpec((ROW_BLOCK, width), lambda i: (i, 0))
-    scalar = pl.BlockSpec(memory_space=pltpu.SMEM)
+    if blocks is None:
+        out_specs, out_shape = block, jax.ShapeDtypeStruct((count, width), low)
+    else:
+        out_specs = [pl.BlockSpec((ROW_BLOCK, width), lambda i: (0, 0))] * blocks
+        out_shape = [jax.ShapeDtypeStruct((ROW_BLOCK, width), low)] * blocks
     return pl.pallas_call(
-        polynomial_body,
+        functools.partial(polynomial_body, scaled=scaled),
         grid=(count // ROW_BLOCK,),
-        in_specs=[scalar, scalar, block, full, full],
-        out_specs=block,
-        out_shape=jax.ShapeDtypeStruct((count, width), low),
-        scratch_shapes=[pltpu.VMEM((ROW_BLOCK, width), wide), pltpu.VMEM((ROW_BLOCK, width), low)],
+        in_specs=[pl.BlockSpec(memory_space=pltpu.SMEM), block, anywhere, anywhere],
+        out_specs=out_specs,
+        out_shape=out_shape,
+        scratch_shapes=[
+            pltpu.VMEM((width, width), low),
+            pltpu.VMEM((ROW_BLOCK, width), wide),
+            pltpu.VMEM((ROW_BLOCK, width), low),
+            pltpu.SMEM((1,), wide),
+            pltpu.SemaphoreType.DMA((width // CHUNK, 2)),
+        ],
         compiler_params=pltpu.CompilerParams(vmem_limit_bytes=VMEM_BYTES),
         cost_estimate=QUICK,
-    )(core, factor, rows, mine, other)
+    )(core, rows, mine, other)
 
 
 def on_device(
@@ -486,9 +662,9 @@
             [rows, first_x, second_x, first_y, second_y, first_xy, second_xy], axis=0
         )
         first_in = modulate(near.reshape(2, 2, here, inner, width), modulation)
-        return active, modulation, first_in.reshape(-1, width)
-
-    active, modulation, first_in = fence(valid, begin, active)
+        return active, modulation, both(first_in.reshape(-1, width)), near
+
+    active, modulation, first_in, tokens_near = fence(valid, begin, active)
     local = modulation[0][:, :, None, :]
     shift_one, scale_one, gate_one = local[:, 0], local[:, 1], local[:, 2]
     shift_two, scale_two, gate_two = local[:, 3], local[:, 4], local[:, 5]
@@ -498,8 +674,7 @@
             (d, d // peers * peers + (d % peers + offset) % peers) for d in range(fabric.count)
         ]
 
-    def attention_forward(attention, first_in):
-        first_in = both(first_in)
+    def attention_forward(attention):
         attention = attention.reshape(planes, 4, shard_rows, width)
         pieces = [lax.dynamic_slice_in_dim(attention, place * heads, heads, 0)]
         for offset in range(1, peers):
@@ -510,13 +685,11 @@
         weight_in = attention[:3].reshape(3 * heads * HD, width)
         weight_out = attention[3]
         projected = whole([dot("tk,jk->tj", rows, weight_in).astype(low) for rows in first_in])
-        upstream = fabric.share(flat(cotangent), (projected,))
+        upstream = fabric.share(after(flat(cotangent), weight_in), (projected,))
         mixed = over_images(attend_body, here, inner, [projected], heads * HD)
-        return weight_in, weight_out, first_in, projected, mixed, upstream
-
-    weight_in, weight_out, first_in, projected, mixed, upstream = fence(
-        valid, attention_forward, attention, first_in
-    )
+        return weight_in, weight_out, projected, mixed, upstream
+
+    weight_in, weight_out, projected, mixed, upstream = fence(valid, attention_forward, attention)
 
     moment = matrix_moment.transpose(1, 0, 2)
 
@@ -532,6 +705,8 @@
 
     def to_rows(batch, count):
         return fabric.trade_planes(batch).reshape(-1, shard_rows, width)[:count]
+
+    ada_moment = to_owner(after(moment[start_ada:], mixed).astype(low), 2)
 
     def middle_forward(mixed, upstream):
         def gated():
@@ -551,8 +726,9 @@
     (
         branch, middle, normed_two, inverse_two, upstream, grad_mlp, second_in,
     ) = fence(valid, middle_forward, mixed, upstream)
-
-    second_in = both(after(second_in, down_weight))
+    second_in, ada_moment = hold(second_in, ada_moment)
+
+    second_in = both(second_in)
     hidden, slope = [], []
     for rows in second_in:
         preact = dot("tk,jk->tj", rows, up_weight)
@@ -560,78 +736,75 @@
         density = jnp.exp(-0.5 * preact * preact) * 0.3989422804014327
         hidden.append((preact * cumulative).astype(low))
         slope.append(cumulative + preact * density)
+    *hidden, down_weight = hold(*hidden, down_weight)
     down_grad = over_tokens(hidden, grad_mlp)
+    grad_total = cotangent.astype(wide)
+
+    *grad_mlp, down_grad = hold(*grad_mlp, down_grad)
+
     down_sum = fabric.reduce_planes(down_grad)
-    grad_pre = [
-        (dot("tk,jk->tj", after(grad_mlp[s], down_grad), down_weight) * slope[s]).astype(low)
-        for s in (0, 1)
-    ]
-    grad_pre = list(lax.optimization_barrier(grad_pre))
-    up_grad = over_tokens(grad_pre, second_in)
+
+    def turn_back(grad_mlp):
+        grad_pre = [
+            (dot("tk,jk->tj", grad_mlp[s], down_weight) * slope[s]).astype(low) for s in (0, 1)
+        ]
+        grad_pre = hold(*grad_pre)
+
+        near, near_too = hold(*parts(grad_pre, up_weight))
+        grad_in = fabric.settle_begin(near, near_too)
+        return hold(*grad_in, over_tokens(grad_pre, second_in))
+
+    *grad_in, up_grad = fence(valid, turn_back, grad_mlp)
     up_sum = fabric.reduce_planes(up_grad)
-    grad_total = cotangent.astype(wide)
-    grad_in_parts = parts(
-        [after(rows, up_grad) for rows in grad_pre], up_weight
-    )
-
-    def middle_back(grad_in_parts):
-        def gate():
-            sums = [
-                gate_sums(hidden[s], down_weight, upstream[s].reshape(2, 2, here, inner, width))
-                for s in (0, 1)
-            ]
-            return [part for part, _ in sums], sums[0][1] + sums[1][1]
-
-        grad_in, (mlp_parts, grad_gate_two) = fabric.settle(*grad_in_parts, gate)
-        grad_in = grad_in.reshape(here, inner, width)
-        grad_gate_two = grad_gate_two[0] + fabric.swap(grad_gate_two[1], ALONG_Y)
-        grad_gate_two += fabric.swap(grad_gate_two, ALONG_X)
-        grad_gate_two += fabric.swap(grad_gate_two, CORE)
+
+    def middle_back(grad_in):
+        grad_in = fabric.settle_end(grad_in).reshape(here, inner, width)
         grad_shift_two = jnp.sum(grad_in, axis=1)
         grad_scale_two = jnp.sum(grad_in * normed_two, axis=1)
         grad_middle = grad_total + norm_back(grad_in * (1.0 + scale_two), normed_two, inverse_two)
         grad_gate_one = jnp.sum(grad_middle * branch, axis=1)
-        grad_branch = fabric.share(flat((grad_middle * gate_one).astype(low)))
+        grad_branch = flat((grad_middle * gate_one).astype(low))
+        *ready, grad_branch = hold(*hidden, grad_branch)
+        seats = [rows.reshape(2, 2, here, inner, width) for rows in upstream]
+        mlp_far, far_gate = gate_sums(ready[1], down_weight, seats[1])
+        grad_branch = fabric.share(grad_branch, (mlp_far,))
+        mlp_near, near_gate = gate_sums(after(ready[0], mlp_far), down_weight, seats[0])
+        grad_branch, mlp_near, mlp_too = hold(grad_branch, mlp_near, fabric.swap(mlp_far, CORE))
+        grad_gate_two = far_gate + near_gate
         return (
-            mlp_parts, grad_shift_two, grad_scale_two, grad_middle, grad_gate_one,
-            grad_gate_two / strips, grad_branch,
-        )
-
+            grad_shift_two, grad_scale_two, grad_middle, grad_gate_one, grad_gate_two, grad_branch,
+            mlp_near, mlp_too,
+        )
+
+    *grad_in, down_sum = hold(*grad_in, down_sum)
     (
-        mlp_parts, grad_shift_two, grad_scale_two, grad_middle, grad_gate_one, grad_gate_two,
-        grad_branch,
-    ) = fence(valid, middle_back, grad_in_parts)
-
-    ada_moment = to_owner(after(moment[start_ada:].astype(low), up_grad), 2)
-    grad_branch, ada_moment = hold(grad_branch, ada_moment)
-
-    def attention_back(grad_branch, down_sum):
+        grad_shift_two, grad_scale_two, grad_middle, grad_gate_one, grad_gate_two, grad_branch,
+        mlp_near, mlp_too,
+    ) = fence(valid, middle_back, grad_in)
+
+    def fresh(first, grad):
+        grad = grad.astype(wide).reshape(-1, shard_rows, width)
+        return matrix_decay * moment[first : first + grad.shape[0]] + grad
+
+    up_sum, down_sum, grad_branch = hold(up_sum, down_sum, grad_branch)
+    dense_momentum = jnp.concatenate([fresh(4, up_sum), fresh(start_down, down_sum)], axis=0)
+    dense_rows, grad_branch = hold(dense_momentum.astype(low), grad_branch)
+    dense_rows = to_owner(dense_rows, 2)
+
+    def attention_back(grad_branch, mlp_near, mlp_too):
         grad_branch = both(grad_branch)
+        mlp_sums = fabric.settle_begin(mlp_near, mlp_too)
         grad_mixed = whole([dot("tk,jk->tj", rows, weight_out).astype(low) for rows in grad_branch])
         grad_project = over_images(
             attend_back_body, here, inner, [projected, grad_mixed], 3 * heads * HD
         )
-        return grad_branch, grad_project
-
-    grad_branch, grad_project = fence(valid, attention_back, grad_branch, down_sum)
-
-    def fresh(first, grad):
-        grad = grad.astype(wide).reshape(-1, shard_rows, width)
-        return matrix_decay * moment[first : first + grad.shape[0]] + grad
-
-    def attention_grads(grad_branch, grad_project, up_sum):
-        dense_momentum = jnp.concatenate([fresh(4, up_sum), fresh(start_down, down_sum)], axis=0)
-        dense_rows = to_owner(dense_momentum.astype(low), 2)
-        grad_first_parts = hold(*parts(halves(grad_project), weight_in))
-
-        def weights():
-            in_grad = over_tokens([grad_project], first_in).reshape(3, heads * HD, width)
-            out_grad = over_tokens([mixed], grad_branch).reshape(1, heads * HD, width)
-            attention_grad = jnp.concatenate([in_grad, out_grad], axis=0)
-            attention_grad = attention_grad.reshape(4, heads, peers, shard_rows, width)
-            return attention_grad.transpose(2, 1, 0, 3, 4)
-
-        grad_first, attention_grad = fabric.settle(*grad_first_parts, weights)
+        grad_project, *mlp_sums = hold(grad_project, *mlp_sums)
+        mlp_out = fabric.settle_end(mlp_sums)
+        in_grad = over_tokens([grad_project], first_in).reshape(3, heads * HD, width)
+        out_grad = over_tokens([mixed], grad_branch).reshape(1, heads * HD, width)
+        attention_grad = jnp.concatenate([in_grad, out_grad], axis=0)
+        attention_grad = attention_grad.reshape(4, heads, peers, shard_rows, width)
+        attention_grad = attention_grad.transpose(2, 1, 0, 3, 4)
         returned = [attention_grad[0]]
         for offset in range(1, peers):
             returned.append(lax.ppermute(attention_grad[offset], WORLD, mates(peers - offset)))
@@ -639,12 +812,13 @@
         attention_grad = lax.dynamic_slice_in_dim(
             attention_grad, (peers - place) % peers * heads, planes, 0
         )
-        attention_grad = attention_grad.reshape(planes * 4 * shard_rows, width)
-        return attention_grad, dense_momentum, dense_rows, grad_first
-
-    attention_grad, dense_momentum, dense_rows, grad_first = fence(
-        valid, attention_grads, grad_branch, grad_project, up_sum
+        return grad_project, attention_grad.reshape(planes * 4 * shard_rows, width), mlp_out
+
+    grad_project, attention_grad, mlp_out = fence(
+        valid, attention_back, grad_branch, mlp_near, mlp_too
     )
+    mlp_out = mlp_out.reshape(here, inner, width)
+    attention_grad, dense_rows = hold(attention_grad, dense_rows)
     attention_sum = fabric.reduce_planes(attention_grad)
 
     def two_of(rows):
@@ -653,146 +827,192 @@
         other = lax.dynamic_index_in_dim(rows, 1 - side, 1, keepdims=False)
         return mine.reshape(slot_rows, width), other.reshape(slot_rows, width)
 
-    def two_back(mine, other):
+    def joined(mine, other):
         mine = mine.reshape(planes, 1, shard_rows, width)
         other = other.reshape(planes, 1, shard_rows, width)
-        both_sides = jnp.where(
-            side == 0,
-            jnp.concatenate([mine, other], axis=1),
-            jnp.concatenate([other, mine], axis=1),
-        )
-        return both_sides.reshape(planes, 2 * shard_rows, width)
-
-    def to_holders(stacked):
-        held = lax.all_to_all(stacked, WORLD, split_axis=2, concat_axis=0, tiled=True)
-        held = held.reshape(fabric.count // strips, strips, here, 6, shard_rows)
-        return jnp.sum(held.astype(wide), axis=1).reshape(images, 6, shard_rows)
+        return fabric.slots_of(jnp.concatenate([mine, other], axis=1))
+
+    def two_units(own, came):
+        rows = fabric.by_plane(own, came)
+        rows = jnp.where(side == 0, rows, rows[:, ::-1])
+        return rows.reshape(2 * planes, shard_rows, width)
 
     def to_owners(stacked):
         spare = 2 * planes - 6
         stacked = jnp.concatenate(
-            [stacked, jnp.zeros((here, spare, width), stacked.dtype)], axis=1
-        ).reshape(here, planes, 2, planes, TEAM, shard_rows)
+            [stacked, jnp.zeros((2 * here, spare, width), stacked.dtype)], axis=1
+        ).reshape(2 * here, planes, 2, planes, TEAM, shard_rows)
         stacked = stacked.transpose(1, 4, 0, 2, 3, 5)
-        stacked = stacked.reshape(fabric.count, here, 2, planes, shard_rows)
+        stacked = stacked.reshape(fabric.count, 2 * here, 2, planes, shard_rows)
         held = lax.all_to_all(stacked, WORLD, split_axis=0, concat_axis=0, tiled=True)
-        held = held.reshape(fabric.count // strips, strips, here, 2, planes, shard_rows)
+        held = held.reshape(planes, TEAM, 2 * here, 2, planes, shard_rows)
         return jnp.sum(held.astype(wide), axis=1).reshape(images, 2, planes, shard_rows)
 
-    def enter(dense_rows, grad_first):
-        normed_one, inverse_one = normalize(tokens.astype(wide))
-        grad_first = grad_first.reshape(here, inner, width)
-        grad_shift_one = jnp.sum(grad_first, axis=1)
-        grad_scale_one = jnp.sum(grad_first * normed_one, axis=1)
-        stacked = jnp.stack(
-            [
-                grad_shift_one,
-                grad_scale_one,
-                grad_gate_one,
-                grad_shift_two,
-                grad_scale_two,
-                grad_gate_two,
-            ],
-            axis=1,
-        ).astype(low)
-        mine, other = two_of(dense_rows)
-        mine, mine_x, mine_y, owned = hold(
-            mine, fabric.swap(other, ALONG_X), fabric.swap(mine, ALONG_Y), to_owners(stacked)
-        )
+    def enter(grad_project, dense_rows):
+        d, d_other = two_of(dense_rows)
+        grads = halves(grad_project)
+        seats = [rows.reshape(2, 2, here, inner, width) for rows in both(tokens_near)]
+        d, d_x, d_y, near, far = hold(
+            d,
+            fabric.swap(d_other, ALONG_X),
+            fabric.swap(d, ALONG_Y),
+            norm_sums(grads[0], weight_in, seats[0]),
+            norm_sums(grads[1], weight_in, seats[1]),
+        )
+        sums = near[1] + far[1]
+        own = jnp.stack([grad_gate_one, grad_shift_two, grad_scale_two], axis=0)
+        own = jnp.stack([own, jnp.zeros_like(own)], axis=1)
+        stacked = jnp.concatenate([sums, own, grad_gate_two[None]], axis=0)
+        stacked = jnp.where(seat // 4 == 0, stacked, stacked[:, ::-1])
+        stacked = stacked.reshape(6, 2 * here, width).transpose(1, 0, 2).astype(low)
+        owned = to_owners(stacked)
+        d_near = [d, d_x, d_y]
+        d_far = [fabric.swap(piece, CORE) for piece in d_near]
+        d_xy = fabric.swap(d_x, ALONG_Y)
+        d_xy, owned, *d_far = hold(d_xy, owned, *d_far)
+        d_far_xy = fabric.swap(d_xy, CORE)
         ada = jnp.einsum("nuzr,nk->zurk", owned, active.astype(wide), precision=highest)
         ada += matrix_decay * ada_moment.astype(wide).reshape(ada.shape)
-        ada_mine, ada_other = two_of(ada.astype(low))
-        mine_xy, ada_mine, ada_other = hold(fabric.swap(mine_x, ALONG_Y), ada_mine, ada_other)
-        near = jnp.concatenate([mine, mine_x, mine_y, mine_xy], axis=0)
-        return near, ada_mine, ada_other, stacked
-
-    dense_near, ada_mine, ada_other, stacked = fence(valid, enter, dense_rows, grad_first)
-
-    d, d_far, ada_mine = hold(dense_near, fabric.swap(dense_near, CORE), ada_mine)
-    a_x = fabric.swap(ada_other, ALONG_X)
-    d_half, d_factor = half_gram(core, d, d_far, True)
-    d, d_half, d_factor, a_x, attention_sum = hold(d, d_half, d_factor, a_x, attention_sum)
+        a, a_other = two_of(ada.astype(low))
+        d_far_xy, a, a_other = hold(d_far_xy, a, a_other)
+        block_out = (middle + gate_two * mlp_out).astype(low)
+        return near[0], far[0], owned, d_near + [d_xy], d_far + [d_far_xy], a, a_other, block_out
+
+    first_near, first_far, owned, d, d_far, a, a_other, block_out = fence(
+        valid, enter, grad_project, dense_rows
+    )
+
+    def steps_one(d, d_far, a, a_other, owned):
+        a_x, a_y = fabric.swap(a_other, ALONG_X), fabric.swap(a, ALONG_Y)
+        grad_mod_all = fabric.trade_planes(owned.transpose(2, 0, 1, 3))
+        d_half, d = half_gram(core, d, d_far)
+        a_far = fabric.swap(a, CORE)
+        d, d_half, grad_mod_all = hold(d, d_half, grad_mod_all)
+        grad_mod_all = grad_mod_all.transpose(1, 0, 2, 3)
+        grad_mod_all = grad_mod_all.reshape(images, 2 * planes, shard_rows)[:, :6]
+        grad_active = jnp.einsum(
+            "nur,ruk->nk", grad_mod_all, ada_weight.astype(wide), precision=highest
+        )
+        d_half, d_other, a_far, grad_active = hold(
+            d_half, fabric.swap(d_half, CORE), a_far, grad_active
+        )
+        d = polynomial(core, d, d_half, d_other, True)
+        grad_active += fabric.swap(grad_active, CORE)
+        return hold(d, a_x, a_y, a_far, grad_mod_all, grad_active)
+
+    d, a_x, a_y, a_far, grad_mod_all, grad_active = fence(
+        valid, steps_one, d, d_far, a, a_other, owned
+    )
+    d, a_x, a_y, attention_sum = hold(d, a_x, a_y, attention_sum)
     attention_momentum = fresh(0, attention_sum)
-    a_y = fabric.swap(ada_mine, ALONG_Y)
-    t_rows = to_owner(attention_momentum.astype(low), 1)
-    d, d_half, d_other = hold(d, d_half, fabric.swap(d_half, CORE))
-    d = polynomial(core, d_factor, d, d_half, d_other)
-    d, a_y, a_x = hold(d, a_y, a_x)
-    a_xy = fabric.swap(a_x, ALONG_Y)
-    d, d_far = hold(d, fabric.swap(d, CORE))
-    d_half, one = half_gram(core, d, d_far, False)
-    d, d_half, a_xy, t_rows = hold(d, d_half, a_xy, t_rows)
-    a = jnp.concatenate([ada_mine, a_x, a_y, a_xy], axis=0)
-    t_rows = t_rows.reshape(slot_rows, width)
-    t_first, t_second = halves(t_rows)
-    t_first_x, t_second_y = fabric.swap(t_first, ALONG_X), fabric.swap(t_second, ALONG_Y)
-    a, a_far, d_other = hold(a, fabric.swap(a, CORE), fabric.swap(d_half, CORE))
-    d_rows = polynomial(core, one, d[: 2 * slot_rows], d_half, d_other)
-    d_rows, a, a_far, t_first_x, t_second_y = hold(d_rows, a, a_far, t_first_x, t_second_y)
-    t_first_y, t_second_x = fabric.swap(t_first, ALONG_Y), fabric.swap(t_second, ALONG_X)
-    t_first_xy, t_second_xy = fabric.swap(t_first_x, ALONG_Y), fabric.swap(t_second_y, ALONG_X)
-    a_half, a_factor = half_gram(core, a, a_far, True)
-    d_rows, a, a_half, a_factor, t_first_y, t_second_x, t_first_xy, t_second_xy = hold(
-        d_rows, a, a_half, a_factor, t_first_y, t_second_x, t_first_xy, t_second_xy
+
+    def steps_two(
+        d, a, a_x, a_y, a_far, attention_momentum, first_near, first_far, grad_active
+    ):
+        t_own = padded(attention_momentum.astype(low), planes)
+        a_xy = fabric.swap(a_x, ALONG_Y)
+        a_far = [a_far, fabric.swap(a_x, CORE), fabric.swap(a_y, CORE)]
+        d, d_far, t_own = hold(d, fabric.swap(d, CORE), t_own)
+        t_slots = {0: lax.dynamic_index_in_dim(t_own, plane, 0, keepdims=False)}
+        t_slots.update(fabric.to_owners(t_own, 0))
+        t_slots.update(fabric.to_owners(t_own, 1))
+        d_half, _ = half_gram(core, [d], [d_far])
+        d, d_half, a_xy, t_slots, a_far = hold(d, d_half, a_xy, t_slots, a_far)
+        t_slots.update(fabric.to_owners(t_own, 2))
+        d_other = fabric.swap(d_half, CORE)
+        a_near, a_far_xy = hold([a, a_x, a_y, a_xy], fabric.swap(a_xy, CORE))
+        grad_active_x = fabric.swap(grad_active, ALONG_X)
+        a_half, a = half_gram(core, a_near, a_far + [a_far_xy])
+        a, a_half, d_half, d_other, t_slots, grad_active_x = hold(
+            a, a_half, d_half, d_other, t_slots, grad_active_x
+        )
+        grad_active += grad_active_x
+        t_slots = [t_slots[j] for j in range(planes)]
+        t_first = jnp.concatenate(t_slots[: planes // 2], axis=0)
+        t_second = jnp.concatenate(t_slots[planes // 2 :], axis=0)
+        t_first_x, t_second_y = fabric.swap(t_first, ALONG_X), fabric.swap(t_second, ALONG_Y)
+        t_far = [fabric.swap(t_first, CORE), fabric.swap(t_second, CORE)]
+        a_other = fabric.swap(a_half, CORE)
+        d_rows, d_beside = polynomial(core, d, d_half, d_other, False, 2)
+        d_rows, d_beside, a_half, a_other, t_first_x, t_second_y, t_far = hold(
+            d_rows, d_beside, a_half, a_other, t_first_x, t_second_y, t_far
+        )
+        t_second_x, t_first_y = fabric.swap(t_second, ALONG_X), fabric.swap(t_first, ALONG_Y)
+        t_second_xy, t_first_xy = fabric.swap(t_second_y, ALONG_X), fabric.swap(t_first_x, ALONG_Y)
+        a = polynomial(core, a, a_half, a_other, True)
+        a, t_second_x, t_first_y, t_second_xy, t_first_xy = hold(
+            a, t_second_x, t_first_y, t_second_xy, t_first_xy
+        )
+        t_near = [t_first, t_second, t_first_x, t_second_x, t_first_y, t_second_y]
+        t_near = t_near + [t_first_xy, t_second_xy]
+        d_x = fabric.swap(d_beside, ALONG_X)
+        first_too = fabric.swap(first_far, CORE)
+        a, a_far = hold(a, fabric.swap(a, CORE))
+        t_far = t_far + [fabric.swap(piece, CORE) for piece in t_near[2:]]
+        first_sums = fabric.settle_begin(first_near, first_too)
+        a_half, _ = half_gram(core, [a], [a_far])
+        a, a_half, t_far, d_x = hold(a, a_half, t_far, d_x)
+        d_slots = joined(d_rows, d_x)
+        d_came = fabric.from_owners(d_slots, 0)
+        a_other = fabric.swap(a_half, CORE)
+        t_half, t = half_gram(core, t_near, t_far)
+        t, t_half, a_half, a_other, d_came = hold(t, t_half, a_half, a_other, d_came)
+        d_came.update(fabric.from_owners(d_slots, 1))
+        t_other = fabric.swap(t_half, CORE)
+        a_rows, a_beside = polynomial(core, a, a_half, a_other, False, 2)
+        a_rows, a_beside, t_half, t_other, d_came, first_sums = hold(
+            a_rows, a_beside, t_half, t_other, d_came, first_sums
+        )
+        d_came.update(fabric.from_owners(d_slots, 2))
+        a_x = fabric.swap(a_beside, ALONG_X)
+        grad_active_y = fabric.swap(grad_active, ALONG_Y)
+        t = polynomial(core, t, t_half, t_other, True)
+        t, a_x, d_came, grad_active_y = hold(t, a_x, d_came, grad_active_y)
+        grad_active += grad_active_y
+        a_slots = joined(a_rows, a_x)
+        a_came = fabric.from_owners(a_slots, 0)
+        a_came.update(fabric.from_owners(a_slots, 1))
+        t, t_far = hold(t, fabric.swap(t, CORE))
+        grad_first = fabric.settle_end(first_sums).reshape(here, inner, width)
+        t_half, _ = half_gram(core, [t], [t_far])
+        t, t_half, a_came, grad_first = hold(t, t_half, a_came, grad_first)
+        a_came.update(fabric.from_owners(a_slots, 2))
+        t_half, t_other = hold(t_half, fabric.swap(t_half, CORE))
+        (t_rows,) = polynomial(core, t, t_half, t_other, False, 1)
+        t_rows, a_came = hold(t_rows, a_came)
+        return t_rows, d_slots[0], d_came, a_slots[0], a_came, grad_first, grad_active
+
+    t_rows, d_own, d_came, a_own, a_came, grad_first, grad_active = fence(
+        valid, steps_two, d, a, a_x, a_y, a_far, attention_momentum, first_near, first_far,
+        grad_active,
     )
-    t = jnp.concatenate(
-        [t_rows, t_first_x, t_second_x, t_first_y, t_second_y, t_first_xy, t_second_xy], axis=0
+    t_slots = [t_rows[j * shard_rows : (j + 1) * shard_rows] for j in range(planes)]
+    t_came = {}
+    for group in range(3):
+        t_came.update(fabric.from_owners(t_slots, group))
+    dense_ortho = two_units(d_own, d_came)
+    ada_ortho = two_units(a_own, a_came)
+    attention_ortho = fabric.by_plane(t_slots[0], t_came)
+    grad_active = fabric.plane_total(grad_active)
+    ada_momentum = matrix_decay * moment[start_ada:] + jnp.einsum(
+        "nur,nk->urk", grad_mod_all, active.astype(wide), precision=highest
     )
-    d_x = fabric.swap(d_rows[slot_rows:], ALONG_X)
-    a_half, a_other, t, t_far = hold(
-        a_half, fabric.swap(a_half, CORE), t, fabric.swap(t, CORE)
-    )
-    t_half, t_factor = half_gram(core, t, t_far, True)
-    a_half, a_other, t, t_half, d_x = hold(a_half, a_other, t, t_half, d_x)
-    dense_ortho = fabric.trade_planes(two_back(d_rows[:slot_rows], d_x))
-    t_other = fabric.swap(t_half, CORE)
-    a = polynomial(core, a_factor, a, a_half, a_other)
-    a, t, t_half, t_other = hold(a, t, t_half, t_other)
-    a_far = fabric.swap(a, CORE)
-    t = polynomial(core, t_factor, t, t_half, t_other)
-    a, a_far, t = hold(a, a_far, t)
-    t_far = fabric.swap(t, CORE)
-    a_half, one = half_gram(core, a, a_far, False)
-    a, a_half, t, t_far = hold(a, a_half, t, t_far)
-    a_other = fabric.swap(a_half, CORE)
-    t_half, one = half_gram(core, t, t_far, False)
-    a, a_half, a_other, t, t_half, dense_ortho = hold(a, a_half, a_other, t, t_half, dense_ortho)
-    t_other = fabric.swap(t_half, CORE)
-    a_rows = polynomial(core, one, a[: 2 * slot_rows], a_half, a_other)
-    a_rows, t, t_half, t_other = hold(a_rows, t, t_half, t_other)
-    a_x = fabric.swap(a_rows[slot_rows:], ALONG_X)
-    t_rows = polynomial(core, one, t[:slot_rows], t_half, t_other)
-    a_rows, a_x, t_rows = hold(a_rows, a_x, t_rows)
-    attention_ortho = fabric.trade_planes(t_rows.reshape(planes, shard_rows, width))
-    ada_ortho = fabric.trade_planes(two_back(a_rows[:slot_rows], a_x))
-
-    near, far = mlp_parts
-    near, far, grad_first, stacked = after_all((near, far, grad_first, stacked), a)
-    mlp_out = settled((near, fabric.swap(far, CORE)))
-    block_out = (middle + gate_two * mlp_out).astype(low)
+
     normed_one, inverse_one = normalize(tokens.astype(wide))
     input_grad = grad_middle + norm_back(
-        grad_first.reshape(here, inner, width) * (1.0 + scale_one), normed_one, inverse_one
+        grad_first * (1.0 + scale_one), normed_one, inverse_one
     )
     input_grad = input_grad.astype(low)
-    grad_mod_all = to_holders(stacked)
-    grad_active = jnp.einsum(
-        "nur,ruk->nk", grad_mod_all, ada_weight.astype(wide), precision=highest
-    )
-    grad_active = fabric.plane_total(fabric.team_total(grad_active))
-    dense_ortho = dense_ortho.reshape(-1, shard_rows, width)[: 2 * blocks]
-    ada_ortho = ada_ortho.reshape(-1, shard_rows, width)[:6]
-    attention_ortho = attention_ortho.reshape(-1, shard_rows, width)[:4]
-
-    active_wide = active.astype(wide)
-    ada_grad = jnp.einsum("nur,nk->urk", grad_mod_all, active_wide, precision=highest)
+    dense_ortho, ada_ortho = dense_ortho[: 2 * blocks], ada_ortho[:6]
+    attention_ortho = attention_ortho[:4]
+
     bias_grad = jnp.sum(grad_mod_all, axis=0)
     table_grad = jnp.dot(selector.T, grad_active, precision=highest) * silu_slope(level_table)
     momentum = jnp.concatenate(
         [
             attention_momentum,
             dense_momentum,
-            matrix_decay * moment[start_ada:] + ada_grad,
+            ada_momentum,
         ],
         axis=0,
     ).transpose(1, 0, 2)

time: 1210 us -> 1070 us (0.88)
  waiting for transfers between devices: 372 us -> 254 us
  blocking collectives: 19.3 us -> 0 us
  local copies, waits for them, and re-layouts: 158 us -> 142 us
  matrix products: 149 us -> 134 us
    all_to_all x6 -> x3, waiting for transfers between devices: 56.6 us -> 0.01 us  [trade_planes(): lax.all_to_all(blocks, WORLD, split_axis=0, concat_axis=0, tiled=True, ax...]
    reduce_scatter x3, waiting for transfers between devices: 46.3 us -> 10.1 us  [reduce_planes(): lax.psum_scatter(parts, WORLD, scatter_dimension=0, tiled=True, axis_inde...]
    unnamed x78 -> x77, local copies, waits for them, and re-layouts: 36.1 us -> 10.8 us
    ppermute x6 -> x18, starting transfers between devices: 11.3 us -> 31.8 us  [turn(): return lax.ppermute(value, WORLD, pairs)]
    ppermute x84 -> x95, waiting for transfers between devices: 197 us -> 178 us  [swap(): return lax.ppermute(value, WORLD, [(d, d ^ bit) for d in range(self.count)])]
    all_to_all x1 -> x0, blocking collectives: 19.3 us -> none  [to_owners(): lax.all_to_all(stacked, WORLD, split_axis=0, concat_axis=0, tiled=True)]
    dot_general x19 -> x17, matrix products: 139 us -> 122 us  [dot(): return jnp.einsum(spec, left, right, preferred_element_type=wide)]
    all_to_all x6 -> x3, starting transfers between devices: 27 us -> 14.2 us  [trade_planes(): lax.all_to_all(blocks, WORLD, split_axis=0, concat_axis=0, tiled=True, ax...]
  transfers between devices with their start and end apart: 106 -> 126, of which waited for: 47 -> 45; matrix products, arithmetic and copies ran while one was open for 28% -> 33% of each run, Pallas kernels for 21% -> 25%
where the time goes in v3:
time: 1070 us; the launch traced here: 1060 us
  Pallas kernels  260 us (24%)
  waiting for transfers between devices  254 us (24%)
  local copies, waits for them, and re-layouts  142 us (13%)
  matrix products  134 us (13%)
  starting transfers between devices  127 us (12%)
  other arithmetic  120 us (11%)
  between operations  15.2 us (1%)
    ppermute x95, waiting for transfers between devices, swap(): return lax.ppermute(value, WORLD, [(d, d ^ bit) for d in range(self.count)])  178 us
    dot_general x17, matrix products, dot(): return jnp.einsum(spec, left, right, preferred_element_type=wide)  122 us
    pallas_call x6, Pallas kernels, polynomial(): pl.pallas_call(functools.partial(polynomial_body, scaled=scaled), grid=(c...  115 us
    pallas_call x6, Pallas kernels, half_gram(): pl.pallas_call(functools.partial(gram_body, near_count=len(near), far_cou...  81.2 us
    ppermute x95, starting transfers between devices, swap(): return lax.ppermute(value, WORLD, [(d, d ^ bit) for d in range(self.count)])  70.6 us
    cond x130, local copies, waits for them, and re-layouts  52.7 us
    ppermute x18, starting transfers between devices, turn(): return lax.ppermute(value, WORLD, pairs)  31.8 us
    ppermute x18, waiting for transfers between devices, turn(): return lax.ppermute(value, WORLD, pairs)  29.2 us
  transfers between devices with their start and end apart: 126, of which 45 were waited for; matrix products, arithmetic and copies ran while one was open for 33% of the time, Pallas kernels for 25%

profile of v3, /device:TPU:0, one launch (start us, length us, event | category | flops | bytes accessed | tf_op | source)
XLA Modules:
  0.0 1057.5 jit_solution(4232625214272753428)
XLA Ops:
  30.1 85.7 %conditional.9 = (bf16[32,2048]{1,0:T(8,128)(2,1)}, f32[2,4,6,2048]{3,2,1,0:T(8,128)}, bf16[1024,2048]{1,0:T(8,128)(2,1)}, bf16[1024,2048]{1,0:T(8,128)(2,1)}, b...) conditional(s32[]{:T(128)} %bitcast.146, () %tuple.156, ...), branch_computations={%region_0.1_spmd, %region_1.2_spmd} | conditional | flops 50638848 | bytes 51841244 | solution.py:51
  57.7 18.4 %all-to-all-done.1 = f32[32,1,3072]{2,1,0:T(1,128)S(1)} async-done(((f32[32,1,3072]{2,1,0:T(1,128)}), f32[32,1,3072]{2,1,0:T(1,128)S(1)}, u32[]{:S(2)}, u32[]{:S(2)}) %all-to-all-start.1) | async-done | bytes 393248 | tf_op jit(solution)/shard_map/cond/branch_1_fun/all_to_all | solution.py:648
  116.4 58.8 %conditional.10 = (bf16[768,2048]{1,0:T(8,128)(2,1)S(1)}, bf16[256,2048]{1,0:T(8,128)(2,1)S(1)}, bf16[2048,768]{0,1:T(8,128)(2,1)}, bf16[2048,256]{1,0:T(8,128)(2,1)}, bf16[1024,2048]{1,0:T(8,128)(2,1)}) conditional(s32[]{:T(128)} %bitcast.146, () %tuple.154, (bf16[1024,2048]{1,0:T(8,128)(2,1)}, s32[]{:T(128)}, bf16[1024,2048]{1,0:T(8,128)(2,1)}, ...), branch_computations={%region_2.3_spmd, %region_3.4_spmd} | conditional | flops 6452412416 | bytes 145752736 | solution.py:51
  186.3 97.9 %conditional.11 = (f32[4,64,2048]{2,1,0:T(8,128)S(1)}, f32[4,64,2048]{2,1,0:T(8,128)}, f32[4,64,2048]{2,1,0:T(8,128)}, f32[4,64,1]{1,0,2:T(4,128)S(1)}, bf16[102...) conditional(s32[]{:T(128)} %bitcast.146, () %tuple.160, ...), branch_computations={%region_4.5_spmd, %region_5.8_spmd} | conditional | flops 2178949376 | bytes 186886784 | solution.py:51
  207.9 16.2 %collective-permute-done.61 = bf16[2,128,2048]{2,1,0:T(8,128)(2,1)S(1)} collective-permute-done((bf16[2,128,2048]{2,1,0:T(8,128)(2,1)S(1)}, bf16[2,128,2048]{2,1,0:T(8,128)(2,1)S(1)}, u32[]{:S(2)}, u32[]{:S(2)}) %collective-permute-start.61) | collective-permute-done | bytes 1048608 | tf_op jit(solution)/shard_map/cond/branch_1_fun/ppermute | solution.py:93
  308.1 14.5 %fusion.81 = bf16[1024,2048]{1,0:T(8,128)(2,1)} fusion(bf16[1024,2048]{1,0:T(8,128)(2,1)} %get-tuple-element.610, bf16[1024,2048]{1,0:T(8,128)(2,1)} %get-tuple-element.608, bf16[1024,1024]{1,0:T(8,128)(2,1)} %get-tuple-element.607, bf16[1024,1024]{1,0:T(8,128)(2,1)} %get-tuple-element.606), kind=kOutput, calls=%fused_computation.254 | convolution fusion | flops 8617197568 | bytes 16777216 | tf_op jit(solution)/shard_map/tj,tk->jk/dot_general | solution.py:33
  322.7 66.0 %conditional.12 = (bf16[2,128,2048]{2,1,0:T(8,128)(2,1)}, bf16[2,128,2048]{2,1,0:T(8,128)(2,1)}, bf16[2,128,2048]{2,1,0:T(8,128)(2,1)}, bf16[2,128,2048]{2,1,0:T(8,128)(2,1)}, bf16[1024,2048]{1,0:T(8,128)(2,1)}) conditional(s32[]{:T(128)} %bitcast.146, () %tuple.159, (bf16[1024,2048]{1,0:T(8,128)(2,1)}, bf16[1024,2048]{1,0:T(8,128)(2,1)}, ...), branch_computations={%region_8.9_spmd, %region_9.10_spmd} | conditional | flops 25824329728 | bytes 201326880 | solution.py:51
  365.1 13.1 %fusion.29 = bf16[1024,2048]{1,0:T(8,128)(2,1)} fusion(bf16[1024,2048]{1,0:T(8,128)(2,1)} %get-tuple-element.273, bf16[1024,2048]{1,0:T(8,128)(2,1)} %get-tuple-element.272, bf16[1024,1024]{1,0:T(8,128)(2,1)S(1)} %copy-done.79, bf16[1024,1024]{1,0:T(8,128)(2,1)S(1)} %fusion.19), kind=kOutput, calls=%fused_computation.90 | convolution fusion | flops 8617197568 | bytes 16777216 | tf_op jit(solution)/shard_map/cond/branch_1_fun/tj,tk->jk/dot_general | solution.py:33
  398.7 76.4 %conditional.13 = (bf16[4,2048]{1,0:T(4,128)(2,1)S(1)}, bf16[4,2048]{1,0:T(4,128)(2,1)S(1)}, f32[4,64,2048]{2,1,0:T(8,128)}, bf16[4,2048]{1,0:T(4,128)(2,1)S(1)}...) conditional(s32[]{:T(128)} %bitcast.146, () %tuple.170, ...), branch_computations={%region_12.13_spmd, %region_13.19_spmd} | conditional | flops 16252930 | bytes 89843168 | solution.py:51
  490.1 84.9 %conditional.14 = (bf16[2048,768]{1,0:T(8,128)(2,1)}, bf16[1024,2048]{1,0:T(8,128)(2,1)}, f32[4,64,2048]{2,1,0:T(8,128)}) conditional(s32[]{:T(128)} %bitcast.146, () %tuple.153, (bf16[2048,768]{0,1:T(8,128)(2,1)}, bf16[1024,2048]{1,0:T(8,128)(2,1)}, bf16[256,2048]{1,0:T(8,128)(2,1)}, bf16[1024,2048]{1,0:T(8,128)(2,1)}, ...), branch_computations={%region_19.20_spmd, %region_20.21_spmd} | conditional | flops 10796662784 | bytes 187695744 | solution.py:51
  577.6 68.1 %conditional.15 = (bf16[1024,2048]{1,0:T(8,128)(2,1)}, bf16[1024,2048]{1,0:T(8,128)(2,1)S(1)}, f32[32,2,4,64]{3,0,2,1:T(8,128)}, bf16[256,2048]{1,0:T(8,128)(2,1...) conditional(s32[]{:T(128)} %bitcast.146, () %tuple.152, ...), branch_computations={%region_21.22_spmd, %region_22.24_spmd} | conditional | flops 409862176 | bytes 118637328 | solution.py:51
  647.7 56.8 %conditional.16 = (bf16[1024,2048]{1,0:T(8,128)(2,1)}, bf16[256,2048]{1,0:T(8,128)(2,1)}, bf16[256,2048]{1,0:T(8,128)(2,1)}, bf16[256,2048]{1,0:T(8,128)(2,1)}, ...) conditional(s32[]{:T(128)} %bitcast.146, () %tuple.178, (s32[1]{0:T(128)}, bf16[256,2048]{1,0:T(8,128)(2,1)}, ...), branch_computations={%region_26.27_spmd, %region_27.28_spmd} | conditional | flops 302055424 | bytes 33915172 | solution.py:51
  654.6 13.6 %branch_1_fun.26 = (bf16[1024,2048]{1,0:T(8,128)(2,1)}, bf16[1024,2048]{1,0:T(8,128)(2,1)}) custom-call(s32[1]{0:T(128)} %get-tuple-element.350.core_ref, bf16[256,2048]{1,0:T(8,128)(2,1)} %get-tuple-element.351.refs_0_, bf16[256,2048]{1,0:T(8,128)(2,1)} %get-tuple-element.352.refs_1_, bf16[256,2048]{1,0:T(8,128)(2,1)} %get-tuple-element.353.refs_2_, ...), custom_call_target="tpu_custom_call" | custom-call | flops 1 | bytes 1 | tf_op jit(solution)/shard_map/cond/branch_1_fun/pallas_call | solution.py:442
  678.9 25.2 %branch_1_fun.27 = bf16[1024,2048]{1,0:T(8,128)(2,1)} custom-call(s32[1]{0:T(128)} %get-tuple-element.350.core_ref, bf16[1024,2048]{1,0:T(8,128)(2,1)} %get-tuple-element.362.rows_ref, bf16[1024,2048]{1,0:T(8,128)(2,1)} %get-tuple-element.367.mine_ref, bf16[1024,2048]{1,0:T(8,128)(2,1)} %collective-permute-done.100.other_ref), custom_call_target="tpu_custom_call" | custom-call | flops 1 | bytes 1 | tf_op jit(solution)/shard_map/cond/branch_1_fun/pallas_call | solution.py:545
  713.9 280.6 %conditional.17 = (bf16[256,2048]{1,0:T(8,128)(2,1)S(1)}, f32[4,64,2048]{2,1,0:T(8,128)}, f32[32,2048]{1,0:T(8,128)}, bf16[1,2,64,2048]{3,2,0,1:T(8,128)(2,1)}, ...) conditional(s32[]{:T(128)} %bitcast.146, () %tuple.177, ...), branch_computations={%region_29.30_spmd, %region_30.31_spmd} | conditional | flops 17432692 | bytes 339217856 | solution.py:51
  726.5 13.3 %branch_1_fun.28 = (bf16[1024,2048]{1,0:T(8,128)(2,1)}, bf16[16,2048]{1,0:T(8,128)(2,1)}) custom-call(s32[1]{0:T(128)} %get-tuple-element.372.core_ref, bf16[1024,2048]{1,0:T(8,128)(2,1)} %get-tuple-element.404.refs_0_.rows_ref, bf16[1024,2048]{1,0:T(8,128)(2,1)} %collective-permute-done.16.refs_1_), custom_call_target="tpu_custom_call" | custom-call | flops 1 | bytes 1 | tf_op jit(solution)/shard_map/cond/branch_1_fun/pallas_call | solution.py:442
  750.0 13.5 %branch_1_fun.29 = (bf16[1024,2048]{1,0:T(8,128)(2,1)}, bf16[1024,2048]{1,0:T(8,128)(2,1)}) custom-call(s32[1]{0:T(128)} %get-tuple-element.372.core_ref, bf16[256,2048]{1,0:T(8,128)(2,1)} %get-tuple-element.385.refs_0_, bf16[256,2048]{1,0:T(8,128)(2,1)} %get-tuple-element.386.refs_1_, bf16[256,2048]{1,0:T(8,128)(2,1)} %get-tuple-element.387.refs_2_, ...), custom_call_target="tpu_custom_call" | custom-call | flops 1 | bytes 1 | tf_op jit(solution)/shard_map/cond/branch_1_fun/pallas_call | solution.py:442
  769.1 15.7 %branch_1_fun.30 = (bf16[256,2048]{1,0:T(8,128)(2,1)}, bf16[256,2048]{1,0:T(8,128)(2,1)}) custom-call(s32[1]{0:T(128)} %get-tuple-element.372.core_ref, bf16[1024,2048]{1,0:T(8,128)(2,1)} %get-tuple-element.404.refs_0_.rows_ref, bf16[1024,2048]{1,0:T(8,128)(2,1)} %get-tuple-element.405.mine_ref, bf16[1024,2048]{1,0:T(8,128)(2,1)} %collective-permute-done.23.other_ref), custom_call_target="tpu_custom_call" | custom-call | flops 1 | bytes 1 | tf_op jit(solution)/shard_map/cond/branch_1_fun/pallas_call | solution.py:545
  789.0 25.2 %branch_1_fun.31.refs_0_.rows_ref = bf16[1024,2048]{1,0:T(8,128)(2,1)} custom-call(s32[1]{0:T(128)} %get-tuple-element.372.core_ref, bf16[1024,2048]{1,0:T(8,128)(2,1)} %get-tuple-element.411.rows_ref, bf16[1024,2048]{1,0:T(8,128)(2,1)} %get-tuple-element.412.mine_ref, bf16[1024,2048]{1,0:T(8,128)(2,1)} %collective-permute-done.26.other_ref), custom_call_target="tpu_custom_call" | custom-call | flops 1 | bytes 1 | tf_op jit(solution)/shard_map/cond/branch_1_fun/pallas_call | solution.py:545
  823.9 13.3 %branch_1_fun.32 = (bf16[1024,2048]{1,0:T(8,128)(2,1)}, bf16[16,2048]{1,0:T(8,128)(2,1)}) custom-call(s32[1]{0:T(128)} %get-tuple-element.372.core_ref, bf16[1024,2048]{1,0:T(8,128)(2,1)} %branch_1_fun.31.refs_0_.rows_ref, bf16[1024,2048]{1,0:T(8,128)(2,1)} %collective-permute-done.35.refs_1_), custom_call_target="tpu_custom_call" | custom-call | flops 1 | bytes 1 | tf_op jit(solution)/shard_map/cond/branch_1_fun/pallas_call | solution.py:442
  846.1 13.9 %branch_1_fun.33 = (bf16[1024,2048]{1,0:T(8,128)(2,1)}, bf16[1024,2048]{1,0:T(8,128)(2,1)}) custom-call(s32[1]{0:T(128)} %get-tuple-element.372.core_ref, bf16[128,2048]{1,0:T(8,128)(2,1)} %copy-done.42, bf16[128,2048]{1,0:T(8,128)(2,1)} %copy-done.41, bf16[128,2048]{1,0:T(8,128)(2,1)} %copy-done.49, bf16[128,2048]{1,0:T(8,128)(2,1)} %collective-permute-done.31.refs_3_, ...), custom_call_target="tpu_custom_call" | custom-call | flops 1 | bytes 1 | tf_op jit(solution)/shard_map/cond/branch_1_fun/pallas_call | solution.py:442
  870.5 15.8 %branch_1_fun.34 = (bf16[256,2048]{1,0:T(8,128)(2,1)}, bf16[256,2048]{1,0:T(8,128)(2,1)}) custom-call(s32[1]{0:T(128)} %get-tuple-element.372.core_ref, bf16[1024,2048]{1,0:T(8,128)(2,1)} %branch_1_fun.31.refs_0_.rows_ref, bf16[1024,2048]{1,0:T(8,128)(2,1)} %get-tuple-element.441.mine_ref, bf16[1024,2048]{1,0:T(8,128)(2,1)} %collective-permute-done.43.other_ref), custom_call_target="tpu_custom_call" | custom-call | flops 1 | bytes 1 | tf_op jit(solution)/shard_map/cond/branch_1_fun/pallas_call | solution.py:545
  897.6 25.2 %branch_1_fun.35.refs_0_.rows_ref = bf16[1024,2048]{1,0:T(8,128)(2,1)} custom-call(s32[1]{0:T(128)} %get-tuple-element.372.core_ref, bf16[1024,2048]{1,0:T(8,128)(2,1)} %get-tuple-element.439.rows_ref, bf16[1024,2048]{1,0:T(8,128)(2,1)} %get-tuple-element.449.mine_ref, bf16[1024,2048]{1,0:T(8,128)(2,1)} %collective-permute-done.45.other_ref), custom_call_target="tpu_custom_call" | custom-call | flops 1 | bytes 1 | tf_op jit(solution)/shard_map/cond/branch_1_fun/pallas_call | solution.py:545
  945.5 13.7 %branch_1_fun.36 = (bf16[1024,2048]{1,0:T(8,128)(2,1)}, bf16[16,2048]{1,0:T(8,128)(2,1)}) custom-call(s32[1]{0:T(128)} %get-tuple-element.372.core_ref, bf16[1024,2048]{1,0:T(8,128)(2,1)} %branch_1_fun.35.refs_0_.rows_ref, bf16[1024,2048]{1,0:T(8,128)(2,1)} %collective-permute-done.53.refs_1_), custom_call_target="tpu_custom_call" | custom-call | flops 1 | bytes 1 | tf_op jit(solution)/shard_map/cond/branch_1_fun/pallas_call | solution.py:442
  (654 shorter events, 787.8 us)
Async XLA Ops:
  7.2 108.6 %all-gather.4.cloned.1.call-start = ((), (), s32[]{:S(2)}) async-start(), calls=%async_computation.8 | async-start | bytes 5242880 | tf_op jit(solution)/shard_map/all_gather | solution.py:100
  24.0 260.4 %all-gather.6.cloned.1.call-start = ((), (), s32[]{:S(2)}) async-start(), calls=%async_computation.9 | async-start | bytes 5242880 | tf_op jit(solution)/shard_map/all_gather | solution.py:100
  46.0 30.0 %all-to-all-start.1 = ((f32[32,1,3072]{2,1,0:T(1,128)}), f32[32,1,3072]{2,1,0:T(1,128)S(1)}, u32[]{:S(2)}, u32[]{:S(2)}) async-start(f32[32,1,3072]{2,1,0:T(1,128)} %reshape.374), calls=%async_computation.1 | async-start | bytes 786432 | tf_op jit(solution)/shard_map/cond/branch_1_fun/all_to_all | solution.py:648
  127.7 32.5 %collective-permute-start.10 = (bf16[128,2048]{1,0:T(8,128)(2,1)}, bf16[128,2048]{1,0:T(8,128)(2,1)}, u32[]{:S(2)}, u32[]{:S(2)}) collective-permute-start(bf16[128,2048]{1,0:T(8,128)(2,1)} %get-tuple-element.945), channel_id=1, source_target_pairs={{0,2},{1,3},{2,0},{3,1},{4,6},{5,7},{6,4},{7,5},{8,10},{9,11},{10,... | collective-permute-start | bytes 1572872 | tf_op jit(solution)/shard_map/cond/branch_1_fun/ppermute | solution.py:93
  129.0 36.8 %collective-permute-start.12 = (bf16[128,2048]{1,0:T(8,128)(2,1)}, bf16[128,2048]{1,0:T(8,128)(2,1)}, u32[]{:S(2)}, u32[]{:S(2)}) collective-permute-start(bf16[128,2048]{1,0:T(8,128)(2,1)} %get-tuple-element.945), channel_id=1, source_target_pairs={{0,4},{1,5},{2,6},{3,7},{4,0},{5,1},{6,2},{7,3},{8,12},{9,13},{10,... | collective-permute-start | bytes 1572872 | tf_op jit(solution)/shard_map/cond/branch_1_fun/ppermute | solution.py:93
  129.6 34.4 %collective-permute-start.11 = (bf16[128,2048]{1,0:T(8,128)(2,1)}, bf16[128,2048]{1,0:T(8,128)(2,1)}, u32[]{:S(2)}, u32[]{:S(2)}) collective-permute-start(bf16[128,2048]{1,0:T(8,128)(2,1)} %get-tuple-element.944), channel_id=1, source_target_pairs={{0,2},{1,3},{2,0},{3,1},{4,6},{5,7},{6,4},{7,5},{8,10},{9,11},{10,... | collective-permute-start | bytes 1572872 | tf_op jit(solution)/shard_map/cond/branch_1_fun/ppermute | solution.py:93
  130.9 30.4 %collective-permute-start.13 = (bf16[128,2048]{1,0:T(8,128)(2,1)}, bf16[128,2048]{1,0:T(8,128)(2,1)}, u32[]{:S(2)}, u32[]{:S(2)}) collective-permute-start(bf16[128,2048]{1,0:T(8,128)(2,1)} %get-tuple-element.944), channel_id=1, source_target_pairs={{0,4},{1,5},{2,6},{3,7},{4,0},{5,1},{6,2},{7,3},{8,12},{9,13},{10,... | collective-permute-start | bytes 1572872 | tf_op jit(solution)/shard_map/cond/branch_1_fun/ppermute | solution.py:93
  181.1 103.2 %all-to-all-start.3 = ((bf16[4,128,2048]{2,1,0:T(8,128)(2,1)}), bf16[4,128,2048]{2,1,0:T(8,128)(2,1)}, u32[]{:S(2)}, u32[]{:S(2)}) async-start(bf16[4,128,2048]{2,1,0:T(8,128)(2,1)} %bitcast.150), calls=%async_computation.3 | async-start | bytes 4194304 | tf_op jit(solution)/shard_map/all_to_all | solution.py:108
  185.5 122.6 %all-gather.8.cloned.1.call-start = ((), (), s32[]{:S(2)}) async-start(), calls=%async_computation.10 | async-start | bytes 5242880 | tf_op jit(solution)/shard_map/all_gather | solution.py:100
  186.3 212.4 %reduce-scatter.6.cloned.1.call-start = ((), (), s32[]{:S(2)}) async-start(), calls=%async_computation.12 | async-start | bytes 5242880 | tf_op jit(solution)/shard_map/reduce_scatter | solution.py:103
  201.0 83.0 %collective-permute-start.65 = (bf16[1024,2048]{1,0:T(8,128)(2,1)}, bf16[1024,2048]{1,0:T(8,128)(2,1)}, u32[]{:S(2)}, u32[]{:S(2)}) collective-permute-start(bf16[1024,2048]{1,0:T(8,128)(2,1)} %get-tuple-element.1062), channel_id=1, source_target_pairs={{0,1},{1,0},{2,3},{3,2},{4,5},{5,4},{6,7},{7,6},{8,9},{9,8},{10,11... | collective-permute-start | bytes 12582920 | tf_op jit(solution)/shard_map/cond/branch_1_fun/ppermute | solution.py:93
  228.8 55.3 %collective-permute-start.66 = (bf16[1024,2048]{1,0:T(8,128)(2,1)}, bf16[1024,2048]{1,0:T(8,128)(2,1)}, u32[]{:S(2)}, u32[]{:S(2)}) collective-permute-start(bf16[1024,2048]{1,0:T(8,128)(2,1)} %fusion.5), channel_id=1, source_target_pairs={{0,1},{1,0},{2,3},{3,2},{4,5},{5,4},{6,7},{7,6},{8,9},{9,8},{10,11... | collective-permute-start | bytes 12582920 | tf_op jit(solution)/shard_map/cond/branch_1_fun/ppermute | solution.py:93
  322.7 155.5 %reduce-scatter.4.cloned.1.call-start = ((), (), s32[]{:S(2)}) async-start(), calls=%async_computation.11 | async-start | bytes 5242880 | tf_op jit(solution)/shard_map/reduce_scatter | solution.py:103
  434.0 41.1 %collective-permute-start.8 = (bf16[1024,2048]{1,0:T(8,128)(2,1)}, bf16[1024,2048]{1,0:T(8,128)(2,1)}, u32[]{:S(2)}, u32[]{:S(2)}) collective-permute-start(bf16[1024,2048]{1,0:T(8,128)(2,1)} %get-tuple-element.291), channel_id=1, source_target_pairs={{0,1},{1,0},{2,3},{3,2},{4,5},{5,4},{6,7},{7,6},{8,9},{9,8},{10,11... | collective-permute-start | bytes 12582920 | tf_op jit(solution)/shard_map/cond/branch_1_fun/ppermute | solution.py:93
  485.6 89.5 %all-to-all-start.4 = ((bf16[4,128,2048]{2,1,0:T(8,128)(2,1)}), bf16[4,128,2048]{2,1,0:T(8,128)(2,1)}, u32[]{:S(2)}, u32[]{:S(2)}) async-start(bf16[4,128,2048]{2,1,0:T(8,128)(2,1)} %bitcast.157), calls=%async_computation.6 | async-start | bytes 4194304 | tf_op jit(solution)/shard_map/all_to_all | solution.py:108
  490.1 220.2 %reduce-scatter.8.cloned.1.call-start = ((), (), s32[]{:S(2)}) async-start(), calls=%async_computation.13 | async-start | bytes 5242880 | tf_op jit(solution)/shard_map/reduce_scatter | solution.py:103
  670.3 33.9 %collective-permute-start.103 = (bf16[256,2048]{1,0:T(8,128)(2,1)}, bf16[256,2048]{1,0:T(8,128)(2,1)}, u32[]{:S(2)}, u32[]{:S(2)}) collective-permute-start(bf16[256,2048]{1,0:T(8,128)(2,1)} %get-tuple-element.364), channel_id=1, source_target_pairs={{0,4},{1,5},{2,6},{3,7},{4,0},{5,1},{6,2},{7,3},{8,12},{9,13},{10,... | collective-permute-start | bytes 3145736 | tf_op jit(solution)/shard_map/cond/branch_1_fun/ppermute | solution.py:93
  671.6 32.6 %collective-permute-start.102 = (bf16[256,2048]{1,0:T(8,128)(2,1)}, bf16[256,2048]{1,0:T(8,128)(2,1)}, u32[]{:S(2)}, u32[]{:S(2)}) collective-permute-start(bf16[256,2048]{1,0:T(8,128)(2,1)} %get-tuple-element.369), channel_id=1, source_target_pairs={{0,2},{1,3},{2,0},{3,1},{4,6},{5,7},{6,4},{7,5},{8,10},{9,11},{10,... | collective-permute-start | bytes 3145736 | tf_op jit(solution)/shard_map/cond/branch_1_fun/ppermute | solution.py:93
  784.8 29.5 %collective-permute-start.31 = (bf16[128,2048]{1,0:T(8,128)(2,1)S(1)}, bf16[128,2048]{1,0:T(8,128)(2,1)}, u32[]{:S(2)}, u32[]{:S(2)}) collective-permute-start(bf16[128,2048]{1,0:T(8,128)(2,1)S(1)} %constant_dynamic-update-slice_fusion.30.refs_1_), channel_id=1, source_target_pairs={{0,2},{1,3},{2,0},{3,1},{4,6},{5,7},{6,4},{7,5},{8,10},{9,11},{10,... | collective-permute-start | bytes 1572872 | tf_op jit(solution)/shard_map/cond/branch_1_fun/ppermute | solution.py:93
  860.1 35.2 %collective-permute-start.45 = (bf16[1024,2048]{1,0:T(8,128)(2,1)}, bf16[1024,2048]{1,0:T(8,128)(2,1)}, u32[]{:S(2)}, u32[]{:S(2)}) collective-permute-start(bf16[1024,2048]{1,0:T(8,128)(2,1)} %get-tuple-element.449.mine_ref), channel_id=1, source_target_pairs={{0,1},{1,0},{2,3},{3,2},{4,5},{5,4},{6,7},{7,6},{8,9},{9,8},{10,11... | collective-permute-start | bytes 12582920 | tf_op jit(solution)/shard_map/cond/branch_1_fun/ppermute | solution.py:93
  994.5 53.6 %collective-permute-start.109 = (f32[32,2048]{1,0:T(8,128)}, f32[32,2048]{1,0:T(8,128)S(1)}, u32[]{:S(2)}, u32[]{:S(2)}) collective-permute-start(f32[32,2048]{1,0:T(8,128)} %get-tuple-element.676), channel_id=1, source_target_pairs={{0,8},{1,9},{2,10},{3,11},{4,12},{5,13},{6,14},{7,15},{8,16},{9,17... | collective-permute-start | bytes 786440 | tf_op jit(solution)/shard_map/ppermute | solution.py:97
  994.5 53.5 %collective-permute-start.110 = (f32[32,2048]{1,0:T(8,128)}, f32[32,2048]{1,0:T(8,128)}, u32[]{:S(2)}, u32[]{:S(2)}) collective-permute-start(f32[32,2048]{1,0:T(8,128)} %get-tuple-element.676), channel_id=1, source_target_pairs={{0,16},{1,17},{2,18},{3,19},{4,20},{5,21},{6,22},{7,23},{8,24},{9,... | collective-permute-start | bytes 786440 | tf_op jit(solution)/shard_map/ppermute | solution.py:97
  997.4 50.6 %collective-permute-start.111 = (f32[32,2048]{1,0:T(8,128)}, f32[32,2048]{1,0:T(8,128)}, u32[]{:S(2)}, u32[]{:S(2)}) collective-permute-start(f32[32,2048]{1,0:T(8,128)} %get-tuple-element.676), channel_id=1, source_target_pairs={{0,24},{1,25},{2,26},{3,27},{4,28},{5,29},{6,30},{7,31},{8,0},{9,1... | collective-permute-start | bytes 786440 | tf_op jit(solution)/shard_map/ppermute | solution.py:97
  999.9 33.1 %collective-permute-start.113 = (bf16[64,2048]{1,0:T(8,128)(2,1)}, bf16[64,2048]{1,0:T(8,128)(2,1)}, u32[]{:S(2)}, u32[]{:S(2)}) collective-permute-start(bf16[64,2048]{1,0:T(8,128)(2,1)} %get-tuple-element.998), channel_id=1, source_target_pairs={{0,8},{1,9},{2,10},{3,11},{4,12},{5,13},{6,14},{7,15},{8,16},{9,17... | collective-permute-start | bytes 786440 | tf_op jit(solution)/shard_map/ppermute | solution.py:97
  (185 other events, 2781.0 us)
Sparse Core Ops, SparseCore 0:
  24.1 89.9 all-gather.3
  116.2 94.6 all-gather.5
  213.1 95.0 all-gather.7
  322.8 75.8 reduce-scatter.5
  400.9 77.2 reduce-scatter.3
  575.2 80.4 reduce-scatter.7

commit v4 on v3

--- a/solution.py
+++ b/solution.py
@@ -147,6 +147,13 @@
             value = value + self.swap(value, bit)
         return value
 
+    def planes_over(self, value):
+        distance = 2
+        while distance < self.planes:
+            value = value + self.swap(value, distance * TEAM)
+            distance *= 2
+        return value
+
     def plane_total(self, value):
         others = [self.turn(value, offset) for offset in range(1, self.planes)]
         for other in others:
@@ -154,17 +161,31 @@
         return value
 
     def share(self, rows, between=()):
+        parts = self.share_begin(rows)
+        if between:
+            first_x, second_y = after_all(parts[3:5], *between)
+            parts = (*parts[:3], first_x, second_y, *parts[5:])
+        return self.share_end(parts)
+
+    def share_begin(self, rows):
         half = rows.shape[0] // 2
         first, second = rows[:half], rows[half:]
-        first_x = self.swap(first, ALONG_X)
-        second_y = self.swap(second, ALONG_Y)
-        first_y = self.swap(first, ALONG_Y)
-        second_x = self.swap(second, ALONG_X)
-        first_xy = self.swap(after(first_x, *between), ALONG_Y)
-        second_xy = self.swap(after(second_y, *between), ALONG_X)
-        return jnp.concatenate(
-            [rows, first_x, second_x, first_y, second_y, first_xy, second_xy], axis=0
-        )
+        return (
+            rows,
+            self.swap(first, ALONG_Y),
+            self.swap(second, ALONG_X),
+            self.swap(first, ALONG_X),
+            self.swap(second, ALONG_Y),
+        )
+
+    def share_end(self, parts):
+        return jnp.concatenate(self.share_last(parts), axis=0)
+
+    def share_last(self, parts):
+        rows, first_y, second_x, first_x, second_y = parts
+        first_xy = self.swap(first_x, ALONG_Y)
+        second_xy = self.swap(second_y, ALONG_X)
+        return [rows, first_x, second_x, first_y, second_y, first_xy, second_xy]
 
     def settle(self, near, near_too, beside=None):
         if beside is None:
@@ -174,21 +195,57 @@
         return self.settle_end(parts), done
 
     def settle_begin(self, near, near_too):
-        width = near.shape[-1]
-        size = near.shape[0] // 8
-        near = add(near, near_too).astype(low).reshape(2, 2, 2, size, width)
+        return self.settle_hops(add(near, near_too).astype(low))
+
+    def settle_pieces(self, near):
+        size, width = near.shape[0] // 8, near.shape[-1]
+        near = near.reshape(2, 2, 2, size, width)
+        first, second = near[:, :, 0], near[:, :, 1]
+        return (first[:, 0], second[0]), [(first[k, 1], second[1, k]) for k in (0, 1)]
+
+    def settle_split(self, near):
+        size, width = near.shape[0] // 8, near.shape[-1]
+        near = near.reshape(2, 2, 2, size, width)
+        first, second = near[:, :, 0], near[:, :, 1]
+        return (first[:, 0], second[0]), (first[:, 1], second[1])
+
+    def settle_hop(self, first, second):
+        return self.swap(first, ALONG_X), self.swap(second, ALONG_Y)
+
+    def settle_joined(self, kept, hops):
+        first, second = kept
+        (first_a, second_a), (first_b, second_b) = hops
+        return (
+            (add(first[0], first_a).astype(low), add(first[1], first_b).astype(low)),
+            (add(second[0], second_a).astype(low), add(second[1], second_b).astype(low)),
+        )
+
+    def settle_hops(self, near):
+        size, width = near.shape[0] // 8, near.shape[-1]
+        near = near.reshape(2, 2, 2, size, width)
         first, second = near[:, :, 0], near[:, :, 1]
         first_x = self.swap(first[:, 1], ALONG_X)
         second_y = self.swap(second[1], ALONG_Y)
         return first[:, 0], second[0], first_x, second_y
 
     def settle_end(self, parts):
+        return self.settle_sum(self.settle_last(self.settle_add(parts)))
+
+    def settle_add(self, parts):
         first, second, first_x, second_y = parts
-        first = add(first, first_x).astype(low)
-        second = add(second, second_y).astype(low)
-        first = add(first[0], self.swap(first[1], ALONG_Y))
-        second = add(second[0], self.swap(second[1], ALONG_X))
-        return jnp.concatenate([first, second], axis=0)
+        return (
+            [add(first[k], first_x[k]).astype(low) for k in (0, 1)],
+            [add(second[k], second_y[k]).astype(low) for k in (0, 1)],
+        )
+
+    def settle_last(self, parts):
+        first, second = parts
+        first_y, second_x = self.swap(first[1], ALONG_Y), self.swap(second[1], ALONG_X)
+        return first[0], second[0], first_y, second_x
+
+    def settle_sum(self, parts):
+        first, second, first_y, second_x = parts
+        return jnp.concatenate([add(first, first_y), add(second, second_x)], axis=0)
 
 
 VMEM_BYTES = 60 * 2**20
@@ -373,6 +430,69 @@
         compiler_params=pltpu.CompilerParams(vmem_limit_bytes=VMEM_BYTES),
         cost_estimate=QUICK,
     )(grads, weight, rows)
+
+
+def finish_body(*refs):
+    mlp, grads, refs = refs[:4], refs[4:8], refs[8:]
+    tokens_ref, middle_ref, gate_ref, upper_ref, scale_ref, out_ref, grad_ref = refs
+
+    def work(kept, came):
+        shape = middle_ref.shape
+        mlp_out = (mlp[kept][...].astype(wide) + mlp[came][...].astype(wide)).reshape(shape)
+        out_ref[...] = (middle_ref[...] + gate_ref[...] * mlp_out).astype(low)
+        grad = (grads[kept][...].astype(wide) + grads[came][...].astype(wide)).reshape(shape)
+        normed, inverse = normalize(tokens_ref[...].astype(wide))
+        grad = norm_back(grad * (1.0 + scale_ref[...]), normed, inverse)
+        grad_ref[...] = (upper_ref[...] + grad).astype(low)
+
+    @pl.when(pl.program_id(0) == 0)
+    def _():
+        work(0, 2)
+
+    @pl.when(pl.program_id(0) == 1)
+    def _():
+        work(1, 3)
+
+
+def finish(mlp, grads, tokens, middle, gate, upper, scale):
+    here, inner, width = tokens.shape
+    part = pl.BlockSpec(mlp[0].shape, lambda i: (0, 0))
+    rows = pl.BlockSpec((here // 2, inner, width), lambda i: (i, 0, 0))
+    line = pl.BlockSpec((here // 2, 1, width), lambda i: (i, 0, 0))
+    return pl.pallas_call(
+        finish_body,
+        grid=(2,),
+        in_specs=[part] * 8 + [rows, rows, line, rows, line],
+        out_specs=[rows, rows],
+        out_shape=[jax.ShapeDtypeStruct(tokens.shape, low)] * 2,
+        compiler_params=pltpu.CompilerParams(vmem_limit_bytes=VMEM_BYTES),
+        cost_estimate=QUICK,
+    )(*mlp, *grads, tokens, middle, gate, upper, scale)
+
+
+def arrange_body(place_ref, *refs, places):
+    *pieces, out_ref, sem = refs
+    copies = [
+        pltpu.make_async_copy(piece, out_ref.at[pl.ds(place(place_ref), piece.shape[0])], sem.at[k])
+        for k, (piece, place) in enumerate(zip(pieces, places))
+    ]
+    for copy in copies:
+        copy.start()
+    for copy in copies:
+        copy.wait()
+
+
+def arrange(place, pieces, places, count):
+    anywhere = pl.BlockSpec(memory_space=pl.ANY)
+    return pl.pallas_call(
+        functools.partial(arrange_body, places=places),
+        in_specs=[pl.BlockSpec(memory_space=pltpu.SMEM)] + [anywhere] * len(pieces),
+        out_specs=pl.BlockSpec(memory_space=pltpu.VMEM),
+        out_shape=jax.ShapeDtypeStruct((count,) + pieces[0].shape[1:], low),
+        scratch_shapes=[pltpu.SemaphoreType.DMA((len(pieces),))],
+        compiler_params=pltpu.CompilerParams(vmem_limit_bytes=VMEM_BYTES),
+        cost_estimate=QUICK,
+    )(place, *pieces)
 
 
 CHUNK = 512
@@ -635,6 +755,21 @@
     up_weight = gathered(4, start_down)
     down_weight = gathered(start_down, start_ada)
 
+    moment = matrix_moment.transpose(1, 0, 2)
+
+    def padded(batch, count):
+        spare = count - batch.shape[0]
+        if spare == 0:
+            return batch
+        return jnp.concatenate([batch, jnp.zeros((spare,) + batch.shape[1:], batch.dtype)], axis=0)
+
+    def to_owner(batch, each):
+        batch = padded(batch, planes * each)
+        return fabric.trade_planes(batch.reshape(planes, each * shard_rows, width))
+
+    def to_rows(batch, count):
+        return fabric.trade_planes(batch).reshape(-1, shard_rows, width)[:count]
+
     def begin(active):
         active = fabric.team_total(active)
         rows, active = hold(flat(tokens), active)
@@ -662,7 +797,8 @@
             [rows, first_x, second_x, first_y, second_y, first_xy, second_xy], axis=0
         )
         first_in = modulate(near.reshape(2, 2, here, inner, width), modulation)
-        return active, modulation, both(first_in.reshape(-1, width)), near
+        first_in = both(first_in.reshape(-1, width))
+        return active, modulation, first_in, near
 
     active, modulation, first_in, tokens_near = fence(valid, begin, active)
     local = modulation[0][:, :, None, :]
@@ -675,6 +811,7 @@
         ]
 
     def attention_forward(attention):
+        upstream = fabric.share_begin(flat(cotangent))
         attention = attention.reshape(planes, 4, shard_rows, width)
         pieces = [lax.dynamic_slice_in_dim(attention, place * heads, heads, 0)]
         for offset in range(1, peers):
@@ -684,37 +821,23 @@
         attention = jnp.stack(pieces).transpose(2, 1, 0, 3, 4).reshape(4, heads * HD, width)
         weight_in = attention[:3].reshape(3 * heads * HD, width)
         weight_out = attention[3]
-        projected = whole([dot("tk,jk->tj", rows, weight_in).astype(low) for rows in first_in])
-        upstream = fabric.share(after(flat(cotangent), weight_in), (projected,))
+        near, far = [dot("tk,jk->tj", rows, weight_in).astype(low) for rows in first_in]
+        projected = whole([near, far]).reshape(2, 2, 2, here, inner, 3 * heads * HD)
+        projected, upstream = hold(projected, upstream)
+        upstream = fabric.share_last(upstream)
         mixed = over_images(attend_body, here, inner, [projected], heads * HD)
         return weight_in, weight_out, projected, mixed, upstream
 
     weight_in, weight_out, projected, mixed, upstream = fence(valid, attention_forward, attention)
 
-    moment = matrix_moment.transpose(1, 0, 2)
-
-    def padded(batch, count):
-        spare = count - batch.shape[0]
-        if spare == 0:
-            return batch
-        return jnp.concatenate([batch, jnp.zeros((spare,) + batch.shape[1:], batch.dtype)], axis=0)
-
-    def to_owner(batch, each):
-        batch = padded(batch, planes * each)
-        return fabric.trade_planes(batch.reshape(planes, each * shard_rows, width))
-
-    def to_rows(batch, count):
-        return fabric.trade_planes(batch).reshape(-1, shard_rows, width)[:count]
-
-    ada_moment = to_owner(after(moment[start_ada:], mixed).astype(low), 2)
 
     def middle_forward(mixed, upstream):
-        def gated():
-            grad_mlp = open_rows(upstream) * modulated(modulation, 5)
-            return grad_mlp.astype(low).reshape(-1, width)
-
-        branch, grad_mlp = fabric.settle(*parts(halves(mixed), weight_out), gated)
-        branch = branch.reshape(here, inner, width)
+        upstream = whole(upstream)
+        branch = fabric.settle_begin(*parts(halves(mixed), weight_out))
+        grad_mlp = open_rows(upstream) * modulated(modulation, 5)
+        grad_mlp = grad_mlp.astype(low).reshape(-1, width)
+        branch, grad_mlp = hold(branch, grad_mlp)
+        branch = fabric.settle_end(branch).reshape(here, inner, width)
         middle = tokens.astype(wide) + gate_one * branch
         normed_two, inverse_two = normalize(middle)
         second_in = flat((normed_two * (1.0 + scale_two) + shift_two).astype(low))
@@ -726,7 +849,6 @@
     (
         branch, middle, normed_two, inverse_two, upstream, grad_mlp, second_in,
     ) = fence(valid, middle_forward, mixed, upstream)
-    second_in, ada_moment = hold(second_in, ada_moment)
 
     second_in = both(second_in)
     hidden, slope = [], []
@@ -752,54 +874,59 @@
 
         near, near_too = hold(*parts(grad_pre, up_weight))
         grad_in = fabric.settle_begin(near, near_too)
-        return hold(*grad_in, over_tokens(grad_pre, second_in))
-
-    *grad_in, up_grad = fence(valid, turn_back, grad_mlp)
+        far_hidden, near_too = hold(hidden[1], near_too)
+        seats = upstream[1].reshape(2, 2, here, inner, width)
+        mlp_far, far_gate = gate_sums(far_hidden, down_weight, seats)
+        return hold(*grad_in, over_tokens(grad_pre, second_in), mlp_far, far_gate)
+
+    *grad_in, up_grad, mlp_far, far_gate = fence(valid, turn_back, grad_mlp)
     up_sum = fabric.reduce_planes(up_grad)
 
-    def middle_back(grad_in):
+    def middle_back(grad_in, mlp_far, far_gate):
         grad_in = fabric.settle_end(grad_in).reshape(here, inner, width)
         grad_shift_two = jnp.sum(grad_in, axis=1)
         grad_scale_two = jnp.sum(grad_in * normed_two, axis=1)
         grad_middle = grad_total + norm_back(grad_in * (1.0 + scale_two), normed_two, inverse_two)
         grad_gate_one = jnp.sum(grad_middle * branch, axis=1)
         grad_branch = flat((grad_middle * gate_one).astype(low))
-        *ready, grad_branch = hold(*hidden, grad_branch)
-        seats = [rows.reshape(2, 2, here, inner, width) for rows in upstream]
-        mlp_far, far_gate = gate_sums(ready[1], down_weight, seats[1])
-        grad_branch = fabric.share(grad_branch, (mlp_far,))
-        mlp_near, near_gate = gate_sums(after(ready[0], mlp_far), down_weight, seats[0])
-        grad_branch, mlp_near, mlp_too = hold(grad_branch, mlp_near, fabric.swap(mlp_far, CORE))
+        ready, grad_branch = hold(hidden[0], grad_branch)
+        seats = upstream[0].reshape(2, 2, here, inner, width)
+        mlp_near, near_gate = gate_sums(ready, down_weight, seats)
+        grad_branch = fabric.share(grad_branch, (mlp_near,))
+        mlp_too = fabric.swap(mlp_far, CORE)
         grad_gate_two = far_gate + near_gate
+        grad_branch = both(grad_branch)
+        grad_mixed = whole([dot("tk,jk->tj", rows, weight_out).astype(low) for rows in grad_branch])
+        grad_project = over_images(
+            attend_back_body, here, inner, [projected, grad_mixed], 3 * heads * HD
+        )
         return (
             grad_shift_two, grad_scale_two, grad_middle, grad_gate_one, grad_gate_two, grad_branch,
-            mlp_near, mlp_too,
+            grad_project, mlp_near, mlp_too,
         )
 
     *grad_in, down_sum = hold(*grad_in, down_sum)
     (
         grad_shift_two, grad_scale_two, grad_middle, grad_gate_one, grad_gate_two, grad_branch,
-        mlp_near, mlp_too,
-    ) = fence(valid, middle_back, grad_in)
+        grad_project, mlp_near, mlp_too,
+    ) = fence(valid, middle_back, grad_in, mlp_far, far_gate)
 
     def fresh(first, grad):
         grad = grad.astype(wide).reshape(-1, shard_rows, width)
         return matrix_decay * moment[first : first + grad.shape[0]] + grad
 
-    up_sum, down_sum, grad_branch = hold(up_sum, down_sum, grad_branch)
-    dense_momentum = jnp.concatenate([fresh(4, up_sum), fresh(start_down, down_sum)], axis=0)
-    dense_rows, grad_branch = hold(dense_momentum.astype(low), grad_branch)
+    up_sum, down_sum, grad_project = hold(up_sum, down_sum, grad_project)
+
+    def dense_momentum():
+        return jnp.concatenate([fresh(4, up_sum), fresh(start_down, down_sum)], axis=0)
+
+    dense_rows, grad_project = hold(dense_momentum().astype(low), grad_project)
     dense_rows = to_owner(dense_rows, 2)
 
-    def attention_back(grad_branch, mlp_near, mlp_too):
-        grad_branch = both(grad_branch)
-        mlp_sums = fabric.settle_begin(mlp_near, mlp_too)
-        grad_mixed = whole([dot("tk,jk->tj", rows, weight_out).astype(low) for rows in grad_branch])
-        grad_project = over_images(
-            attend_back_body, here, inner, [projected, grad_mixed], 3 * heads * HD
-        )
-        grad_project, *mlp_sums = hold(grad_project, *mlp_sums)
-        mlp_out = fabric.settle_end(mlp_sums)
+    def attention_back(grad_branch, grad_project):
+        grads = halves(grad_project)
+        seats = [rows.reshape(2, 2, here, inner, width) for rows in both(tokens_near)]
+        near, far = [norm_sums(grads[k], weight_in, seats[k]) for k in (0, 1)]
         in_grad = over_tokens([grad_project], first_in).reshape(3, heads * HD, width)
         out_grad = over_tokens([mixed], grad_branch).reshape(1, heads * HD, width)
         attention_grad = jnp.concatenate([in_grad, out_grad], axis=0)
@@ -812,12 +939,19 @@
         attention_grad = lax.dynamic_slice_in_dim(
             attention_grad, (peers - place) % peers * heads, planes, 0
         )
-        return grad_project, attention_grad.reshape(planes * 4 * shard_rows, width), mlp_out
-
-    grad_project, attention_grad, mlp_out = fence(
-        valid, attention_back, grad_branch, mlp_near, mlp_too
+        sums = near[1] + far[1]
+        own = jnp.stack([grad_gate_one, grad_shift_two, grad_scale_two], axis=0)
+        own = jnp.stack([own, jnp.zeros_like(own)], axis=1)
+        stacked = jnp.concatenate([sums, own, grad_gate_two[None]], axis=0)
+        stacked = jnp.where(seat // 4 == 0, stacked, stacked[:, ::-1])
+        stacked = stacked.reshape(6, 2 * here, fabric.count, shard_rows).astype(low)
+        stacked = stacked.transpose(2, 1, 0, 3)
+        attention_grad = attention_grad.reshape(planes * 4 * shard_rows, width)
+        return attention_grad, stacked, near[0], far[0]
+
+    attention_grad, stacked, first_near, first_far = fence(
+        valid, attention_back, grad_branch, grad_project
     )
-    mlp_out = mlp_out.reshape(here, inner, width)
     attention_grad, dense_rows = hold(attention_grad, dense_rows)
     attention_sum = fabric.reduce_planes(attention_grad)
 
@@ -830,199 +964,267 @@
     def joined(mine, other):
         mine = mine.reshape(planes, 1, shard_rows, width)
         other = other.reshape(planes, 1, shard_rows, width)
-        return fabric.slots_of(jnp.concatenate([mine, other], axis=1))
+        rows = jnp.concatenate([mine, other, mine], axis=1)
+        return [
+            lax.dynamic_slice(
+                rows, ((plane - j) % planes, side, 0, 0), (1, 2, shard_rows, width)
+            )[0]
+            for j in range(planes)
+        ]
 
     def two_units(own, came):
-        rows = fabric.by_plane(own, came)
-        rows = jnp.where(side == 0, rows, rows[:, ::-1])
-        return rows.reshape(2 * planes, shard_rows, width)
-
-    def to_owners(stacked):
-        spare = 2 * planes - 6
-        stacked = jnp.concatenate(
-            [stacked, jnp.zeros((2 * here, spare, width), stacked.dtype)], axis=1
-        ).reshape(2 * here, planes, 2, planes, TEAM, shard_rows)
-        stacked = stacked.transpose(1, 4, 0, 2, 3, 5)
-        stacked = stacked.reshape(fabric.count, 2 * here, 2, planes, shard_rows)
-        held = lax.all_to_all(stacked, WORLD, split_axis=0, concat_axis=0, tiled=True)
-        held = held.reshape(planes, TEAM, 2 * here, 2, planes, shard_rows)
-        return jnp.sum(held.astype(wide), axis=1).reshape(images, 2, planes, shard_rows)
-
-    def enter(grad_project, dense_rows):
+        return fabric.by_plane(own, came).reshape(2 * planes, shard_rows, width)
+
+    def to_holders(stacked):
+        return lax.all_to_all(stacked, WORLD, split_axis=0, concat_axis=0, tiled=True)
+
+    def summed_parts(held):
+        held = held.reshape(planes, TEAM, 2 * here, 6, shard_rows)
+        return jnp.sum(held.astype(wide), axis=1).reshape(images, 6, shard_rows)
+
+    def enter(dense_rows, stacked, first_far):
         d, d_other = two_of(dense_rows)
-        grads = halves(grad_project)
-        seats = [rows.reshape(2, 2, here, inner, width) for rows in both(tokens_near)]
-        d, d_x, d_y, near, far = hold(
-            d,
-            fabric.swap(d_other, ALONG_X),
-            fabric.swap(d, ALONG_Y),
-            norm_sums(grads[0], weight_in, seats[0]),
-            norm_sums(grads[1], weight_in, seats[1]),
-        )
-        sums = near[1] + far[1]
-        own = jnp.stack([grad_gate_one, grad_shift_two, grad_scale_two], axis=0)
-        own = jnp.stack([own, jnp.zeros_like(own)], axis=1)
-        stacked = jnp.concatenate([sums, own, grad_gate_two[None]], axis=0)
-        stacked = jnp.where(seat // 4 == 0, stacked, stacked[:, ::-1])
-        stacked = stacked.reshape(6, 2 * here, width).transpose(1, 0, 2).astype(low)
-        owned = to_owners(stacked)
-        d_near = [d, d_x, d_y]
-        d_far = [fabric.swap(piece, CORE) for piece in d_near]
-        d_xy = fabric.swap(d_x, ALONG_Y)
-        d_xy, owned, *d_far = hold(d_xy, owned, *d_far)
-        d_far_xy = fabric.swap(d_xy, CORE)
-        ada = jnp.einsum("nuzr,nk->zurk", owned, active.astype(wide), precision=highest)
-        ada += matrix_decay * ada_moment.astype(wide).reshape(ada.shape)
-        a, a_other = two_of(ada.astype(low))
-        d_far_xy, a, a_other = hold(d_far_xy, a, a_other)
-        block_out = (middle + gate_two * mlp_out).astype(low)
-        return near[0], far[0], owned, d_near + [d_xy], d_far + [d_far_xy], a, a_other, block_out
-
-    first_near, first_far, owned, d, d_far, a, a_other, block_out = fence(
-        valid, enter, grad_project, dense_rows
+        d_x, d_y = fabric.swap(d_other, ALONG_X), fabric.swap(d, ALONG_Y)
+        held = to_holders(stacked)
+        first_too = fabric.swap(first_far, CORE)
+        mlp_split = fabric.settle_split(add(mlp_near, mlp_too).astype(low))
+        d, d_x, d_y, first_too, mlp_split, held = hold(d, d_x, d_y, first_too, mlp_split, held)
+        grad_mod_all = summed_parts(held)
+        d_far = [fabric.swap(piece, CORE) for piece in (d, d_x, d_y)]
+        ada_momentum = matrix_decay * moment[start_ada:] + jnp.einsum(
+            "nur,nk->urk", grad_mod_all, active.astype(wide), precision=highest
+        )
+        ada_rows = ada_momentum.astype(low)
+        ada_momentum, ada_rows, d_far = hold(ada_momentum, ada_rows, d_far)
+        return grad_mod_all, ada_momentum, ada_rows, mlp_split, first_too, [d, d_x, d_y], d_far
+
+    grad_mod_all, ada_momentum, ada_rows, mlp_split, first_too, d, d_far = fence(
+        valid, enter, dense_rows, stacked, first_far
     )
-
-    def steps_one(d, d_far, a, a_other, owned):
-        a_x, a_y = fabric.swap(a_other, ALONG_X), fabric.swap(a, ALONG_Y)
-        grad_mod_all = fabric.trade_planes(owned.transpose(2, 0, 1, 3))
-        d_half, d = half_gram(core, d, d_far)
-        a_far = fabric.swap(a, CORE)
-        d, d_half, grad_mod_all = hold(d, d_half, grad_mod_all)
-        grad_mod_all = grad_mod_all.transpose(1, 0, 2, 3)
-        grad_mod_all = grad_mod_all.reshape(images, 2 * planes, shard_rows)[:, :6]
+    ada_rows = to_owner(ada_rows, 2)
+
+    step_size = matrix_rate * 0.2 * math.sqrt(width)
+
+    def steps_one(d, d_far, grad_mod_all, mlp_hops, first_near, first_too):
+        first_split = fabric.settle_pieces(add(first_near, first_too).astype(low))
         grad_active = jnp.einsum(
             "nur,ruk->nk", grad_mod_all, ada_weight.astype(wide), precision=highest
         )
-        d_half, d_other, a_far, grad_active = hold(
-            d_half, fabric.swap(d_half, CORE), a_far, grad_active
-        )
+        grad_active_core = fabric.swap(grad_active, CORE)
+        d_xy, first_split, grad_active_core = hold(
+            fabric.swap(d[1], ALONG_Y), first_split, grad_active_core
+        )
+        grad_active = grad_active + grad_active_core
+        d_far_xy, grad_active = hold(fabric.swap(d_xy, CORE), grad_active)
+        d, d_far = d + [d_xy], d_far + [d_far_xy]
+        grad_active_x = fabric.swap(grad_active, ALONG_X)
+        d_half, d = half_gram(core, d, d_far)
+        d, d_half, grad_active_x = hold(d, d_half, grad_active_x)
+        grad_active = grad_active + grad_active_x
+        d_half, d_other, grad_active, mlp_hops = hold(
+            d_half, fabric.swap(d_half, CORE), grad_active, mlp_hops
+        )
+        mlp_came = fabric.settle_hop(*mlp_hops)
         d = polynomial(core, d, d_half, d_other, True)
-        grad_active += fabric.swap(grad_active, CORE)
-        return hold(d, a_x, a_y, a_far, grad_mod_all, grad_active)
-
-    d, a_x, a_y, a_far, grad_mod_all, grad_active = fence(
-        valid, steps_one, d, d_far, a, a_other, owned
+        d, mlp_came = hold(d, mlp_came)
+        return d, grad_active, mlp_came, first_split
+
+    mlp_kept = mlp_split[0]
+    d, grad_active, mlp_came, first_split = fence(
+        valid, steps_one, d, d_far, grad_mod_all, mlp_split[1], first_near, first_too
     )
-    d, a_x, a_y, attention_sum = hold(d, a_x, a_y, attention_sum)
-    attention_momentum = fresh(0, attention_sum)
+    mlp_sum = (*mlp_kept, *mlp_came)
+    d, ada_rows, attention_sum = hold(d, ada_rows, attention_sum)
 
     def steps_two(
-        d, a, a_x, a_y, a_far, attention_momentum, first_near, first_far, grad_active
+        d, ada_rows, attention_sum, mlp_sum, first_split, grad_active, ada_momentum
     ):
-        t_own = padded(attention_momentum.astype(low), planes)
-        a_xy = fabric.swap(a_x, ALONG_Y)
-        a_far = [a_far, fabric.swap(a_x, CORE), fabric.swap(a_y, CORE)]
-        d, d_far, t_own = hold(d, fabric.swap(d, CORE), t_own)
+        a, a_other = hold(*two_of(ada_rows))
+        a_x, a_y = fabric.swap(a_other, ALONG_X), fabric.swap(a, ALONG_Y)
+        t_own = padded(fresh(0, attention_sum).astype(low), planes)
+        d, d_far, t_own, attention_sum = hold(d, fabric.swap(d, CORE), t_own, attention_sum)
+
         t_slots = {0: lax.dynamic_index_in_dim(t_own, plane, 0, keepdims=False)}
         t_slots.update(fabric.to_owners(t_own, 0))
         t_slots.update(fabric.to_owners(t_own, 1))
+        a_far = fabric.swap(a, CORE)
         d_half, _ = half_gram(core, [d], [d_far])
-        d, d_half, a_xy, t_slots, a_far = hold(d, d_half, a_xy, t_slots, a_far)
-        t_slots.update(fabric.to_owners(t_own, 2))
-        d_other = fabric.swap(d_half, CORE)
-        a_near, a_far_xy = hold([a, a_x, a_y, a_xy], fabric.swap(a_xy, CORE))
-        grad_active_x = fabric.swap(grad_active, ALONG_X)
-        a_half, a = half_gram(core, a_near, a_far + [a_far_xy])
-        a, a_half, d_half, d_other, t_slots, grad_active_x = hold(
-            a, a_half, d_half, d_other, t_slots, grad_active_x
-        )
-        grad_active += grad_active_x
+        d, d_half, t_slots, a_x, a_y, a_far = hold(d, d_half, t_slots, a_x, a_y, a_far)
+
+        a_xy = fabric.swap(a_x, ALONG_Y)
+        first_kept, first_hops = first_split
+        mlp_sum = fabric.settle_add(mlp_sum)
+        d_half, d_other, mlp_sum = hold(d_half, fabric.swap(d_half, CORE), mlp_sum)
+
+        t_last = fabric.to_owners(t_own, 2)
+        a_far = [a_far] + [fabric.swap(piece, CORE) for piece in (a_x, a_y)]
+        d_rows, d_beside = polynomial(core, d, d_half, d_other, False, 2)
+        d_rows, d_beside, t_last, a_far, a_xy = hold(d_rows, d_beside, t_last, a_far, a_xy)
+
+        t_slots.update(t_last)
         t_slots = [t_slots[j] for j in range(planes)]
         t_first = jnp.concatenate(t_slots[: planes // 2], axis=0)
         t_second = jnp.concatenate(t_slots[planes // 2 :], axis=0)
-        t_first_x, t_second_y = fabric.swap(t_first, ALONG_X), fabric.swap(t_second, ALONG_Y)
-        t_far = [fabric.swap(t_first, CORE), fabric.swap(t_second, CORE)]
+        a_far_xy, t_first, t_second, grad_active = hold(
+            fabric.swap(a_xy, CORE), t_first, t_second, grad_active
+        )
+
+        d_x = fabric.swap(d_beside, ALONG_X)
+        t_second_y = fabric.swap(t_second, ALONG_Y)
+        t_first_far, t_second_far = fabric.swap(t_first, CORE), fabric.swap(t_second, CORE)
+        grad_active_y = fabric.swap(grad_active, ALONG_Y)
+        a_half, a = half_gram(core, [a, a_x, a_y, a_xy], a_far + [a_far_xy])
+        a, a_half, t_second_y, t_first_far, t_second_far, d_x, grad_active_y = hold(
+            a, a_half, t_second_y, t_first_far, t_second_far, d_x, grad_active_y
+        )
+
+        d_slots = joined(d_rows, d_x)
+        grad_active = grad_active + grad_active_y
+        a_half, a_other, d_slots, grad_active = hold(
+            a_half, fabric.swap(a_half, CORE), d_slots, grad_active
+        )
+
+        t_first_x, t_first_y = fabric.swap(t_first, ALONG_X), fabric.swap(t_first, ALONG_Y)
+        t_second_x = fabric.swap(t_second, ALONG_X)
+        d_came = fabric.from_owners(d_slots, 0)
+        d_came.update(fabric.from_owners(d_slots, 1))
+        a = polynomial(core, a, a_half, a_other, True)
+        a, t_first_x, t_first_y, t_second_x, d_came, grad_active = hold(
+            a, t_first_x, t_first_y, t_second_x, d_came, grad_active
+        )
+
+        grad_active_z = fabric.swap(grad_active, TEAM)
+        momentum = jnp.concatenate(
+            [fresh(0, attention_sum), dense_momentum(), ada_momentum], axis=0
+        ).transpose(1, 0, 2)
+        a, a_far, grad_active_z, momentum = hold(
+            a, fabric.swap(a, CORE), grad_active_z, momentum
+        )
+        grad_active = grad_active + grad_active_z
+
+        t_first_xy, t_second_xy = fabric.swap(t_first_x, ALONG_Y), fabric.swap(t_second_y, ALONG_X)
+        t_first_x_far, t_second_y_far = fabric.swap(t_first_x, CORE), fabric.swap(t_second_y, CORE)
+        grad_active = fabric.planes_over(grad_active)
+        a_half, _ = half_gram(core, [a], [a_far])
+        a, a_half, t_first_x_far, t_second_y_far, t_first_xy, t_second_xy, grad_active = hold(
+            a, a_half, t_first_x_far, t_second_y_far, t_first_xy, t_second_xy, grad_active
+        )
+
+        a_half, t_first_y_far, t_second_x_far, t_first_xy_far, t_second_xy_far = hold(
+            a_half,
+            *[
+                fabric.swap(piece, CORE)
+                for piece in (t_first_y, t_second_x, t_first_xy, t_second_xy)
+            ],
+        )
+
         a_other = fabric.swap(a_half, CORE)
-        d_rows, d_beside = polynomial(core, d, d_half, d_other, False, 2)
-        d_rows, d_beside, a_half, a_other, t_first_x, t_second_y, t_far = hold(
-            d_rows, d_beside, a_half, a_other, t_first_x, t_second_y, t_far
-        )
-        t_second_x, t_first_y = fabric.swap(t_second, ALONG_X), fabric.swap(t_first, ALONG_Y)
-        t_second_xy, t_first_xy = fabric.swap(t_second_y, ALONG_X), fabric.swap(t_first_x, ALONG_Y)
-        a = polynomial(core, a, a_half, a_other, True)
-        a, t_second_x, t_first_y, t_second_xy, t_first_xy = hold(
-            a, t_second_x, t_first_y, t_second_xy, t_first_xy
-        )
-        t_near = [t_first, t_second, t_first_x, t_second_x, t_first_y, t_second_y]
-        t_near = t_near + [t_first_xy, t_second_xy]
-        d_x = fabric.swap(d_beside, ALONG_X)
-        first_too = fabric.swap(first_far, CORE)
-        a, a_far = hold(a, fabric.swap(a, CORE))
-        t_far = t_far + [fabric.swap(piece, CORE) for piece in t_near[2:]]
-        first_sums = fabric.settle_begin(first_near, first_too)
-        a_half, _ = half_gram(core, [a], [a_far])
-        a, a_half, t_far, d_x = hold(a, a_half, t_far, d_x)
-        d_slots = joined(d_rows, d_x)
-        d_came = fabric.from_owners(d_slots, 0)
-        a_other = fabric.swap(a_half, CORE)
-        t_half, t = half_gram(core, t_near, t_far)
-        t, t_half, a_half, a_other, d_came = hold(t, t_half, a_half, a_other, d_came)
-        d_came.update(fabric.from_owners(d_slots, 1))
+        d_mine = fabric.from_owners([rows[:1] for rows in d_slots], 2)
+        first_came = [fabric.settle_hop(*first_hops[0])]
+        t_half, t = half_gram(
+            core,
+            [t_first, t_second, t_first_x, t_second_x, t_first_y, t_second_y, t_first_xy,
+             t_second_xy],
+            [t_first_far, t_second_far, t_first_x_far, t_second_x_far, t_first_y_far,
+             t_second_y_far, t_first_xy_far, t_second_xy_far],
+        )
+        t, t_half, a_half, a_other, d_mine, first_came = hold(
+            t, t_half, a_half, a_other, d_mine, first_came
+        )
+
+        d_next = fabric.from_owners([rows[1:] for rows in d_slots], 2)
+        first_came = first_came + [fabric.settle_hop(*first_hops[1])]
         t_other = fabric.swap(t_half, CORE)
         a_rows, a_beside = polynomial(core, a, a_half, a_other, False, 2)
-        a_rows, a_beside, t_half, t_other, d_came, first_sums = hold(
-            a_rows, a_beside, t_half, t_other, d_came, first_sums
-        )
-        d_came.update(fabric.from_owners(d_slots, 2))
+        a_rows, a_beside, t_half, t_other, d_next, first_came = hold(
+            a_rows, a_beside, t_half, t_other, d_next, first_came
+        )
+
         a_x = fabric.swap(a_beside, ALONG_X)
-        grad_active_y = fabric.swap(grad_active, ALONG_Y)
+        a_slots = fabric.slots_of(a_rows.reshape(planes, shard_rows, width))
+        a_came = {}
+        for group in range(3):
+            a_came.update(fabric.from_owners(a_slots, group))
         t = polynomial(core, t, t_half, t_other, True)
-        t, a_x, d_came, grad_active_y = hold(t, a_x, d_came, grad_active_y)
-        grad_active += grad_active_y
-        a_slots = joined(a_rows, a_x)
-        a_came = fabric.from_owners(a_slots, 0)
-        a_came.update(fabric.from_owners(a_slots, 1))
-        t, t_far = hold(t, fabric.swap(t, CORE))
-        grad_first = fabric.settle_end(first_sums).reshape(here, inner, width)
+        t, a_x, a_came = hold(t, a_x, a_came)
+
+        a_side = fabric.slots_of(a_x.reshape(planes, shard_rows, width))
+        first_sum = fabric.settle_joined(first_kept, first_came)
+        table_grad = jnp.dot(selector.T, grad_active, precision=highest) * silu_slope(level_table)
+        table_momentum = vector_decay * table_moment + table_grad
+        table_new = level_table - table_rate * table_momentum
+        t, t_far, a_side, first_sum, *tables = hold(
+            t, fabric.swap(t, CORE), a_side, first_sum, table_grad, table_momentum, table_new
+        )
+
+        side_came = fabric.from_owners(a_side, 0)
+        side_came.update(fabric.from_owners(a_side, 1))
+        mlp_sum = fabric.settle_last(mlp_sum)
         t_half, _ = half_gram(core, [t], [t_far])
-        t, t_half, a_came, grad_first = hold(t, t_half, a_came, grad_first)
-        a_came.update(fabric.from_owners(a_slots, 2))
+        t, t_half, side_came, mlp_sum = hold(t, t_half, side_came, mlp_sum)
+
+        first_sum = fabric.settle_last(first_sum)
+        side_last = fabric.from_owners(a_side, 2)
         t_half, t_other = hold(t_half, fabric.swap(t_half, CORE))
+
         (t_rows,) = polynomial(core, t, t_half, t_other, False, 1)
-        t_rows, a_came = hold(t_rows, a_came)
-        return t_rows, d_slots[0], d_came, a_slots[0], a_came, grad_first, grad_active
-
-    t_rows, d_own, d_came, a_own, a_came, grad_first, grad_active = fence(
-        valid, steps_two, d, a, a_x, a_y, a_far, attention_momentum, first_near, first_far,
-        grad_active,
+        t_rows, side_last, first_sum, mlp_sum = hold(t_rows, side_last, first_sum, mlp_sum)
+
+        side_came.update(side_last)
+        t_slots = [t_rows[j * shard_rows : (j + 1) * shard_rows] for j in range(planes)]
+        t_came = {}
+        for group in (2, 0, 1):
+            t_came.update(fabric.from_owners(t_slots, group))
+        block_out, input_grad = finish(
+            mlp_sum, first_sum, tokens, middle, gate_two, grad_middle, scale_one
+        )
+
+        place = jnp.stack([plane, side]).astype(jnp.int32)
+
+        def put(came, base, each, which=lambda side: 0):
+            return [
+                (
+                    rows.reshape(-1, shard_rows, width),
+                    lambda ref, distance=distance: base
+                    + (ref[0] + distance) % planes * each
+                    + which(ref[1]),
+                )
+                for distance, rows in came.items()
+            ]
+
+        near_t = fabric.pieces()[0][0]
+        t_came[near_t], d_next, d_mine = hold(t_came[near_t], d_next, d_mine)
+        items = put({0: d_slots[0], **d_came, **d_mine}, 0, 2)
+        items += put(d_next, 0, 2, lambda side: 1)
+        items += put({0: a_slots[0], **a_came}, 2 * planes, 2, lambda side: side)
+        items += put({0: a_side[0], **side_came}, 2 * planes, 2, lambda side: 1 - side)
+        ortho = arrange(place, *zip(*items), 4 * planes)
+        ortho = jnp.concatenate(
+            [
+                jnp.zeros((4, shard_rows, width), low),
+                ortho[: 2 * blocks],
+                ortho[2 * planes : 2 * planes + 6],
+            ],
+            axis=0,
+        ).transpose(1, 0, 2)
+        matrix_new = matrices - step_size * ortho.astype(wide)
+        t_came, block_out, input_grad, matrix_new = hold(
+            t_came, block_out, input_grad, matrix_new
+        )
+        ortho = arrange(place, *zip(*put({0: t_slots[0], **t_came}, 0, 1)), planes)
+        ortho = ortho[:4].transpose(1, 0, 2).astype(wide)
+        matrix_new = matrix_new.at[:, :4].set(matrices[:, :4] - step_size * ortho)
+        return matrix_new, block_out, input_grad, tables, momentum
+
+    matrix_new, block_out, input_grad, tables, momentum = fence(
+        valid, steps_two, d, ada_rows, attention_sum, mlp_sum, first_split, grad_active,
+        ada_momentum,
     )
-    t_slots = [t_rows[j * shard_rows : (j + 1) * shard_rows] for j in range(planes)]
-    t_came = {}
-    for group in range(3):
-        t_came.update(fabric.from_owners(t_slots, group))
-    dense_ortho = two_units(d_own, d_came)
-    ada_ortho = two_units(a_own, a_came)
-    attention_ortho = fabric.by_plane(t_slots[0], t_came)
-    grad_active = fabric.plane_total(grad_active)
-    ada_momentum = matrix_decay * moment[start_ada:] + jnp.einsum(
-        "nur,nk->urk", grad_mod_all, active.astype(wide), precision=highest
-    )
-
-    normed_one, inverse_one = normalize(tokens.astype(wide))
-    input_grad = grad_middle + norm_back(
-        grad_first * (1.0 + scale_one), normed_one, inverse_one
-    )
-    input_grad = input_grad.astype(low)
-    dense_ortho, ada_ortho = dense_ortho[: 2 * blocks], ada_ortho[:6]
-    attention_ortho = attention_ortho[:4]
 
     bias_grad = jnp.sum(grad_mod_all, axis=0)
-    table_grad = jnp.dot(selector.T, grad_active, precision=highest) * silu_slope(level_table)
-    momentum = jnp.concatenate(
-        [
-            attention_momentum,
-            dense_momentum,
-            ada_momentum,
-        ],
-        axis=0,
-    ).transpose(1, 0, 2)
-    ortho = jnp.concatenate([attention_ortho, dense_ortho, ada_ortho], axis=0).transpose(1, 0, 2)
-    step_size = matrix_rate * 0.2 * math.sqrt(width)
-    matrix_new = matrices - step_size * ortho.astype(wide)
+    table_grad, table_momentum, table_new = tables
     bias_momentum = vector_decay * bias_moment + bias_grad
     bias_new = modulation_bias - bias_rate * bias_momentum
-    table_momentum = vector_decay * table_moment + table_grad
-    table_new = level_table - table_rate * table_momentum
     return (
         block_out,
         input_grad,

time: 1070 us -> 978 us (0.914)
  waiting for transfers between devices: 254 us -> 185 us
  local copies, waits for them, and re-layouts: 142 us -> 119 us
  Pallas kernels: 260 us -> 276 us
  other arithmetic: 120 us -> 106 us
    ppermute x95 -> x99, waiting for transfers between devices: 178 us -> 145 us  [swap(): return lax.ppermute(value, WORLD, [(d, d ^ bit) for d in range(self.count)])]
    ppermute x18 -> x19, waiting for transfers between devices: 29.2 us -> 1.04 us  [turn(): return lax.ppermute(value, WORLD, pairs)]
    pallas_call x0 -> x3, Pallas kernels: none -> 14.3 us  [the longest x2 7.84 us: arrange(): pl.pallas_call(functools.partial(arrange_body, places=places), in_specs=[...]
    convert_element_type x16 -> x14, other arithmetic: 39.9 us -> 33 us  [the longest x1 5.58 us: middle_forward(): grad_mlp = grad_mlp.astype(low).reshape(-1, width)]
    cond x130 -> x136, local copies, waits for them, and re-layouts: 52.7 us -> 47.6 us
    ppermute x95 -> x99, starting transfers between devices: 70.6 us -> 74.4 us  [swap(): return lax.ppermute(value, WORLD, [(d, d ^ bit) for d in range(self.count)])]
    ppermute x18 -> x19, starting transfers between devices: 31.8 us -> 31.3 us  [turn(): return lax.ppermute(value, WORLD, pairs)]
  transfers between devices with their start and end apart: 126 -> 130, of which waited for: 45 -> 43; matrix products, arithmetic and copies ran while one was open for 33% -> 33% of each run, Pallas kernels for 25% -> 28%
where the time goes in v4:
time: 978 us; the launch traced here: 967 us
  Pallas kernels  276 us (28%)
  waiting for transfers between devices  185 us (19%)
  matrix products  137 us (14%)
  starting transfers between devices  126 us (13%)
  local copies, waits for them, and re-layouts  119 us (12%)
  other arithmetic  106 us (11%)
  between operations  14.9 us (2%)
    ppermute x99, waiting for transfers between devices, swap(): return lax.ppermute(value, WORLD, [(d, d ^ bit) for d in range(self.count)])  145 us
    dot_general x17, matrix products, dot(): return jnp.einsum(spec, left, right, preferred_element_type=wide)  125 us
    pallas_call x6, Pallas kernels, polynomial(): pl.pallas_call(functools.partial(polynomial_body, scaled=scaled), grid=(c...  116 us
    pallas_call x6, Pallas kernels, half_gram(): pl.pallas_call(functools.partial(gram_body, near_count=len(near), far_cou...  81.6 us
    ppermute x99, starting transfers between devices, swap(): return lax.ppermute(value, WORLD, [(d, d ^ bit) for d in range(self.count)])  74.4 us
    cond x136, local copies, waits for them, and re-layouts  47.6 us
    ppermute x19, starting transfers between devices, turn(): return lax.ppermute(value, WORLD, pairs)  31.3 us
    pallas_call x2, Pallas kernels, over_images(): pl.pallas_call(body, grid=(2, here), in_specs=[block(rows.shape[-1]) for...  21.8 us
  transfers between devices with their start and end apart: 130, of which 43 were waited for; matrix products, arithmetic and copies ran while one was open for 33% of the time, Pallas kernels for 28%

profile of v4, /device:TPU:0, one launch (start us, length us, event | category | flops | bytes accessed | tf_op | source)
XLA Modules:
  0.0 967.3 jit_solution(13739268531749801727)
XLA Ops:
  28.1 85.7 %conditional.9 = (bf16[32,2048]{1,0:T(8,128)(2,1)}, f32[2,4,6,2048]{3,2,1,0:T(8,128)}, bf16[1024,2048]{1,0:T(8,128)(2,1)}, bf16[1024,2048]{1,0:T(8,128)(2,1)}, b...) conditional(s32[]{:T(128)} %bitcast.159, () %tuple.144, ...), branch_computations={%region_0.1_spmd, %region_1.2_spmd} | conditional | flops 50638848 | bytes 51841244 | solution.py:51
  55.6 16.3 %all-to-all-done.1 = f32[32,1,3072]{2,1,0:T(1,128)S(1)} async-done(((f32[32,1,3072]{2,1,0:T(1,128)}), f32[32,1,3072]{2,1,0:T(1,128)S(1)}, u32[]{:S(2)}, u32[]{:S(2)}) %all-to-all-start.1) | async-done | bytes 393248 | tf_op jit(solution)/shard_map/cond/branch_1_fun/all_to_all | solution.py:783
  114.5 46.2 %conditional.10 = (bf16[768,2048]{1,0:T(8,128)(2,1)S(1)}, bf16[256,2048]{1,0:T(8,128)(2,1)}, bf16[2,2,2,4,64,768]{5,4,3,2,1,0:T(8,128)(2,1)}, bf16[2048,256]{1,0...) conditional(s32[]{:T(128)} %bitcast.159, () %tuple.148, ...), branch_computations={%region_2.3_spmd, %region_3.4_spmd} | conditional | flops 6452412416 | bytes 139461344 | solution.py:51
  162.4 101.7 %conditional.11 = (f32[4,64,2048]{2,1,0:T(8,128)S(1)}, f32[4,64,2048]{2,1,0:T(8,128)}, f32[4,64,2048]{2,1,0:T(8,128)}, f32[4,64,1]{1,0,2:T(4,128)S(1)}, bf16[102...) conditional(s32[]{:T(128)} %bitcast.159, () %tuple.147, ...), branch_computations={%region_4.5_spmd, %region_5.8_spmd} | conditional | flops 2178949376 | bytes 178498176 | solution.py:51
  286.1 14.6 %fusion.87 = bf16[1024,2048]{1,0:T(8,128)(2,1)} fusion(bf16[1024,2048]{1,0:T(8,128)(2,1)} %get-tuple-element.786, bf16[1024,2048]{1,0:T(8,128)(2,1)} %get-tuple-element.784, bf16[1024,1024]{1,0:T(8,128)(2,1)} %get-tuple-element.783, bf16[1024,1024]{1,0:T(8,128)(2,1)} %get-tuple-element.782), kind=kOutput, calls=%fused_computation.250 | convolution fusion | flops 8617197568 | bytes 16777216 | tf_op jit(solution)/shard_map/tj,tk->jk/dot_general | solution.py:33
  300.7 65.8 %conditional.12 = (bf16[2,128,2048]{2,1,0:T(8,128)(2,1)}, bf16[2,128,2048]{2,1,0:T(8,128)(2,1)}, bf16[2,128,2048]{2,1,0:T(8,128)(2,1)}, bf16[2,128,2048]{2,1,0:T...) conditional(s32[]{:T(128)} %bitcast.159, () %tuple.146, ...), branch_computations={%region_8.9_spmd, %region_9.10_spmd} | conditional | flops 25824329728 | bytes 201326912 | solution.py:51
  341.1 13.1 %fusion.33 = bf16[1024,2048]{1,0:T(8,128)(2,1)} fusion(bf16[1024,2048]{1,0:T(8,128)(2,1)} %get-tuple-element.364, bf16[1024,2048]{1,0:T(8,128)(2,1)} %get-tuple-element.363, bf16[1024,1024]{1,0:T(8,128)(2,1)S(1)} %copy-done.71, bf16[1024,1024]{1,0:T(8,128)(2,1)S(1)} %fusion.23), kind=kOutput, calls=%fused_computation.92 | convolution fusion | flops 8617197568 | bytes 16777216 | tf_op jit(solution)/shard_map/cond/branch_1_fun/tj,tk->jk/dot_general | solution.py:33
  376.7 88.6 %conditional.13 = (bf16[4,2048]{1,0:T(4,128)(2,1)S(1)}, bf16[4,2048]{1,0:T(4,128)(2,1)}, f32[4,64,2048]{2,1,0:T(8,128)}, bf16[4,2048]{1,0:T(4,128)(2,1)}, bf16[2...) conditional(s32[]{:T(128)} %bitcast.159, () %tuple.158, ...), branch_computations={%region_12.13_spmd, %region_13.19_spmd} | conditional | flops 2166358016 | bytes 116057624 | solution.py:51
  474.7 48.9 %conditional.14 = (bf16[1024,2048]{1,0:T(8,128)(2,1)}, bf16[32,8,6,64]{3,0,1,2:T(8,128)(2,1)S(1)}, bf16[1024,2048]{1,0:T(8,128)(2,1)}, bf16[1024,2048]{1,0:T(8,128)(2,1)}) conditional(s32[]{:T(128)} %bitcast.159, () %tuple.143, (bf16[1024,2048]{1,0:T(8,128)(2,1)}, bf16[1024,2048]{1,0:T(8,128)(2,1)}, bf16[2048,768]{1,0:T(8,128)(2,1)}, ...), branch_computations={%region_19.20_spmd, %region_20.21_spmd} | conditional | flops 8633073664 | bytes 92520920 | solution.py:51
  523.8 39.5 %conditional.15 = (f32[32,6,64]{2,1,0:T(8,128)}, f32[6,64,2048]{2,1,0:T(8,128)}, bf16[6,64,2048]{2,1,0:T(8,128)(2,1)}, bf16[2,128,2048]{2,1,0:T(8,128)(2,1)S(1)}...) conditional(s32[]{:T(128)} %bitcast.159, () %tuple.142, ...), branch_computations={%region_21.22_spmd, %region_22.24_spmd} | conditional | flops 312922112 | bytes 77267408 | solution.py:51
  572.6 79.5 %conditional.16 = (bf16[1024,2048]{1,0:T(8,128)(2,1)}, f32[32,2048]{1,0:T(8,128)S(1)}, bf16[2,128,2048]{2,1,0:T(8,128)(2,1)}, bf16[2,128,2048]{2,1,0:T(8,128)(2,...) conditional(s32[]{:T(128)} %bitcast.159, () %tuple.141, ...), branch_computations={%region_24.25_spmd, %region_25.26_spmd} | conditional | flops 310509568 | bytes 76857760 | solution.py:51
  585.7 12.8 %collective-permute-done.23.refs_3_ = bf16[256,2048]{1,0:T(8,128)(2,1)S(1)} collective-permute-done((bf16[256,2048]{1,0:T(8,128)(2,1)}, bf16[256,2048]{1,0:T(8,128)(2,1)S(1)}, u32[]{:S(2)}, u32[]{:S(2)}) %collective-permute-start.23) | collective-permute-done | bytes 1048608 | tf_op jit(solution)/shard_map/cond/branch_1_fun/ppermute | solution.py:93
  603.5 13.5 %branch_1_fun.29 = (bf16[1024,2048]{1,0:T(8,128)(2,1)}, bf16[1024,2048]{1,0:T(8,128)(2,1)}) custom-call(s32[1]{0:T(128)} %get-tuple-element.433.core_ref, bf16[256,2048]{1,0:T(8,128)(2,1)} %get-tuple-element.434.refs_0_, bf16[256,2048]{1,0:T(8,128)(2,1)} %get-tuple-element.435.refs_1_, bf16[256,2048]{1,0:T(8,128)(2,1)} %get-tuple-element.436.refs_2_, ...), custom_call_target="tpu_custom_call" | custom-call | flops 1 | bytes 1 | tf_op jit(solution)/shard_map/cond/branch_1_fun/pallas_call | solution.py:562
  626.9 25.2 %branch_1_fun.30 = bf16[1024,2048]{1,0:T(8,128)(2,1)} custom-call(s32[1]{0:T(128)} %get-tuple-element.433.core_ref, bf16[1024,2048]{1,0:T(8,128)(2,1)} %get-tuple-element.450.rows_ref, bf16[1024,2048]{1,0:T(8,128)(2,1)} %get-tuple-element.455.mine_ref, bf16[1024,2048]{1,0:T(8,128)(2,1)} %collective-permute-done.27.other_ref), custom_call_target="tpu_custom_call" | custom-call | flops 1 | bytes 1 | tf_op jit(solution)/shard_map/cond/branch_1_fun/pallas_call | solution.py:665
  652.8 307.3 %conditional.17 = (f32[64,18,2048]{2,0,1:T(8,128)}, bf16[4,64,2048]{2,1,0:T(8,128)(2,1)}, bf16[4,64,2048]{2,1,0:T(8,128)(2,1)}, f32[32,2048]{1,0:T(8,128)}, f32[...) conditional(s32[]{:T(128)} %bitcast.159, () %tuple.140, (bf16[1024,2048]{1,0:T(8,128)(2,1)}, ...), branch_computations={%region_27.28_spmd, %region_28.29_spmd} | conditional | flops 62324876 | bytes 432808448 | solution.py:51
  665.2 13.4 %branch_1_fun.31 = (bf16[1024,2048]{1,0:T(8,128)(2,1)}, bf16[16,2048]{1,0:T(8,128)(2,1)}) custom-call(s32[1]{0:T(128)} %get-tuple-element.469.core_ref, bf16[1024,2048]{1,0:T(8,128)(2,1)} %get-tuple-element.485.refs_0_.rows_ref, bf16[1024,2048]{1,0:T(8,128)(2,1)} %collective-permute-done.30.refs_1_), custom_call_target="tpu_custom_call" | custom-call | flops 1 | bytes 1 | tf_op jit(solution)/shard_map/cond/branch_1_fun/pallas_call | solution.py:562
  692.9 15.5 %branch_1_fun.32 = (bf16[256,2048]{1,0:T(8,128)(2,1)}, bf16[256,2048]{1,0:T(8,128)(2,1)}) custom-call(s32[1]{0:T(128)} %get-tuple-element.469.core_ref, bf16[1024,2048]{1,0:T(8,128)(2,1)} %get-tuple-element.485.refs_0_.rows_ref, bf16[1024,2048]{1,0:T(8,128)(2,1)} %get-tuple-element.491.mine_ref, bf16[1024,2048]{1,0:T(8,128)(2,1)} %collective-permute-done.36.other_ref), custom_call_target="tpu_custom_call" | custom-call | flops 1 | bytes 1 | tf_op jit(solution)/shard_map/cond/branch_1_fun/pallas_call | solution.py:665
  717.3 13.7 %branch_1_fun.33 = (bf16[1024,2048]{1,0:T(8,128)(2,1)}, bf16[1024,2048]{1,0:T(8,128)(2,1)}) custom-call(s32[1]{0:T(128)} %get-tuple-element.469.core_ref, bf16[256,2048]{1,0:T(8,128)(2,1)} %bitcast.389, bf16[256,2048]{1,0:T(8,128)(2,1)} %collective-permute-done.33.refs_1_, bf16[256,2048]{1,0:T(8,128)(2,1)} %collective-permute-done.34.refs_2_, ...), custom_call_target="tpu_custom_call" | custom-call | flops 1 | bytes 1 | tf_op jit(solution)/shard_map/cond/branch_1_fun/pallas_call | solution.py:562
  746.5 25.2 %branch_1_fun.34.refs_0_.rows_ref = bf16[1024,2048]{1,0:T(8,128)(2,1)} custom-call(s32[1]{0:T(128)} %get-tuple-element.469.core_ref, bf16[1024,2048]{1,0:T(8,128)(2,1)} %get-tuple-element.514.rows_ref, bf16[1024,2048]{1,0:T(8,128)(2,1)} %get-tuple-element.519.mine_ref, bf16[1024,2048]{1,0:T(8,128)(2,1)} %collective-permute-done.47.other_ref), custom_call_target="tpu_custom_call" | custom-call | flops 1 | bytes 1 | tf_op jit(solution)/shard_map/cond/branch_1_fun/pallas_call | solution.py:665
  790.2 13.3 %branch_1_fun.35 = (bf16[1024,2048]{1,0:T(8,128)(2,1)}, bf16[16,2048]{1,0:T(8,128)(2,1)}) custom-call(s32[1]{0:T(128)} %get-tuple-element.469.core_ref, bf16[1024,2048]{1,0:T(8,128)(2,1)} %branch_1_fun.34.refs_0_.rows_ref, bf16[1024,2048]{1,0:T(8,128)(2,1)} %collective-permute-done.53.refs_1_), custom_call_target="tpu_custom_call" | custom-call | flops 1 | bytes 1 | tf_op jit(solution)/shard_map/cond/branch_1_fun/pallas_call | solution.py:562
  810.7 14.3 %branch_1_fun.36 = (bf16[1024,2048]{1,0:T(8,128)(2,1)}, bf16[1024,2048]{1,0:T(8,128)(2,1)}) custom-call(s32[1]{0:T(128)} %get-tuple-element.469.core_ref, bf16[128,2048]{1,0:T(8,128)(2,1)} %pad_maximum_fusion.5.refs_0_, bf16[128,2048]{1,0:T(8,128)(2,1)} %pad_maximum_fusion.6.refs_1_, bf16[128,2048]{1,0:T(8,128)(2,1)} %collective-permute-done.48.refs_2_, ...), custom_call_target="tpu_custom_call" | custom-call | flops 1 | bytes 1 | tf_op jit(solution)/shard_map/cond/branch_1_fun/pallas_call | solution.py:562
  830.2 15.5 %branch_1_fun.37 = (bf16[256,2048]{1,0:T(8,128)(2,1)}, bf16[256,2048]{1,0:T(8,128)(2,1)}) custom-call(s32[1]{0:T(128)} %get-tuple-element.469.core_ref, bf16[1024,2048]{1,0:T(8,128)(2,1)} %branch_1_fun.34.refs_0_.rows_ref, bf16[1024,2048]{1,0:T(8,128)(2,1)} %get-tuple-element.557.mine_ref, bf16[1024,2048]{1,0:T(8,128)(2,1)} %collective-permute-done.64.other_ref), custom_call_target="tpu_custom_call" | custom-call | flops 1 | bytes 1 | tf_op jit(solution)/shard_map/cond/branch_1_fun/pallas_call | solution.py:665
  853.1 25.3 %branch_1_fun.38.refs_0_.rows_ref = bf16[1024,2048]{1,0:T(8,128)(2,1)} custom-call(s32[1]{0:T(128)} %get-tuple-element.469.core_ref, bf16[1024,2048]{1,0:T(8,128)(2,1)} %get-tuple-element.555.rows_ref, bf16[1024,2048]{1,0:T(8,128)(2,1)} %get-tuple-element.566.mine_ref, bf16[1024,2048]{1,0:T(8,128)(2,1)} %collective-permute-done.68.other_ref), custom_call_target="tpu_custom_call" | custom-call | flops 1 | bytes 1 | tf_op jit(solution)/shard_map/cond/branch_1_fun/pallas_call | solution.py:665
  891.2 13.5 %branch_1_fun.39 = (bf16[1024,2048]{1,0:T(8,128)(2,1)}, bf16[16,2048]{1,0:T(8,128)(2,1)}) custom-call(s32[1]{0:T(128)} %get-tuple-element.469.core_ref, bf16[1024,2048]{1,0:T(8,128)(2,1)} %branch_1_fun.38.refs_0_.rows_ref, bf16[1024,2048]{1,0:T(8,128)(2,1)} %collective-permute-done.76.refs_1_), custom_call_target="tpu_custom_call" | custom-call | flops 1 | bytes 1 | tf_op jit(solution)/shard_map/cond/branch_1_fun/pallas_call | solution.py:562
  (596 shorter events, 703.0 us)
Async XLA Ops:
  7.2 106.9 %all-gather.4.cloned.1.call-start = ((), (), s32[]{:S(2)}) async-start(), calls=%async_computation.7 | async-start | bytes 5242880 | tf_op jit(solution)/shard_map/all_gather | solution.py:100
  23.9 240.3 %all-gather.6.cloned.1.call-start = ((), (), s32[]{:S(2)}) async-start(), calls=%async_computation.8 | async-start | bytes 5242880 | tf_op jit(solution)/shard_map/all_gather | solution.py:100
  24.7 261.4 %all-gather.8.cloned.1.call-start = ((), (), s32[]{:S(2)}) async-start(), calls=%async_computation.9 | async-start | bytes 5242880 | tf_op jit(solution)/shard_map/all_gather | solution.py:100
  25.4 351.3 %reduce-scatter.6.cloned.1.call-start = ((), (), s32[]{:S(2)}) async-start(), calls=%async_computation.11 | async-start | bytes 5242880 | tf_op jit(solution)/shard_map/reduce_scatter | solution.py:103
  44.0 27.9 %all-to-all-start.1 = ((f32[32,1,3072]{2,1,0:T(1,128)}), f32[32,1,3072]{2,1,0:T(1,128)S(1)}, u32[]{:S(2)}, u32[]{:S(2)}) async-start(f32[32,1,3072]{2,1,0:T(1,128)} %reshape.454), calls=%async_computation.1 | async-start | bytes 786432 | tf_op jit(solution)/shard_map/cond/branch_1_fun/all_to_all | solution.py:783
  53.7 27.7 %collective-permute-start.109 = (bf16[128,2048]{1,0:T(8,128)(2,1)}, bf16[128,2048]{1,0:T(8,128)(2,1)S(1)}, u32[]{:S(2)}, u32[]{:S(2)}) collective-permute-start(bf16[128,2048]{1,0:T(8,128)(2,1)} %get-tuple-element.1018), channel_id=1, source_target_pairs={{0,4},{1,5},{2,6},{3,7},{4,0},{5,1},{6,2},{7,3},{8,12},{9,13},{10,... | collective-permute-start | bytes 1572872 | tf_op jit(solution)/shard_map/cond/branch_1_fun/ppermute | solution.py:93
  185.1 78.5 %collective-permute-start.93 = (bf16[1024,2048]{1,0:T(8,128)(2,1)}, bf16[1024,2048]{1,0:T(8,128)(2,1)}, u32[]{:S(2)}, u32[]{:S(2)}) collective-permute-start(bf16[1024,2048]{1,0:T(8,128)(2,1)} %constant_dynamic-update-slice_fusion.7), channel_id=1, source_target_pairs={{0,1},{1,0},{2,3},{3,2},{4,5},{5,4},{6,7},{7,6},{8,9},{9,8},{10,11... | collective-permute-start | bytes 12582920 | tf_op jit(solution)/shard_map/cond/branch_1_fun/ppermute | solution.py:93
  206.7 57.0 %collective-permute-start.94 = (bf16[1024,2048]{1,0:T(8,128)(2,1)}, bf16[1024,2048]{1,0:T(8,128)(2,1)}, u32[]{:S(2)}, u32[]{:S(2)}) collective-permute-start(bf16[1024,2048]{1,0:T(8,128)(2,1)} %fusion.5), channel_id=1, source_target_pairs={{0,1},{1,0},{2,3},{3,2},{4,5},{5,4},{6,7},{7,6},{8,9},{9,8},{10,11... | collective-permute-start | bytes 12582920 | tf_op jit(solution)/shard_map/cond/branch_1_fun/ppermute | solution.py:93
  300.7 164.7 %reduce-scatter.4.cloned.1.call-start = ((), (), s32[]{:S(2)}) async-start(), calls=%async_computation.10 | async-start | bytes 5242880 | tf_op jit(solution)/shard_map/reduce_scatter | solution.py:103
  470.0 53.7 %all-to-all-start.2 = ((bf16[4,128,2048]{2,1,0:T(8,128)(2,1)}), bf16[4,128,2048]{2,1,0:T(8,128)(2,1)}, u32[]{:S(2)}, u32[]{:S(2)}) async-start(bf16[4,128,2048]{2,1,0:T(8,128)(2,1)} %bitcast.384), calls=%async_computation.4 | async-start | bytes 4194304 | tf_op jit(solution)/shard_map/all_to_all | solution.py:108
  474.6 178.1 %reduce-scatter.8.cloned.1.call-start = ((), (), s32[]{:S(2)}) async-start(), calls=%async_computation.12 | async-start | bytes 5242880 | tf_op jit(solution)/shard_map/reduce_scatter | solution.py:103
  474.9 38.5 %collective-permute-start.105 = (bf16[1024,2048]{1,0:T(8,128)(2,1)}, bf16[1024,2048]{1,0:T(8,128)(2,1)}, u32[]{:S(2)}, u32[]{:S(2)}) collective-permute-start(bf16[1024,2048]{1,0:T(8,128)(2,1)} %get-tuple-element.402), channel_id=1, source_target_pairs={{0,1},{1,0},{2,3},{3,2},{4,5},{5,4},{6,7},{7,6},{8,9},{9,8},{10,11... | collective-permute-start | bytes 12582920 | tf_op jit(solution)/shard_map/cond/branch_1_fun/ppermute | solution.py:93
  524.1 32.0 %collective-permute-start.2 = (bf16[1024,2048]{1,0:T(8,128)(2,1)}, bf16[1024,2048]{1,0:T(8,128)(2,1)}, u32[]{:S(2)}, u32[]{:S(2)}) collective-permute-start(bf16[1024,2048]{1,0:T(8,128)(2,1)} %get-tuple-element.413), channel_id=1, source_target_pairs={{0,1},{1,0},{2,3},{3,2},{4,5},{5,4},{6,7},{7,6},{8,9},{9,8},{10,11... | collective-permute-start | bytes 12582920 | tf_op jit(solution)/shard_map/cond/branch_1_fun/ppermute | solution.py:93
  526.9 29.1 %collective-permute-start.1 = (bf16[256,2048]{1,0:T(8,128)(2,1)}, bf16[256,2048]{1,0:T(8,128)(2,1)}, u32[]{:S(2)}, u32[]{:S(2)}) collective-permute-start(bf16[256,2048]{1,0:T(8,128)(2,1)} %bitcast.84), channel_id=1, source_target_pairs={{0,4},{1,5},{2,6},{3,7},{4,0},{5,1},{6,2},{7,3},{8,12},{9,13},{10,... | collective-permute-start | bytes 3145736 | tf_op jit(solution)/shard_map/cond/branch_1_fun/ppermute | solution.py:93
  528.3 27.7 %collective-permute-start = (bf16[256,2048]{1,0:T(8,128)(2,1)S(1)}, bf16[256,2048]{1,0:T(8,128)(2,1)}, u32[]{:S(2)}, u32[]{:S(2)}) collective-permute-start(bf16[256,2048]{1,0:T(8,128)(2,1)S(1)} %bitcast.409), channel_id=1, source_target_pairs={{0,2},{1,3},{2,0},{3,1},{4,6},{5,7},{6,4},{7,5},{8,10},{9,11},{10,... | collective-permute-start | bytes 3145736 | tf_op jit(solution)/shard_map/cond/branch_1_fun/ppermute | solution.py:93
  566.8 86.0 %all-to-all-start.3 = ((bf16[4,128,2048]{2,1,0:T(8,128)(2,1)}), bf16[4,128,2048]{2,1,0:T(8,128)(2,1)}, u32[]{:S(2)}, u32[]{:S(2)}) async-start(bf16[4,128,2048]{2,1,0:T(8,128)(2,1)} %bitcast.385), calls=%async_computation.5 | async-start | bytes 4194304 | tf_op jit(solution)/shard_map/all_to_all | solution.py:108
  735.6 36.1 %collective-permute-start.48 = (bf16[128,2048]{1,0:T(8,128)(2,1)}, bf16[128,2048]{1,0:T(8,128)(2,1)}, u32[]{:S(2)}, u32[]{:S(2)}) collective-permute-start(bf16[128,2048]{1,0:T(8,128)(2,1)} %pad_maximum_fusion.5.refs_0_), channel_id=1, source_target_pairs={{0,2},{1,3},{2,0},{3,1},{4,6},{5,7},{6,4},{7,5},{8,10},{9,11},{10,... | collective-permute-start | bytes 1572872 | tf_op jit(solution)/shard_map/cond/branch_1_fun/ppermute | solution.py:93
  736.7 35.0 %collective-permute-start.49 = (bf16[128,2048]{1,0:T(8,128)(2,1)}, bf16[128,2048]{1,0:T(8,128)(2,1)}, u32[]{:S(2)}, u32[]{:S(2)}) collective-permute-start(bf16[128,2048]{1,0:T(8,128)(2,1)} %pad_maximum_fusion.5.refs_0_), channel_id=1, source_target_pairs={{0,4},{1,5},{2,6},{3,7},{4,0},{5,1},{6,2},{7,3},{8,12},{9,13},{10,... | collective-permute-start | bytes 1572872 | tf_op jit(solution)/shard_map/cond/branch_1_fun/ppermute | solution.py:93
  738.1 33.7 %collective-permute-start.50 = (bf16[128,2048]{1,0:T(8,128)(2,1)}, bf16[128,2048]{1,0:T(8,128)(2,1)}, u32[]{:S(2)}, u32[]{:S(2)}) collective-permute-start(bf16[128,2048]{1,0:T(8,128)(2,1)} %pad_maximum_fusion.6.refs_1_), channel_id=1, source_target_pairs={{0,2},{1,3},{2,0},{3,1},{4,6},{5,7},{6,4},{7,5},{8,10},{9,11},{10,... | collective-permute-start | bytes 1572872 | tf_op jit(solution)/shard_map/cond/branch_1_fun/ppermute | solution.py:93
  743.0 28.7 %collective-permute-start.51 = (bf16[2,64,2048]{2,1,0:T(8,128)(2,1)}, bf16[2,64,2048]{2,1,0:T(8,128)(2,1)}, u32[]{:S(2)}, u32[]{:S(2)}) collective-permute-start(bf16[2,64,2048]{2,1,0:T(8,128)(2,1)} %get-tuple-element.521), channel_id=1, source_target_pairs={{0,24},{1,25},{2,26},{3,27},{4,28},{5,29},{6,30},{7,31},{8,0},{9,1... | collective-permute-start | bytes 1572872 | tf_op jit(solution)/shard_map/cond/branch_1_fun/ppermute | solution.py:97
  776.2 28.1 %collective-permute-start.56 = (bf16[128,2048]{1,0:T(8,128)(2,1)}, bf16[128,2048]{1,0:T(8,128)(2,1)S(1)}, u32[]{:S(2)}, u32[]{:S(2)}) collective-permute-start(bf16[128,2048]{1,0:T(8,128)(2,1)} %collective-permute-done.42.refs_5_), channel_id=1, source_target_pairs={{0,1},{1,0},{2,3},{3,2},{4,5},{5,4},{6,7},{7,6},{8,9},{9,8},{10,11... | collective-permute-start | bytes 1572872 | tf_op jit(solution)/shard_map/cond/branch_1_fun/ppermute | solution.py:93
  776.5 28.3 %collective-permute-start.58 = (bf16[128,2048]{1,0:T(8,128)(2,1)}, bf16[128,2048]{1,0:T(8,128)(2,1)S(1)}, u32[]{:S(2)}, u32[]{:S(2)}) collective-permute-start(bf16[128,2048]{1,0:T(8,128)(2,1)} %collective-permute-done.42.refs_5_), channel_id=1, source_target_pairs={{0,2},{1,3},{2,0},{3,1},{4,6},{5,7},{6,4},{7,5},{8,10},{9,11},{10,... | collective-permute-start | bytes 1572872 | tf_op jit(solution)/shard_map/cond/branch_1_fun/ppermute | solution.py:93
  846.7 31.8 %collective-permute-start.72 = (bf16[256,2048]{1,0:T(8,128)(2,1)}, bf16[256,2048]{1,0:T(8,128)(2,1)S(1)}, u32[]{:S(2)}, u32[]{:S(2)}) collective-permute-start(bf16[256,2048]{1,0:T(8,128)(2,1)} %get-tuple-element.568), channel_id=1, source_target_pairs={{0,2},{1,3},{2,0},{3,1},{4,6},{5,7},{6,4},{7,5},{8,10},{9,11},{10,... | collective-permute-start | bytes 3145736 | tf_op jit(solution)/shard_map/cond/branch_1_fun/ppermute | solution.py:93
  849.9 28.6 %collective-permute-start.73 = (bf16[64,2048]{1,0:T(8,128)(2,1)}, bf16[64,2048]{1,0:T(8,128)(2,1)}, u32[]{:S(2)}, u32[]{:S(2)}) collective-permute-start(bf16[64,2048]{1,0:T(8,128)(2,1)} %get-tuple-element.1082), channel_id=1, source_target_pairs={{0,24},{1,25},{2,26},{3,27},{4,28},{5,29},{6,30},{7,31},{8,0},{9,1... | collective-permute-start | bytes 786440 | tf_op jit(solution)/shard_map/cond/branch_1_fun/ppermute | solution.py:97
  (179 other events, 2919.4 us)
Sparse Core Ops, SparseCore 0:
  24.0 89.9 all-gather.3
  116.2 79.2 all-gather.5
  197.6 79.2 all-gather.7
  300.8 75.8 reduce-scatter.5
  378.9 77.2 reduce-scatter.3
  523.9 107.9 reduce-scatter.7

commit v5 on v4

--- a/solution.py
+++ b/solution.py
@@ -1005,17 +1005,18 @@
 
     step_size = matrix_rate * 0.2 * math.sqrt(width)
 
-    def steps_one(d, d_far, grad_mod_all, mlp_hops, first_near, first_too):
-        first_split = fabric.settle_pieces(add(first_near, first_too).astype(low))
+    first_split = fabric.settle_pieces(
+        add(after(first_near, ada_momentum), first_too).astype(low)
+    )
+    d_xy, first_split = hold(fabric.swap(d[1], ALONG_Y), first_split)
+
+    def steps_one(d, d_xy, d_far, grad_mod_all, mlp_hops):
         grad_active = jnp.einsum(
             "nur,ruk->nk", grad_mod_all, ada_weight.astype(wide), precision=highest
         )
         grad_active_core = fabric.swap(grad_active, CORE)
-        d_xy, first_split, grad_active_core = hold(
-            fabric.swap(d[1], ALONG_Y), first_split, grad_active_core
-        )
+        d_far_xy, grad_active_core = hold(fabric.swap(d_xy, CORE), grad_active_core)
         grad_active = grad_active + grad_active_core
-        d_far_xy, grad_active = hold(fabric.swap(d_xy, CORE), grad_active)
         d, d_far = d + [d_xy], d_far + [d_far_xy]
         grad_active_x = fabric.swap(grad_active, ALONG_X)
         d_half, d = half_gram(core, d, d_far)
@@ -1027,11 +1028,11 @@
         mlp_came = fabric.settle_hop(*mlp_hops)
         d = polynomial(core, d, d_half, d_other, True)
         d, mlp_came = hold(d, mlp_came)
-        return d, grad_active, mlp_came, first_split
+        return d, grad_active, mlp_came
 
     mlp_kept = mlp_split[0]
-    d, grad_active, mlp_came, first_split = fence(
-        valid, steps_one, d, d_far, grad_mod_all, mlp_split[1], first_near, first_too
+    d, grad_active, mlp_came = fence(
+        valid, steps_one, d, d_xy, d_far, grad_mod_all, mlp_split[1]
     )
     mlp_sum = (*mlp_kept, *mlp_came)
     d, ada_rows, attention_sum = hold(d, ada_rows, attention_sum)

time: 978 us -> 973 us (level)
    ppermute x99, waiting for transfers between devices: 145 us -> 135 us  [swap(): return lax.ppermute(value, WORLD, [(d, d ^ bit) for d in range(self.count)])]
    cond x136 -> x140, local copies, waits for them, and re-layouts: 47.6 us -> 44.9 us
  transfers between devices with their start and end apart: 130 -> 130, of which waited for: 43 -> 45; matrix products, arithmetic and copies ran while one was open for 33% -> 34% of each run, Pallas kernels for 28% -> 28%
where the time goes in v5:
time: 973 us; the launch traced here: 963 us
  Pallas kernels  276 us (28%)
  waiting for transfers between devices  176 us (18%)
  matrix products  136 us (14%)
  starting transfers between devices  124 us (13%)
  local copies, waits for them, and re-layouts  119 us (12%)
  other arithmetic  113 us (12%)
  between operations  14.8 us (2%)
    ppermute x99, waiting for transfers between devices, swap(): return lax.ppermute(value, WORLD, [(d, d ^ bit) for d in range(self.count)])  135 us
    dot_general x17, matrix products, dot(): return jnp.einsum(spec, left, right, preferred_element_type=wide)  125 us
    pallas_call x6, Pallas kernels, polynomial(): pl.pallas_call(functools.partial(polynomial_body, scaled=scaled), grid=(c...  116 us
    pallas_call x6, Pallas kernels, half_gram(): pl.pallas_call(functools.partial(gram_body, near_count=len(near), far_cou...  81.3 us
    ppermute x99, starting transfers between devices, swap(): return lax.ppermute(value, WORLD, [(d, d ^ bit) for d in range(self.count)])  74.7 us
    cond x140, local copies, waits for them, and re-layouts  44.9 us
    ppermute x19, starting transfers between devices, turn(): return lax.ppermute(value, WORLD, pairs)  28.9 us
    pallas_call x2, Pallas kernels, over_images(): pl.pallas_call(body, grid=(2, here), in_specs=[block(rows.shape[-1]) for...  21.8 us
  transfers between devices with their start and end apart: 130, of which 45 were waited for; matrix products, arithmetic and copies ran while one was open for 34% of the time, Pallas kernels for 28%

profile of v5, /device:TPU:0, one launch (start us, length us, event | category | flops | bytes accessed | tf_op | source)
XLA Modules:
  0.0 962.6 jit_solution(1022170059086027969)
XLA Ops:
  28.1 85.7 %conditional.9 = (bf16[32,2048]{1,0:T(8,128)(2,1)}, f32[2,4,6,2048]{3,2,1,0:T(8,128)}, bf16[1024,2048]{1,0:T(8,128)(2,1)}, bf16[1024,2048]{1,0:T(8,128)(2,1)}, b...) conditional(s32[]{:T(128)} %bitcast.150, () %tuple.147, ...), branch_computations={%region_0.1_spmd, %region_1.2_spmd} | conditional | flops 50638848 | bytes 51841244 | solution.py:51
  55.6 16.3 %all-to-all-done.1 = f32[32,1,3072]{2,1,0:T(1,128)S(1)} async-done(((f32[32,1,3072]{2,1,0:T(1,128)}), f32[32,1,3072]{2,1,0:T(1,128)S(1)}, u32[]{:S(2)}, u32[]{:S(2)}) %all-to-all-start.1) | async-done | bytes 393248 | tf_op jit(solution)/shard_map/cond/branch_1_fun/all_to_all | solution.py:783
  114.4 46.2 %conditional.10 = (bf16[768,2048]{1,0:T(8,128)(2,1)S(1)}, bf16[256,2048]{1,0:T(8,128)(2,1)}, bf16[2,2,2,4,64,768]{5,4,3,2,1,0:T(8,128)(2,1)}, bf16[2048,256]{1,0...) conditional(s32[]{:T(128)} %bitcast.150, () %tuple.151, ...), branch_computations={%region_2.3_spmd, %region_3.4_spmd} | conditional | flops 6452412416 | bytes 139461344 | solution.py:51
  162.3 101.8 %conditional.11 = (f32[4,64,2048]{2,1,0:T(8,128)S(1)}, f32[4,64,2048]{2,1,0:T(8,128)}, f32[4,64,2048]{2,1,0:T(8,128)}, f32[4,64,1]{1,0,2:T(4,128)S(1)}, bf16[102...) conditional(s32[]{:T(128)} %bitcast.150, () %tuple.150, ...), branch_computations={%region_4.5_spmd, %region_5.8_spmd} | conditional | flops 2178949376 | bytes 178498176 | solution.py:51
  286.1 14.5 %fusion.87 = bf16[1024,2048]{1,0:T(8,128)(2,1)} fusion(bf16[1024,2048]{1,0:T(8,128)(2,1)} %get-tuple-element.778, bf16[1024,2048]{1,0:T(8,128)(2,1)} %get-tuple-element.776, bf16[1024,1024]{1,0:T(8,128)(2,1)} %get-tuple-element.775, bf16[1024,1024]{1,0:T(8,128)(2,1)} %get-tuple-element.774), kind=kOutput, calls=%fused_computation.242 | convolution fusion | flops 8617197568 | bytes 16777216 | tf_op jit(solution)/shard_map/tj,tk->jk/dot_general | solution.py:33
  300.7 65.8 %conditional.12 = (bf16[2,128,2048]{2,1,0:T(8,128)(2,1)}, bf16[2,128,2048]{2,1,0:T(8,128)(2,1)}, bf16[2,128,2048]{2,1,0:T(8,128)(2,1)}, bf16[2,128,2048]{2,1,0:T...) conditional(s32[]{:T(128)} %bitcast.150, () %tuple.149, ...), branch_computations={%region_8.9_spmd, %region_9.10_spmd} | conditional | flops 25824329728 | bytes 201326912 | solution.py:51
  341.1 13.1 %fusion.33 = bf16[1024,2048]{1,0:T(8,128)(2,1)} fusion(bf16[1024,2048]{1,0:T(8,128)(2,1)} %get-tuple-element.363, bf16[1024,2048]{1,0:T(8,128)(2,1)} %get-tuple-element.362, bf16[1024,1024]{1,0:T(8,128)(2,1)S(1)} %copy-done.73, bf16[1024,1024]{1,0:T(8,128)(2,1)S(1)} %fusion.23), kind=kOutput, calls=%fused_computation.92 | convolution fusion | flops 8617197568 | bytes 16777216 | tf_op jit(solution)/shard_map/cond/branch_1_fun/tj,tk->jk/dot_general | solution.py:33
  376.6 88.6 %conditional.13 = (bf16[4,2048]{1,0:T(4,128)(2,1)S(1)}, bf16[4,2048]{1,0:T(4,128)(2,1)}, f32[4,64,2048]{2,1,0:T(8,128)}, bf16[4,2048]{1,0:T(4,128)(2,1)}, bf16[2...) conditional(s32[]{:T(128)} %bitcast.150, () %tuple.161, ...), branch_computations={%region_12.13_spmd, %region_13.19_spmd} | conditional | flops 2166358016 | bytes 116057624 | solution.py:51
  452.9 12.3 %branch_1_fun.26 = bf16[2,2,2,4,64,768]{5,4,3,2,1,0:T(8,128)(2,1)} custom-call(bf16[2,2,2,4,64,768]{5,4,3,2,1,0:T(8,128)(2,1)} %get-tuple-element.389.projected_ref, bf16[2,2,2,4,64,256]{5,4,3,2,1,0:T(8,128)(2,1)S(1)} %bitcast.361), custom_call_target="tpu_custom_call" | custom-call | flops 1 | bytes 1 | tf_op jit(solution)/shard_map/cond/branch_1_fun/pallas_call | solution.py:311
  474.6 48.9 %conditional.14 = (bf16[1024,2048]{1,0:T(8,128)(2,1)}, bf16[32,8,6,64]{3,0,1,2:T(8,128)(2,1)S(1)}, bf16[1024,2048]{1,0:T(8,128)(2,1)}, bf16[1024,2048]{1,0:T(8,128)(2,1)}) conditional(s32[]{:T(128)} %bitcast.150, () %tuple.146, (bf16[1024,2048]{1,0:T(8,128)(2,1)}, bf16[1024,2048]{1,0:T(8,128)(2,1)}, bf16[2048,768]{1,0:T(8,128)(2,1)}, ...), branch_computations={%region_19.20_spmd, %region_20.21_spmd} | conditional | flops 8633073664 | bytes 92520920 | solution.py:51
  524.2 45.1 %conditional.15 = (f32[32,6,64]{2,1,0:T(8,128)}, f32[6,64,2048]{2,1,0:T(8,128)S(1)}, bf16[6,64,2048]{2,1,0:T(8,128)(2,1)}, bf16[2,128,2048]{2,1,0:T(8,128)(2,1)}...) conditional(s32[]{:T(128)} %bitcast.150, () %tuple.145, ...), branch_computations={%region_21.22_spmd, %region_22.24_spmd} | conditional | flops 315019264 | bytes 89850320 | solution.py:51
  595.1 53.9 %conditional.16 = (bf16[1024,2048]{1,0:T(8,128)(2,1)}, f32[32,2048]{1,0:T(8,128)S(1)}, bf16[2,128,2048]{2,1,0:T(8,128)(2,1)}, bf16[2,128,2048]{2,1,0:T(8,128)(2,1)}) conditional(s32[]{:T(128)} %bitcast.150, () %tuple.144, (bf16[256,2048]{1,0:T(8,128)(2,1)}, f32[32,6,64]{2,1,0:T(8,128)}, bf16[64,6,2048]{2,0,1:T(8,128)(2,1)S(1)}, s32[1]{0:T(128)}, ...), branch_computations={%region_24.25_spmd, %region_25.26_spmd} | conditional | flops 302120960 | bytes 34914576 | solution.py:51
  600.7 13.5 %branch_1_fun.29 = (bf16[1024,2048]{1,0:T(8,128)(2,1)}, bf16[1024,2048]{1,0:T(8,128)(2,1)}) custom-call(s32[1]{0:T(128)} %get-tuple-element.432.core_ref, bf16[256,2048]{1,0:T(8,128)(2,1)} %get-tuple-element.433.refs_0_, bf16[256,2048]{1,0:T(8,128)(2,1)} %get-tuple-element.434.refs_1_, bf16[256,2048]{1,0:T(8,128)(2,1)} %get-tuple-element.435.refs_2_, ...), custom_call_target="tpu_custom_call" | custom-call | flops 1 | bytes 1 | tf_op jit(solution)/shard_map/cond/branch_1_fun/pallas_call | solution.py:562
  623.8 25.2 %branch_1_fun.30 = bf16[1024,2048]{1,0:T(8,128)(2,1)} custom-call(s32[1]{0:T(128)} %get-tuple-element.432.core_ref, bf16[1024,2048]{1,0:T(8,128)(2,1)} %get-tuple-element.446.rows_ref, bf16[1024,2048]{1,0:T(8,128)(2,1)} %get-tuple-element.451.mine_ref, bf16[1024,2048]{1,0:T(8,128)(2,1)} %collective-permute-done.26.other_ref), custom_call_target="tpu_custom_call" | custom-call | flops 1 | bytes 1 | tf_op jit(solution)/shard_map/cond/branch_1_fun/pallas_call | solution.py:665
  650.5 305.0 %conditional.17 = (f32[64,18,2048]{2,0,1:T(8,128)}, bf16[4,64,2048]{2,1,0:T(8,128)(2,1)}, bf16[4,64,2048]{2,1,0:T(8,128)(2,1)}, f32[32,2048]{1,0:T(8,128)}, f32[...) conditional(s32[]{:T(128)} %bitcast.150, () %tuple.143, (bf16[1024,2048]{1,0:T(8,128)(2,1)}, ...), branch_computations={%region_27.28_spmd, %region_28.29_spmd} | conditional | flops 62324876 | bytes 450634368 | solution.py:51
  663.2 13.3 %branch_1_fun.31 = (bf16[1024,2048]{1,0:T(8,128)(2,1)}, bf16[16,2048]{1,0:T(8,128)(2,1)}) custom-call(s32[1]{0:T(128)} %get-tuple-element.459.core_ref, bf16[1024,2048]{1,0:T(8,128)(2,1)} %get-tuple-element.475.refs_0_.rows_ref, bf16[1024,2048]{1,0:T(8,128)(2,1)} %collective-permute-done.29.refs_1_), custom_call_target="tpu_custom_call" | custom-call | flops 1 | bytes 1 | tf_op jit(solution)/shard_map/cond/branch_1_fun/pallas_call | solution.py:562
  689.8 15.5 %branch_1_fun.32 = (bf16[256,2048]{1,0:T(8,128)(2,1)}, bf16[256,2048]{1,0:T(8,128)(2,1)}) custom-call(s32[1]{0:T(128)} %get-tuple-element.459.core_ref, bf16[1024,2048]{1,0:T(8,128)(2,1)} %get-tuple-element.475.refs_0_.rows_ref, bf16[1024,2048]{1,0:T(8,128)(2,1)} %get-tuple-element.481.mine_ref, bf16[1024,2048]{1,0:T(8,128)(2,1)} %collective-permute-done.35.other_ref), custom_call_target="tpu_custom_call" | custom-call | flops 1 | bytes 1 | tf_op jit(solution)/shard_map/cond/branch_1_fun/pallas_call | solution.py:665
  715.9 13.5 %branch_1_fun.33 = (bf16[1024,2048]{1,0:T(8,128)(2,1)}, bf16[1024,2048]{1,0:T(8,128)(2,1)}) custom-call(s32[1]{0:T(128)} %get-tuple-element.459.core_ref, bf16[256,2048]{1,0:T(8,128)(2,1)} %bitcast.389, bf16[256,2048]{1,0:T(8,128)(2,1)} %collective-permute-done.32.refs_1_, bf16[256,2048]{1,0:T(8,128)(2,1)} %collective-permute-done.33.refs_2_, ...), custom_call_target="tpu_custom_call" | custom-call | flops 1 | bytes 1 | tf_op jit(solution)/shard_map/cond/branch_1_fun/pallas_call | solution.py:562
  743.6 25.4 %branch_1_fun.34.refs_0_.rows_ref = bf16[1024,2048]{1,0:T(8,128)(2,1)} custom-call(s32[1]{0:T(128)} %get-tuple-element.459.core_ref, bf16[1024,2048]{1,0:T(8,128)(2,1)} %get-tuple-element.504.rows_ref, bf16[1024,2048]{1,0:T(8,128)(2,1)} %get-tuple-element.509.mine_ref, bf16[1024,2048]{1,0:T(8,128)(2,1)} %collective-permute-done.46.other_ref), custom_call_target="tpu_custom_call" | custom-call | flops 1 | bytes 1 | tf_op jit(solution)/shard_map/cond/branch_1_fun/pallas_call | solution.py:665
  785.4 13.3 %branch_1_fun.35 = (bf16[1024,2048]{1,0:T(8,128)(2,1)}, bf16[16,2048]{1,0:T(8,128)(2,1)}) custom-call(s32[1]{0:T(128)} %get-tuple-element.459.core_ref, bf16[1024,2048]{1,0:T(8,128)(2,1)} %branch_1_fun.34.refs_0_.rows_ref, bf16[1024,2048]{1,0:T(8,128)(2,1)} %collective-permute-done.52.refs_1_), custom_call_target="tpu_custom_call" | custom-call | flops 1 | bytes 1 | tf_op jit(solution)/shard_map/cond/branch_1_fun/pallas_call | solution.py:562
  807.5 14.3 %branch_1_fun.36 = (bf16[1024,2048]{1,0:T(8,128)(2,1)}, bf16[1024,2048]{1,0:T(8,128)(2,1)}) custom-call(s32[1]{0:T(128)} %get-tuple-element.459.core_ref, bf16[128,2048]{1,0:T(8,128)(2,1)} %pad_maximum_fusion.5.refs_0_, bf16[128,2048]{1,0:T(8,128)(2,1)} %pad_maximum_fusion.6.refs_1_, bf16[128,2048]{1,0:T(8,128)(2,1)} %collective-permute-done.47.refs_2_, ...), custom_call_target="tpu_custom_call" | custom-call | flops 1 | bytes 1 | tf_op jit(solution)/shard_map/cond/branch_1_fun/pallas_call | solution.py:562
  826.2 15.5 %branch_1_fun.37 = (bf16[256,2048]{1,0:T(8,128)(2,1)}, bf16[256,2048]{1,0:T(8,128)(2,1)}) custom-call(s32[1]{0:T(128)} %get-tuple-element.459.core_ref, bf16[1024,2048]{1,0:T(8,128)(2,1)} %branch_1_fun.34.refs_0_.rows_ref, bf16[1024,2048]{1,0:T(8,128)(2,1)} %get-tuple-element.547.mine_ref, bf16[1024,2048]{1,0:T(8,128)(2,1)} %collective-permute-done.63.other_ref), custom_call_target="tpu_custom_call" | custom-call | flops 1 | bytes 1 | tf_op jit(solution)/shard_map/cond/branch_1_fun/pallas_call | solution.py:665
  848.7 25.5 %branch_1_fun.38.refs_0_.rows_ref = bf16[1024,2048]{1,0:T(8,128)(2,1)} custom-call(s32[1]{0:T(128)} %get-tuple-element.459.core_ref, bf16[1024,2048]{1,0:T(8,128)(2,1)} %get-tuple-element.545.rows_ref, bf16[1024,2048]{1,0:T(8,128)(2,1)} %get-tuple-element.556.mine_ref, bf16[1024,2048]{1,0:T(8,128)(2,1)} %collective-permute-done.67.other_ref), custom_call_target="tpu_custom_call" | custom-call | flops 1 | bytes 1 | tf_op jit(solution)/shard_map/cond/branch_1_fun/pallas_call | solution.py:665
  887.2 13.5 %branch_1_fun.39 = (bf16[1024,2048]{1,0:T(8,128)(2,1)}, bf16[16,2048]{1,0:T(8,128)(2,1)}) custom-call(s32[1]{0:T(128)} %get-tuple-element.459.core_ref, bf16[1024,2048]{1,0:T(8,128)(2,1)} %branch_1_fun.38.refs_0_.rows_ref, bf16[1024,2048]{1,0:T(8,128)(2,1)} %collective-permute-done.75.refs_1_), custom_call_target="tpu_custom_call" | custom-call | flops 1 | bytes 1 | tf_op jit(solution)/shard_map/cond/branch_1_fun/pallas_call | solution.py:562
  (601 shorter events, 698.8 us)
Async XLA Ops:
  7.2 106.9 %all-gather.4.cloned.1.call-start = ((), (), s32[]{:S(2)}) async-start(), calls=%async_computation.7 | async-start | bytes 5242880 | tf_op jit(solution)/shard_map/all_gather | solution.py:100
  23.9 240.3 %all-gather.6.cloned.1.call-start = ((), (), s32[]{:S(2)}) async-start(), calls=%async_computation.8 | async-start | bytes 5242880 | tf_op jit(solution)/shard_map/all_gather | solution.py:100
  24.7 261.4 %all-gather.8.cloned.1.call-start = ((), (), s32[]{:S(2)}) async-start(), calls=%async_computation.9 | async-start | bytes 5242880 | tf_op jit(solution)/shard_map/all_gather | solution.py:100
  25.4 351.2 %reduce-scatter.6.cloned.1.call-start = ((), (), s32[]{:S(2)}) async-start(), calls=%async_computation.11 | async-start | bytes 5242880 | tf_op jit(solution)/shard_map/reduce_scatter | solution.py:103
  43.9 27.9 %all-to-all-start.1 = ((f32[32,1,3072]{2,1,0:T(1,128)}), f32[32,1,3072]{2,1,0:T(1,128)S(1)}, u32[]{:S(2)}, u32[]{:S(2)}) async-start(f32[32,1,3072]{2,1,0:T(1,128)} %reshape.455), calls=%async_computation.1 | async-start | bytes 786432 | tf_op jit(solution)/shard_map/cond/branch_1_fun/all_to_all | solution.py:783
  53.7 27.7 %collective-permute-start.108 = (bf16[128,2048]{1,0:T(8,128)(2,1)}, bf16[128,2048]{1,0:T(8,128)(2,1)S(1)}, u32[]{:S(2)}, u32[]{:S(2)}) collective-permute-start(bf16[128,2048]{1,0:T(8,128)(2,1)} %get-tuple-element.1011), channel_id=1, source_target_pairs={{0,4},{1,5},{2,6},{3,7},{4,0},{5,1},{6,2},{7,3},{8,12},{9,13},{10,... | collective-permute-start | bytes 1572872 | tf_op jit(solution)/shard_map/cond/branch_1_fun/ppermute | solution.py:93
  54.3 27.1 %collective-permute-start.109 = (bf16[128,2048]{1,0:T(8,128)(2,1)}, bf16[128,2048]{1,0:T(8,128)(2,1)}, u32[]{:S(2)}, u32[]{:S(2)}) collective-permute-start(bf16[128,2048]{1,0:T(8,128)(2,1)} %get-tuple-element.1010), channel_id=1, source_target_pairs={{0,2},{1,3},{2,0},{3,1},{4,6},{5,7},{6,4},{7,5},{8,10},{9,11},{10,... | collective-permute-start | bytes 1572872 | tf_op jit(solution)/shard_map/cond/branch_1_fun/ppermute | solution.py:93
  185.1 78.5 %collective-permute-start.92 = (bf16[1024,2048]{1,0:T(8,128)(2,1)}, bf16[1024,2048]{1,0:T(8,128)(2,1)}, u32[]{:S(2)}, u32[]{:S(2)}) collective-permute-start(bf16[1024,2048]{1,0:T(8,128)(2,1)} %constant_dynamic-update-slice_fusion.7), channel_id=1, source_target_pairs={{0,1},{1,0},{2,3},{3,2},{4,5},{5,4},{6,7},{7,6},{8,9},{9,8},{10,11... | collective-permute-start | bytes 12582920 | tf_op jit(solution)/shard_map/cond/branch_1_fun/ppermute | solution.py:93
  206.7 57.0 %collective-permute-start.93 = (bf16[1024,2048]{1,0:T(8,128)(2,1)}, bf16[1024,2048]{1,0:T(8,128)(2,1)}, u32[]{:S(2)}, u32[]{:S(2)}) collective-permute-start(bf16[1024,2048]{1,0:T(8,128)(2,1)} %fusion.5), channel_id=1, source_target_pairs={{0,1},{1,0},{2,3},{3,2},{4,5},{5,4},{6,7},{7,6},{8,9},{9,8},{10,11... | collective-permute-start | bytes 12582920 | tf_op jit(solution)/shard_map/cond/branch_1_fun/ppermute | solution.py:93
  300.7 164.6 %reduce-scatter.4.cloned.1.call-start = ((), (), s32[]{:S(2)}) async-start(), calls=%async_computation.10 | async-start | bytes 5242880 | tf_op jit(solution)/shard_map/reduce_scatter | solution.py:103
  469.9 53.7 %all-to-all-start.2 = ((bf16[4,128,2048]{2,1,0:T(8,128)(2,1)}), bf16[4,128,2048]{2,1,0:T(8,128)(2,1)}, u32[]{:S(2)}, u32[]{:S(2)}) async-start(bf16[4,128,2048]{2,1,0:T(8,128)(2,1)} %bitcast.384), calls=%async_computation.4 | async-start | bytes 4194304 | tf_op jit(solution)/shard_map/all_to_all | solution.py:108
  474.6 175.9 %reduce-scatter.8.cloned.1.call-start = ((), (), s32[]{:S(2)}) async-start(), calls=%async_computation.12 | async-start | bytes 5242880 | tf_op jit(solution)/shard_map/reduce_scatter | solution.py:103
  474.8 38.4 %collective-permute-start.104 = (bf16[1024,2048]{1,0:T(8,128)(2,1)}, bf16[1024,2048]{1,0:T(8,128)(2,1)}, u32[]{:S(2)}, u32[]{:S(2)}) collective-permute-start(bf16[1024,2048]{1,0:T(8,128)(2,1)} %get-tuple-element.401), channel_id=1, source_target_pairs={{0,1},{1,0},{2,3},{3,2},{4,5},{5,4},{6,7},{7,6},{8,9},{9,8},{10,11... | collective-permute-start | bytes 12582920 | tf_op jit(solution)/shard_map/cond/branch_1_fun/ppermute | solution.py:93
  524.4 32.0 %collective-permute-start.2 = (bf16[1024,2048]{1,0:T(8,128)(2,1)}, bf16[1024,2048]{1,0:T(8,128)(2,1)}, u32[]{:S(2)}, u32[]{:S(2)}) collective-permute-start(bf16[1024,2048]{1,0:T(8,128)(2,1)} %get-tuple-element.412), channel_id=1, source_target_pairs={{0,1},{1,0},{2,3},{3,2},{4,5},{5,4},{6,7},{7,6},{8,9},{9,8},{10,11... | collective-permute-start | bytes 12582920 | tf_op jit(solution)/shard_map/cond/branch_1_fun/ppermute | solution.py:93
  527.4 29.0 %collective-permute-start.1 = (bf16[256,2048]{1,0:T(8,128)(2,1)}, bf16[256,2048]{1,0:T(8,128)(2,1)}, u32[]{:S(2)}, u32[]{:S(2)}) collective-permute-start(bf16[256,2048]{1,0:T(8,128)(2,1)} %bitcast.84), channel_id=1, source_target_pairs={{0,4},{1,5},{2,6},{3,7},{4,0},{5,1},{6,2},{7,3},{8,12},{9,13},{10,... | collective-permute-start | bytes 3145736 | tf_op jit(solution)/shard_map/cond/branch_1_fun/ppermute | solution.py:93
  528.9 27.5 %collective-permute-start = (bf16[256,2048]{1,0:T(8,128)(2,1)S(1)}, bf16[256,2048]{1,0:T(8,128)(2,1)}, u32[]{:S(2)}, u32[]{:S(2)}) collective-permute-start(bf16[256,2048]{1,0:T(8,128)(2,1)S(1)} %bitcast.408), channel_id=1, source_target_pairs={{0,2},{1,3},{2,0},{3,1},{4,6},{5,7},{6,4},{7,5},{8,10},{9,11},{10,... | collective-permute-start | bytes 3145736 | tf_op jit(solution)/shard_map/cond/branch_1_fun/ppermute | solution.py:93
  574.0 76.4 %all-to-all-start.3 = ((bf16[4,128,2048]{2,1,0:T(8,128)(2,1)}), bf16[4,128,2048]{2,1,0:T(8,128)(2,1)}, u32[]{:S(2)}, u32[]{:S(2)}) async-start(bf16[4,128,2048]{2,1,0:T(8,128)(2,1)} %bitcast.385), calls=%async_computation.5 | async-start | bytes 4194304 | tf_op jit(solution)/shard_map/all_to_all | solution.py:108
  621.8 27.3 %collective-permute-start.27 = (bf16[2,128,2048]{2,1,0:T(8,128)(2,1)}, bf16[2,128,2048]{2,1,0:T(8,128)(2,1)}, u32[]{:S(2)}, u32[]{:S(2)}) collective-permute-start(bf16[2,128,2048]{2,1,0:T(8,128)(2,1)} %get-tuple-element.453), channel_id=1, source_target_pairs={{0,2},{1,3},{2,0},{3,1},{4,6},{5,7},{6,4},{7,5},{8,10},{9,11},{10,... | collective-permute-start | bytes 3145736 | tf_op jit(solution)/shard_map/cond/branch_1_fun/ppermute | solution.py:93
  734.2 34.8 %collective-permute-start.47 = (bf16[128,2048]{1,0:T(8,128)(2,1)}, bf16[128,2048]{1,0:T(8,128)(2,1)}, u32[]{:S(2)}, u32[]{:S(2)}) collective-permute-start(bf16[128,2048]{1,0:T(8,128)(2,1)} %pad_maximum_fusion.5.refs_0_), channel_id=1, source_target_pairs={{0,2},{1,3},{2,0},{3,1},{4,6},{5,7},{6,4},{7,5},{8,10},{9,11},{10,... | collective-permute-start | bytes 1572872 | tf_op jit(solution)/shard_map/cond/branch_1_fun/ppermute | solution.py:93
  735.6 33.5 %collective-permute-start.48 = (bf16[128,2048]{1,0:T(8,128)(2,1)}, bf16[128,2048]{1,0:T(8,128)(2,1)}, u32[]{:S(2)}, u32[]{:S(2)}) collective-permute-start(bf16[128,2048]{1,0:T(8,128)(2,1)} %pad_maximum_fusion.5.refs_0_), channel_id=1, source_target_pairs={{0,4},{1,5},{2,6},{3,7},{4,0},{5,1},{6,2},{7,3},{8,12},{9,13},{10,... | collective-permute-start | bytes 1572872 | tf_op jit(solution)/shard_map/cond/branch_1_fun/ppermute | solution.py:93
  736.1 32.9 %collective-permute-start.49 = (bf16[128,2048]{1,0:T(8,128)(2,1)}, bf16[128,2048]{1,0:T(8,128)(2,1)}, u32[]{:S(2)}, u32[]{:S(2)}) collective-permute-start(bf16[128,2048]{1,0:T(8,128)(2,1)} %pad_maximum_fusion.6.refs_1_), channel_id=1, source_target_pairs={{0,2},{1,3},{2,0},{3,1},{4,6},{5,7},{6,4},{7,5},{8,10},{9,11},{10,... | collective-permute-start | bytes 1572872 | tf_op jit(solution)/shard_map/cond/branch_1_fun/ppermute | solution.py:93
  741.6 27.5 %collective-permute-start.50 = (bf16[2,64,2048]{2,1,0:T(8,128)(2,1)}, bf16[2,64,2048]{2,1,0:T(8,128)(2,1)}, u32[]{:S(2)}, u32[]{:S(2)}) collective-permute-start(bf16[2,64,2048]{2,1,0:T(8,128)(2,1)} %get-tuple-element.511), channel_id=1, source_target_pairs={{0,24},{1,25},{2,26},{3,27},{4,28},{5,29},{6,30},{7,31},{8,0},{9,1... | collective-permute-start | bytes 1572872 | tf_op jit(solution)/shard_map/cond/branch_1_fun/ppermute | solution.py:97
  841.8 32.4 %collective-permute-start.71 = (bf16[256,2048]{1,0:T(8,128)(2,1)}, bf16[256,2048]{1,0:T(8,128)(2,1)}, u32[]{:S(2)}, u32[]{:S(2)}) collective-permute-start(bf16[256,2048]{1,0:T(8,128)(2,1)} %get-tuple-element.558), channel_id=1, source_target_pairs={{0,2},{1,3},{2,0},{3,1},{4,6},{5,7},{6,4},{7,5},{8,10},{9,11},{10,... | collective-permute-start | bytes 3145736 | tf_op jit(solution)/shard_map/cond/branch_1_fun/ppermute | solution.py:93
  845.4 28.9 %collective-permute-start.72 = (bf16[64,2048]{1,0:T(8,128)(2,1)}, bf16[64,2048]{1,0:T(8,128)(2,1)}, u32[]{:S(2)}, u32[]{:S(2)}) collective-permute-start(bf16[64,2048]{1,0:T(8,128)(2,1)} %get-tuple-element.1067), channel_id=1, source_target_pairs={{0,24},{1,25},{2,26},{3,27},{4,28},{5,29},{6,30},{7,31},{8,0},{9,1... | collective-permute-start | bytes 786440 | tf_op jit(solution)/shard_map/cond/branch_1_fun/ppermute | solution.py:97
  (181 other events, 2766.4 us)
Sparse Core Ops, SparseCore 0:
  24.0 89.9 all-gather.3
  116.2 79.2 all-gather.5
  197.6 79.2 all-gather.7
  300.8 75.8 reduce-scatter.5
  378.9 77.2 reduce-scatter.3
  523.8 102.5 reduce-scatter.7
